TPU v7x, 32 devices: a whole 2x2x4 slice. The times are simulated.
32 devices in a mesh: wide: 16 (over z, y, x), narrow: 2 (over core).
Axes of the slice: x: 2, y: 2, z: 4, core: 2. Of those that a mesh axis runs over, the one named last changes fastest.
Arguments:
- char_ids: int32 [4096, 50], P('wide'), may hold values from 0 to 261
- char_mask: int32 [4096, 50], P('wide'), may hold values 0 or 1
- word_lengths: int32 [4096], P('wide'), may hold values from 1 to 50, as said below
- char_table: bfloat16 [262, 16], replicated, may hold values from -6 to 6
- conv_weight: bfloat16 [112, 2048], P(None, 'narrow'), may hold values from -0.5 to 0.5
- conv_bias: float32 [2048], P('narrow'), may hold values from -4 to 4
- highway_weight: bfloat16 [2, 2048, 2, 2048], P(None, 'wide', None, 'narrow'), may hold values from -0.125 to 0.125
- highway_bias: float32 [2, 2, 2048], P(None, None, 'narrow'), may hold values from -6 to 6
- proj_weight: bfloat16 [2048, 768], P('narrow', 'wide'), may hold values from -0.125 to 0.125
- qkv_weight: bfloat16 [768, 3, 768], P('wide', None, 'narrow'), may hold values from -0.21875 to 0.21875
- qv_bias: float32 [2, 768], P(None, 'narrow'), may hold values from -4 to 4
- out_weight: bfloat16 [768, 768], P('narrow', 'wide'), may hold values from -0.875 to 0.875
- up_weight: bfloat16 [768, 3072], P('wide', 'narrow'), may hold values from -0.21875 to 0.21875
- up_bias: float32 [3072], P('narrow'), may hold values from -4 to 4
- down_weight: bfloat16 [3072, 768], P('narrow', 'wide'), may hold values from -0.109375 to 0.109375
- vector_biases: float32 [5, 768], replicated, may hold values from -4 to 4
- norm_gains: float32 [2, 768], replicated, may hold values from 0.5 to 1.5
- cotangent: bfloat16 [4096, 768], P('wide'), may hold values from -6 to 6
Outputs:
- encoded: bfloat16 [4096, 768], P('wide')
- char_grad: float32 [262, 16], replicated
- conv_grad: float32 [112, 2048], P(None, 'narrow')
- conv_bias_grad: float32 [2048], P('narrow')
- highway_grad: float32 [2, 2048, 2, 2048], P(None, 'wide', None, 'narrow')
- highway_bias_grad: float32 [2, 2, 2048], P(None, None, 'narrow')
- proj_grad: float32 [2048, 768], P('narrow', 'wide')
- qkv_grad: float32 [768, 3, 768], P('wide', None, 'narrow')
- qv_bias_grad: float32 [2, 768], P(None, 'narrow')
- out_grad: float32 [768, 768], P('narrow', 'wide')
- up_grad: float32 [768, 3072], P('wide', 'narrow')
- up_bias_grad: float32 [3072], P('narrow')
- down_grad: float32 [3072, 768], P('narrow', 'wide')
- bias_grads: float32 [5, 768], replicated
- gain_grads: float32 [2, 768], replicated
Inputs may be any that keep to these rules, and one draw needn't show every extreme that they name: `word_lengths`: in every sequence of 128 words some word has 50 characters; lengths are heavy-tailed.
All inputs are finite; a program needn't handle non-finite values. No bound on the sum of `char_mask` on one device may be relied on, other than what follows from the above.
Results may differ from a plain program's by a relative error of at most 0.014.
Values may be sent and summed in bfloat16 or wider, within the bound.
No kernel may reach another device: no remote copies, remote signals or barrier semaphores. Data moves between devices by JAX's collectives and lax.ppermute only.
A program may use at most 192 MiB of HBM per device.

v0:
```python
from functools import reduce

import jax
import jax.numpy as jnp
from jax import lax
from jax.sharding import PartitionSpec as P

HEAD_DIM = 64
FILTERS = 2048
CHAR_DIM = 16
CHAR_VOCAB = 262
CHARS_MAX = 50
TAPS = 7
HW_LAYERS = 2
CNN_BLOCKS = 8
LENGTH = 128


BOUNDS = ((1, 2), (3, 4), (7, 8), (15, 16), (31, 32), (63, 64))
EPSILON = 1e-06


def channel_widths(first_channel, count):
    channels = first_channel + jnp.arange(count, dtype=jnp.int32)
    widths = jnp.full((count,), TAPS, jnp.int32)
    for numerator, denominator in BOUNDS:
        widths = widths - (channels >= FILTERS * numerator // denominator).astype(jnp.int32)
    return widths


def tap_columns(embedded):
    char_slots = embedded.shape[1]
    padded = jnp.pad(embedded, ((0, 0), (0, TAPS - 1), (0, 0)))
    return jnp.concatenate(
        [padded[:, offset : offset + char_slots, :] for offset in range(TAPS)], axis=-1
    )


def fold_taps(grad_columns):
    char_slots = grad_columns.shape[1]
    pieces = []
    for offset in range(TAPS):
        piece_grad = grad_columns[:, :, offset * CHAR_DIM : (offset + 1) * CHAR_DIM]
        pieces.append(jnp.pad(piece_grad, ((0, 0), (offset, TAPS - 1 - offset), (0, 0))))
    return reduce(jnp.add, pieces)[:, :char_slots, :]


def pool_windows(convolved, lengths, widths, chan_scale, conv_bias):
    shifted_in = convolved * chan_scale + conv_bias
    counts = jnp.maximum(lengths[:, None] - widths[None, :] + 1, 1)
    places = jnp.arange(convolved.shape[1], dtype=jnp.int32)
    valid = places[None, :, None] < counts[:, None, :]
    summit = jnp.max(jnp.where(valid, shifted_in, -1e30), axis=1)
    exponent = jnp.where(valid, shifted_in - summit[:, None, :], -80.0)
    weights = jnp.where(valid, jnp.exp(exponent), 0.0)
    totals = jnp.sum(weights, axis=1)
    pooled = summit + jnp.log(totals) - jnp.log(counts.astype(jnp.float32))
    return (pooled, weights / totals[:, None, :])


def gelu_exact(values):
    return jax.nn.gelu(values, approximate=False)


def layer_norm(values, gain_row, bias_row):
    center = jnp.mean(values, axis=-1, keepdims=True)
    spread = jnp.mean(jnp.square(values - center), axis=-1, keepdims=True)
    return (values - center) * lax.rsqrt(spread + EPSILON) * gain_row + bias_row


def highway_mix(mixed_pre, carried):
    gate_value = jax.nn.sigmoid(mixed_pre[:, 1])
    return gate_value * carried + (1.0 - gate_value) * gelu_exact(mixed_pre[:, 0])


def pair_sum(partial_value):
    return lax.psum(partial_value, "narrow")


def pair_grad_sum(partial_value):
    return lax.psum(partial_value.astype(jnp.bfloat16), "narrow").astype(jnp.float32)


def per_device(
    char_ids,
    char_mask,
    word_lengths,
    char_table,
    conv_weight,
    conv_bias,
    highway_weight,
    highway_bias,
    proj_weight,
    qkv_weight,
    qv_bias,
    out_weight,
    up_weight,
    up_bias,
    down_weight,
    vector_biases,
    norm_gains,
    cotangent,
):
    f32 = jnp.float32
    bf16 = jnp.bfloat16
    own_filters = conv_weight.shape[1]
    widths = channel_widths(lax.axis_index("narrow") * own_filters, own_filters)
    tap_rows = jnp.arange(TAPS * CHAR_DIM, dtype=jnp.int32) // CHAR_DIM
    tap_mask = (tap_rows[:, None] < widths[None, :]).astype(bf16)
    masked_filters = conv_weight * tap_mask
    chan_scale = jnp.sqrt(TAPS / widths.astype(f32))
    word_count = char_ids.shape[0]
    seq_count = word_count // LENGTH
    block_words = word_count // CNN_BLOCKS
    places = jnp.arange(CHARS_MAX, dtype=jnp.int32)
    alive = (char_mask * (places[None, :] < word_lengths[:, None]).astype(jnp.int32)).astype(f32)
    block_ids = char_ids.reshape(CNN_BLOCKS, block_words, CHARS_MAX)
    block_alive = alive.reshape(CNN_BLOCKS, block_words, CHARS_MAX)
    block_lengths = word_lengths.reshape(CNN_BLOCKS, block_words)
    vocab_ids = jnp.arange(CHAR_VOCAB, dtype=jnp.int32)

    def convolve(row_ids, row_alive):
        onehot = (row_ids.reshape(-1)[:, None] == vocab_ids[None, :]).astype(bf16)
        embedded = jnp.dot(onehot, char_table, preferred_element_type=f32)
        embedded = (embedded.reshape(row_ids.shape + (CHAR_DIM,)) * row_alive[:, :, None]).astype(
            bf16
        )
        columns = tap_columns(embedded)
        convolved = jnp.einsum("wpt,tf->wpf", columns, masked_filters, preferred_element_type=f32)
        return (onehot, columns, convolved)

    def pool_block(inputs):
        row_ids, row_alive, row_lengths = inputs
        convolved = convolve(row_ids, row_alive)[2]
        return pool_windows(convolved, row_lengths, widths, chan_scale, conv_bias)[0]

    pooled = lax.map(pool_block, (block_ids, block_alive, block_lengths)).reshape(
        word_count, own_filters
    )
    current = gelu_exact(pooled).astype(bf16)
    own_shards = (highway_weight, proj_weight, qkv_weight, out_weight, up_weight, down_weight)
    gathered = (
        lax.all_gather(own_shards[0], "wide", axis=1, tiled=True),
        lax.all_gather(own_shards[1], "wide", axis=1, tiled=True),
        lax.all_gather(own_shards[2], "wide", axis=0, tiled=True),
        lax.all_gather(own_shards[3], "wide", axis=1, tiled=True),
        lax.all_gather(own_shards[4], "wide", axis=0, tiled=True),
        lax.all_gather(own_shards[5], "wide", axis=1, tiled=True),
    )
    highway_full, proj_full, qkv_full, out_full, up_full, down_full = gathered
    kept_layers = []
    for layer_index in range(HW_LAYERS):
        whole_input = lax.all_gather(current, "narrow", axis=1, tiled=True)
        mixed_pre = (
            jnp.einsum(
                "wi,igf->wgf", whole_input, highway_full[layer_index], preferred_element_type=f32
            )
            + highway_bias[layer_index]
        )
        carried = current.astype(f32)
        kept_layers.append((whole_input, mixed_pre, carried))
        current = highway_mix(mixed_pre, carried).astype(bf16)
    start_rows = (
        pair_sum(jnp.dot(current, proj_full, preferred_element_type=f32)) + vector_biases[0]
    )
    start_low = start_rows.astype(bf16)
    qkv_bias = jnp.stack([qv_bias[0], jnp.zeros_like(qv_bias[0]), qv_bias[1]])
    projected = (
        jnp.einsum("wd,dgc->wgc", start_low, qkv_full, preferred_element_type=f32) + qkv_bias
    ).astype(bf16)
    heads_here = qkv_full.shape[2] // HEAD_DIM
    seq_shape = (seq_count, LENGTH, heads_here, HEAD_DIM)
    query = projected[:, 0].reshape(seq_shape)
    keys_here = projected[:, 1].reshape(seq_shape)
    values_here = projected[:, 2].reshape(seq_shape)
    attn_scale = HEAD_DIM ** (-0.5)

    def attention_scores():
        return (
            jnp.einsum("sqhe,skhe->shqk", query, keys_here, preferred_element_type=f32) * attn_scale
        )

    scores = attention_scores()
    log_total = jax.nn.logsumexp(scores, axis=-1, keepdims=True)
    probs_low = jnp.exp(scores - log_total).astype(bf16)
    context = (
        jnp.einsum("shqk,skhe->sqhe", probs_low, values_here, preferred_element_type=f32)
        .reshape(word_count, -1)
        .astype(bf16)
    )
    attended = pair_sum(jnp.dot(context, out_full, preferred_element_type=f32)) + vector_biases[1]
    before_one = start_rows + attended
    normed_one = layer_norm(before_one, norm_gains[0], vector_biases[3])
    normed_low = normed_one.astype(bf16)
    hidden_pre = jnp.dot(normed_low, up_full, preferred_element_type=f32) + up_bias
    hidden_low = gelu_exact(hidden_pre).astype(bf16)
    lowered = (
        pair_sum(jnp.dot(hidden_low, down_full, preferred_element_type=f32)) + vector_biases[2]
    )
    before_two = normed_one + lowered
    encoded = layer_norm(before_two, norm_gains[1], vector_biases[4]).astype(bf16)
    back_weights = (
        lax.all_gather(own_shards[0], "wide", axis=1, tiled=True),
        lax.all_gather(own_shards[1], "wide", axis=1, tiled=True),
        lax.all_gather(own_shards[2], "wide", axis=0, tiled=True),
        lax.all_gather(own_shards[3], "wide", axis=1, tiled=True),
        lax.all_gather(own_shards[4], "wide", axis=0, tiled=True),
        lax.all_gather(own_shards[5], "wide", axis=1, tiled=True),
    )
    highway_back, proj_back, qkv_back, out_back, up_back, down_back = back_weights
    grad_output = cotangent.astype(f32)
    ln_two_back = jax.vjp(layer_norm, before_two, norm_gains[1], vector_biases[4])[1]
    grad_before_two, gain_two, bias_two = ln_two_back(grad_output)
    grad_lowered = grad_before_two.astype(bf16)
    down_grad_local = jnp.dot(hidden_low.T, grad_lowered, preferred_element_type=f32)
    bias_down = jnp.sum(grad_lowered.astype(f32), axis=0)
    grad_hidden = jnp.dot(grad_lowered, down_back.T, preferred_element_type=f32)
    grad_hidden_pre = jax.vjp(gelu_exact, hidden_pre)[1](grad_hidden)[0].astype(bf16)
    up_grad_local = jnp.dot(normed_low.T, grad_hidden_pre, preferred_element_type=f32)
    bias_up = jnp.sum(grad_hidden_pre.astype(f32), axis=0)
    grad_normed_one = grad_before_two + pair_grad_sum(
        jnp.dot(grad_hidden_pre, up_back.T, preferred_element_type=f32)
    )
    ln_one_back = jax.vjp(layer_norm, before_one, norm_gains[0], vector_biases[3])[1]
    grad_before_one, gain_one, bias_one = ln_one_back(grad_normed_one)
    grad_attended = grad_before_one.astype(bf16)
    out_grad_local = jnp.dot(context.T, grad_attended, preferred_element_type=f32)
    bias_attended = jnp.sum(grad_attended.astype(f32), axis=0)
    grad_context = (
        jnp.dot(grad_attended, out_back.T, preferred_element_type=f32)
        .astype(bf16)
        .reshape(seq_shape)
    )
    probs_again = jnp.exp(attention_scores() - log_total)
    probs_again_low = probs_again.astype(bf16)
    grad_probs = jnp.einsum(
        "sqhe,skhe->shqk", grad_context, values_here, preferred_element_type=f32
    )
    grad_value = jnp.einsum(
        "shqk,sqhe->skhe", probs_again_low, grad_context, preferred_element_type=f32
    )
    grad_scores = (
        probs_again * (grad_probs - jnp.sum(probs_again * grad_probs, axis=-1, keepdims=True))
    ).astype(bf16)
    grad_query = (
        jnp.einsum("shqk,skhe->sqhe", grad_scores, keys_here, preferred_element_type=f32)
        * attn_scale
    )
    grad_key = (
        jnp.einsum("shqk,sqhe->skhe", grad_scores, query, preferred_element_type=f32) * attn_scale
    )
    grad_projected = jnp.stack(
        [
            grad_query.reshape(word_count, -1),
            grad_key.reshape(word_count, -1),
            grad_value.reshape(word_count, -1),
        ],
        axis=1,
    ).astype(bf16)
    qkv_grad_local = jnp.einsum(
        "wd,wgc->dgc", start_low, grad_projected, preferred_element_type=f32
    )
    bias_qv = jnp.sum(grad_projected[:, 0::2].astype(f32), axis=0)
    grad_start = grad_before_one + pair_grad_sum(
        jnp.einsum("wgc,dgc->wd", grad_projected, qkv_back, preferred_element_type=f32)
    )
    grad_start_low = grad_start.astype(bf16)
    proj_grad_local = jnp.dot(current.T, grad_start_low, preferred_element_type=f32)
    bias_start = jnp.sum(grad_start_low.astype(f32), axis=0)
    grad_current = jnp.dot(grad_start_low, proj_back.T, preferred_element_type=f32)
    highway_grads = []
    highway_bias_grads = []
    for layer_index in reversed(range(HW_LAYERS)):
        whole_input, mixed_pre, carried = kept_layers[layer_index]
        mix_back = jax.vjp(highway_mix, mixed_pre, carried)[1]
        grad_mixed, grad_carried = mix_back(grad_current)
        grad_mixed_low = grad_mixed.astype(bf16)
        layer_grad_local = jnp.einsum(
            "wi,wgf->igf", whole_input, grad_mixed_low, preferred_element_type=f32
        )
        highway_grads.insert(0, layer_grad_local)
        highway_bias_grads.insert(0, jnp.sum(grad_mixed_low.astype(f32), axis=0))
        grad_whole = jnp.einsum(
            "wgf,igf->wi", grad_mixed_low, highway_back[layer_index], preferred_element_type=f32
        )
        grad_current = grad_carried + lax.psum_scatter(
            grad_whole.astype(jnp.bfloat16), "narrow", scatter_dimension=1, tiled=True
        ).astype(jnp.float32)
    highway_stacked = jnp.stack(highway_grads)
    highway_bias_local = jnp.stack(highway_bias_grads)
    grad_pooled = jax.vjp(gelu_exact, pooled)[1](grad_current)[0]
    block_grads = grad_pooled.reshape(CNN_BLOCKS, block_words, own_filters)

    def conv_back(carry, inputs):
        grad_filter, grad_bias, grad_chars = carry
        row_ids, row_alive, row_lengths, row_grad = inputs
        onehot, columns, convolved = convolve(row_ids, row_alive)
        share = pool_windows(convolved, row_lengths, widths, chan_scale, conv_bias)[1]
        grad_shifted = share * row_grad[:, None, :]
        grad_conv = (grad_shifted * chan_scale).astype(bf16)
        grad_filter = grad_filter + jnp.einsum(
            "wpt,wpf->tf", columns, grad_conv, preferred_element_type=f32
        )
        grad_bias = grad_bias + jnp.sum(grad_shifted, axis=(0, 1))
        grad_columns = jnp.einsum(
            "wpf,tf->wpt", grad_conv, masked_filters, preferred_element_type=f32
        )
        grad_embedded = fold_taps(grad_columns) * row_alive[:, :, None]
        grad_chars = grad_chars + jnp.dot(
            onehot.astype(f32).T,
            grad_embedded.reshape(-1, CHAR_DIM),
            precision=lax.Precision.HIGHEST,
        )
        return ((grad_filter, grad_bias, grad_chars), None)

    start_carry = (
        jnp.zeros((TAPS * CHAR_DIM, own_filters), f32),
        jnp.zeros((own_filters,), f32),
        jnp.zeros((CHAR_VOCAB, CHAR_DIM), f32),
    )
    (grad_filter, grad_conv_bias, grad_chars), _ = lax.scan(
        conv_back, start_carry, (block_ids, block_alive, block_lengths, block_grads)
    )
    grad_filter = grad_filter * tap_mask.astype(f32)
    highway_grad, proj_grad, qkv_grad, out_grad, up_grad, down_grad = (
        lax.psum_scatter(highway_stacked, "wide", scatter_dimension=1, tiled=True),
        lax.psum_scatter(proj_grad_local, "wide", scatter_dimension=1, tiled=True),
        lax.psum_scatter(qkv_grad_local, "wide", scatter_dimension=0, tiled=True),
        lax.psum_scatter(out_grad_local, "wide", scatter_dimension=1, tiled=True),
        lax.psum_scatter(up_grad_local, "wide", scatter_dimension=0, tiled=True),
        lax.psum_scatter(down_grad_local, "wide", scatter_dimension=1, tiled=True),
    )
    bias_local = jnp.stack([bias_start, bias_attended, bias_down, bias_one, bias_two])
    gain_local = jnp.stack([gain_one, gain_two])
    (
        conv_grad,
        conv_bias_grad,
        highway_bias_grad,
        qv_bias_grad,
        up_bias_grad,
        bias_grads,
        gain_grads,
    ) = lax.psum(
        (grad_filter, grad_conv_bias, highway_bias_local, bias_qv, bias_up, bias_local, gain_local),
        "wide",
    )
    char_grad = lax.psum(grad_chars, ("wide", "narrow"))
    return (
        encoded,
        char_grad,
        conv_grad,
        conv_bias_grad,
        highway_grad,
        highway_bias_grad,
        proj_grad,
        qkv_grad,
        qv_bias_grad,
        out_grad,
        up_grad,
        up_bias_grad,
        down_grad,
        bias_grads,
        gain_grads,
    )


def solution(mesh):
    placed = (
        P("wide", None),
        P("wide", None),
        P("wide"),
        P(),
        P(None, "narrow"),
        P("narrow"),
        P(None, "wide", None, "narrow"),
        P(None, None, "narrow"),
        P("narrow", "wide"),
        P("wide", None, "narrow"),
        P(None, "narrow"),
        P("narrow", "wide"),
        P("wide", "narrow"),
        P("narrow"),
        P("narrow", "wide"),
        P(),
        P(),
        P("wide", None),
    )
    return jax.shard_map(
        per_device,
        mesh=mesh,
        in_specs=placed,
        out_specs=(
            P("wide", None),
            P(),
            P(None, "narrow"),
            P("narrow"),
            P(None, "wide", None, "narrow"),
            P(None, None, "narrow"),
            P("narrow", "wide"),
            P("wide", None, "narrow"),
            P(None, "narrow"),
            P("narrow", "wide"),
            P("wide", "narrow"),
            P("narrow"),
            P("narrow", "wide"),
            P(),
            P(),
        ),
        check_vma=False,
    )
```

profile of v0, /device:TPU:0, one launch (start us, length us, event | category | flops | bytes accessed | tf_op | source)
XLA Modules:
  0.0 2288.8 jit_solution(11571203154334189599)
XLA Ops:
  12.3 104.5 %while.33 = (s32[]{:T(128)}, f32[8,32,1024]{2,1,0:T(8,128)}, s32[8,32]{1,0:T(8,128)S(1)}, s32[8,32,50]{2,1,0:T(8,128)}, bf16[262,16]{0,1:T(8,128)(2,1)}, /*index...) while((s32[]{:T(128)}, f32[8,32,1024]{2,1,0:T(8,128)}, ...), condition=%wide.region_3.4_spmd.clone.clone, body=%wide.region_0.3_spmd.clone.clone.sunk | while | flops 400817536 | bytes 16724833 | solution.py:137
  124.3 10.3 all-gather.8.cloned.1.call-done
  134.5 196.0 %all-gather.10.cloned.1.call-done = bf16[2,2048,2,1024]{3,1,2,0:T(8,128)(2,1)} async-done(((bf16[2,128,2,1024]{3,1,2,0:T(8,128)(2,1)}), bf16[2,2048,2,1024]{3,1,2,0:T(8,128)(2,1)}) %all-gather.10.cloned.1.call-update) | async-done | bytes 16777232 | tf_op jit(solution)/shard_map/all_gather | solution.py:143
  358.4 50.8 %all-gather.14.cloned.1.call-done = bf16[1024,768]{0,1:T(8,128)(2,1)} async-done(((bf16[1024,48]{0,1:T(8,128)(2,1)}), bf16[1024,768]{0,1:T(8,128)(2,1)}) %all-gather.14.cloned.1.call-update) | async-done | bytes 1572880 | tf_op jit(solution)/shard_map/all_gather | solution.py:144
  412.4 43.6 %all_gather.35 = bf16[384,768]{0,1:T(8,128)(2,1)S(1)} all-gather(bf16[384,48]{0,1:T(8,128)(2,1)S(1)} %copy-done.75), channel_id=1, replica_groups=mesh['wide'=16,'narrow'=2] {'wide'}, dimensions={1}, use_global_device_ids=true | all-gather | bytes 626688 | tf_op jit(solution)/shard_map/all_gather | solution.py:146
  456.0 14.7 all-gather.16.cloned.1.call-done
  470.7 20.2 all-reduce.21.cloned.1.call-done
  498.4 18.6 all-reduce.23.cloned.1.call-done
  518.6 64.7 %all-gather.18.cloned.1.call-done = bf16[768,1536]{1,0:T(8,128)(2,1)} async-done(((bf16[48,1536]{1,0:T(8,128)(2,1)}), bf16[768,1536]{1,0:T(8,128)(2,1)}) %all-gather.18.cloned.1.call-update) | async-done | bytes 2359312 | tf_op jit(solution)/shard_map/all_gather | solution.py:147
  590.2 57.0 %all-gather.20.cloned.1.call-done = bf16[1536,768]{0,1:T(8,128)(2,1)} async-done(((bf16[1536,48]{0,1:T(8,128)(2,1)}), bf16[1536,768]{0,1:T(8,128)(2,1)}) %all-gather.20.cloned.1.call-update) | async-done | bytes 2359312 | tf_op jit(solution)/shard_map/all_gather | solution.py:148
  650.7 18.1 all-reduce.25.cloned.1.call-done
  677.2 19.7 all-reduce.27.cloned.1.call-done
  708.7 19.6 all-reduce.29.cloned.1.call-done
  771.2 11.7 pad_maximum_fusion
  788.5 228.1 %while.34 = (s32[]{:T(128)}, f32[112,1024]{1,0:T(8,128)}, f32[1024]{0:T(1024)S(1)}, f32[262,16]{0,1:T(8,128)S(1)}, s32[8,32,50]{2,1,0:T(8,128)}, /*index=5*/bf16...) while((s32[]{:T(128)}, f32[112,1024]{1,0:T(8,128)}, ...), condition=%wide.region_28.29_spmd.clone.clone.clone, body=%wide.region_24.28_spmd.clone.clone.clone.sunk | while | flops 1591272448 | bytes 67489944 | solution.py:321
  796.4 10.1 fusion.307
  824.8 10.1 fusion.307
  853.3 10.1 fusion.307
  881.7 10.1 fusion.307
  910.1 10.1 fusion.307
  938.6 10.1 fusion.307
  967.0 10.1 fusion.307
  995.5 10.1 fusion.307
  1043.2 79.5 %all-reduce.13 = (f32[1024]{0:T(1024)}, f32[2,2,1024]{2,1,0:T(2,128)}, f32[2,384]{1,0:T(2,128)}, f32[1536]{0:T(1024)}, f32[5,768]{1,0:T(8,128)}, /*index=5*/f32[2,768]{1,0:T(2,128)}) all-reduce(f32[1024]{0:T(1024)S(1)} %get-tuple-element.331, ...), channel_id=1, replica_groups=mesh['wide'=16,'narrow'=2] {'wide'}, use_global_device_ids=true, to_apply=%region_31.32 | all-reduce | flops 12800 | bytes 102400 | tf_op jit(solution)/shard_map/psum | solution.py:343
  1122.7 47.8 %psum.96 = f32[262,16]{0,1:T(8,128)} all-reduce(f32[262,16]{0,1:T(8,128)S(1)} %copy-done.79), channel_id=1, replica_groups=mesh['wide'=16,'narrow'=2] {'wide','narrow'}, use_global_device_ids=true, to_apply=%region_29.30 | all-reduce | flops 4192 | bytes 33536 | tf_op jit(solution)/shard_map/psum | solution.py:347
  1170.5 301.2 %reduce-scatter.13.cloned.1.call-done = f32[2,128,2,1024]{3,1,2,0:T(8,128)} async-done(((f32[2,2048,2,1024]{3,1,2,0:T(8,128)}), f32[2,128,2,1024]{3,1,2,0:T(8,128)}) %reduce-scatter.13.cloned.1.call-update) | async-done | bytes 2097168 | tf_op jit(solution)/shard_map/reduce_scatter | solution.py:326
  1476.3 130.5 %reduce-scatter.19.cloned.1.call-done = f32[384,48]{0,1:T(8,128)} async-done(((f32[384,768]{0,1:T(8,128)}), f32[384,48]{0,1:T(8,128)}) %reduce-scatter.19.cloned.1.call-update) | async-done | bytes 73744 | tf_op jit(solution)/shard_map/reduce_scatter | solution.py:329
  1606.7 113.7 %all-reduce.31.cloned.1.call-done = f32[112,1024]{1,0:T(8,128)} async-done(((f32[112,1024]{1,0:T(8,128)}), f32[112,1024]{1,0:T(8,128)}) %all-reduce.31.cloned.1.call-update) | async-done | bytes 458768 | tf_op jit(solution)/shard_map/psum | solution.py:343
  1720.4 136.0 %reduce-scatter.15.cloned.1.call-done = f32[1024,48]{0,1:T(8,128)} async-done(((f32[1024,768]{0,1:T(8,128)}), f32[1024,48]{0,1:T(8,128)}) %reduce-scatter.15.cloned.1.call-update) | async-done | bytes 196624 | tf_op jit(solution)/shard_map/reduce_scatter | solution.py:327
  1856.4 139.1 %reduce-scatter.17.cloned.1.call-done = f32[48,3,384]{2,0,1:T(8,128)} async-done(((f32[768,3,384]{2,0,1:T(8,128)}), f32[48,3,384]{2,0,1:T(8,128)}) %reduce-scatter.17.cloned.1.call-update) | async-done | bytes 221200 | tf_op jit(solution)/shard_map/reduce_scatter | solution.py:328
  1995.5 142.8 %reduce-scatter.21.cloned.1.call-done = f32[48,1536]{1,0:T(8,128)} async-done(((f32[768,1536]{1,0:T(8,128)}), f32[48,1536]{1,0:T(8,128)}) %reduce-scatter.21.cloned.1.call-update) | async-done | bytes 294928 | tf_op jit(solution)/shard_map/reduce_scatter | solution.py:330
  2138.2 141.5 %reduce-scatter.23.cloned.1.call-done = f32[1536,48]{0,1:T(8,128)} async-done(((f32[1536,768]{0,1:T(8,128)}), f32[1536,48]{0,1:T(8,128)}) %reduce-scatter.23.cloned.1.call-update) | async-done | bytes 294928 | tf_op jit(solution)/shard_map/reduce_scatter | solution.py:331
  (751 shorter events, 413.0 us)
Async XLA Ops:
  7.2 127.4 %all-gather.8.cloned.1.call-start = ((), (), s32[]{:S(2)}) async-start(), calls=%async_computation.8 | async-start | bytes 1572864 | tf_op jit(solution)/shard_map/all_gather | solution.py:153
  122.6 207.9 %all-gather.10.cloned.1.call-start = ((), (), s32[]{:S(2)}) async-start(), calls=%async_computation.9 | async-start | bytes 17825792 | tf_op jit(solution)/shard_map/all_gather | solution.py:143
  124.0 223.5 %all-gather.12.cloned.1.call-start = ((), (), s32[]{:S(2)}) async-start(), calls=%async_computation.10 | async-start | bytes 1572864 | tf_op jit(solution)/shard_map/all_gather | solution.py:153
  340.1 69.1 %all-gather.14.cloned.1.call-start = ((), (), s32[]{:S(2)}) async-start(), calls=%async_computation.11 | async-start | bytes 1671168 | tf_op jit(solution)/shard_map/all_gather | solution.py:144
  340.7 130.0 %all-gather.16.cloned.1.call-start = ((), (), s32[]{:S(2)}) async-start(), calls=%async_computation.13 | async-start | bytes 1880064 | tf_op jit(solution)/shard_map/all_gather | solution.py:145
  341.3 149.6 %all-reduce.21.cloned.1.call-start = ((), (), s32[]{:S(2)}) async-start(), calls=%async_computation.12 | async-start | bytes 1572864 | tf_op jit(solution)/shard_map/psum | solution.py:77
  358.3 97.7 %copy-start.34 = (bf16[256,1024]{1,0:T(8,128)(2,1)}, bf16[256,1024]{1,0:T(8,128)(2,1)S(1)}, u32[]{:S(2)}) copy-start(bf16[256,1024]{1,0:T(8,128)(2,1)S(1)} %get-tuple-element.598) | copy-start | bytes 1572868
  412.1 104.8 %all-reduce.23.cloned.1.call-start = ((), (), s32[]{:S(2)}) async-start(), calls=%async_computation.14 | async-start | bytes 1572864 | tf_op jit(solution)/shard_map/psum | solution.py:77
  412.3 104.7 %copy-start.76 = (f32[768]{0:T(1024)}, f32[768]{0:T(1024)S(1)}, u32[]{:S(2)}) copy-start(f32[768]{0:T(1024)S(1)} %get-tuple-element.534) | copy-start | bytes 9220
  412.3 256.5 %copy-start.65 = (f32[768]{0:T(1024)}, f32[768]{0:T(1024)S(1)}, u32[]{:S(2)}) copy-start(f32[768]{0:T(1024)S(1)} %get-tuple-element.532) | copy-start | bytes 9220
  496.4 86.9 %copy-start.93 = (f32[1536]{0:T(1024)S(1)}, f32[1536]{0:T(1024)}, u32[]{:S(2)}) copy-start(f32[1536]{0:T(1024)} %param.35) | copy-start | bytes 18436
  496.4 86.9 %all-gather.18.cloned.1.call-start = ((), (), s32[]{:S(2)}) async-start(), calls=%async_computation.15 | async-start | bytes 2506752 | tf_op jit(solution)/shard_map/all_gather | solution.py:147
  497.2 150.1 %all-gather.20.cloned.1.call-start = ((), (), s32[]{:S(2)}) async-start(), calls=%async_computation.16 | async-start | bytes 2506752 | tf_op jit(solution)/shard_map/all_gather | solution.py:148
  497.9 170.9 %all-reduce.25.cloned.1.call-start = ((), (), s32[]{:S(2)}) async-start(), calls=%async_computation.17 | async-start | bytes 1572864 | tf_op jit(solution)/shard_map/psum | solution.py:77
  498.4 200.9 %copy-start.63 = (f32[768]{0:T(1024)}, f32[768]{0:T(1024)S(1)}, u32[]{:S(2)}) copy-start(f32[768]{0:T(1024)S(1)} %get-tuple-element.537) | copy-start | bytes 9220
  518.3 181.0 %copy-start.1 = (f32[256,768]{1,0:T(8,128)}, f32[256,768]{1,0:T(8,128)S(1)}, u32[]{:S(2)}) copy-start(f32[256,768]{1,0:T(8,128)S(1)} %get-tuple-element.597) | copy-start | bytes 2359300
  518.3 181.0 %copy-start.69 = (f32[256]{0:T(256)}, f32[256]{0:T(256)S(1)}, u32[]{:S(2)}) copy-start(f32[256]{0:T(256)S(1)} %broadcast_multiply_fusion.2) | copy-start | bytes 3076
  518.6 180.7 %copy-start.71 = (f32[256]{0:T(256)}, f32[256]{0:T(256)S(1)}, u32[]{:S(2)}) copy-start(f32[256]{0:T(256)S(1)} %fusion.203) | copy-start | bytes 3076
  650.6 46.3 %all-reduce.27.cloned.1.call-start = ((), (), s32[]{:S(2)}) async-start(), calls=%async_computation.18 | async-start | bytes 786432 | tf_op jit(solution)/shard_map/psum | solution.py:81
  677.1 51.2 %all-reduce.29.cloned.1.call-start = ((), (), s32[]{:S(2)}) async-start(), calls=%async_computation.19 | async-start | bytes 786432 | tf_op jit(solution)/shard_map/psum | solution.py:81
  708.5 42.8 %reduce-scatter.9.cloned.1.call-start = ((), (), s32[]{:S(2)}) async-start(), calls=%async_computation.20 | async-start | bytes 1572864 | tf_op jit(solution)/shard_map/reduce_scatter | solution.py:286
  741.5 43.8 %reduce-scatter.11.cloned.1.call-start = ((), (), s32[]{:S(2)}) async-start(), calls=%async_computation.21 | async-start | bytes 1572864 | tf_op jit(solution)/shard_map/reduce_scatter | solution.py:286
  763.2 708.5 %reduce-scatter.13.cloned.1.call-start = ((), (), s32[]{:S(2)}) async-start(), calls=%async_computation.23 | async-start | bytes 35651584 | tf_op jit(solution)/shard_map/reduce_scatter | solution.py:326
  782.9 823.8 %reduce-scatter.19.cloned.1.call-start = ((), (), s32[]{:S(2)}) async-start(), calls=%async_computation.26 | async-start | bytes 1253376 | tf_op jit(solution)/shard_map/reduce_scatter | solution.py:329
  785.2 935.2 %all-reduce.31.cloned.1.call-start = ((), (), s32[]{:S(2)}) async-start(), calls=%async_computation.22 | async-start | bytes 917504 | tf_op jit(solution)/shard_map/psum | solution.py:343
  788.4 228.1 %copy-start.74 = (s32[1024]{0:T(1024)S(1)}, s32[1024]{0:T(1024)}, u32[]{:S(2)}) copy-start(s32[1024]{0:T(1024)} %copy-done.73) | copy-start | bytes 12292
  788.4 228.1 %copy-start.89 = (s32[112]{0:T(128)S(1)}, s32[112]{0:T(128)}, u32[]{:S(2)}) copy-start(s32[112]{0:T(128)} %copy-done.88) | copy-start | bytes 1348
  1018.5 837.9 %reduce-scatter.15.cloned.1.call-start = ((), (), s32[]{:S(2)}) async-start(), calls=%async_computation.24 | async-start | bytes 3342336 | tf_op jit(solution)/shard_map/reduce_scatter | solution.py:327
  1022.0 973.5 %reduce-scatter.17.cloned.1.call-start = ((), (), s32[]{:S(2)}) async-start(), calls=%async_computation.25 | async-start | bytes 3760128 | tf_op jit(solution)/shard_map/reduce_scatter | solution.py:328
  1025.8 1112.4 %reduce-scatter.21.cloned.1.call-start = ((), (), s32[]{:S(2)}) async-start(), calls=%async_computation.27 | async-start | bytes 5013504 | tf_op jit(solution)/shard_map/reduce_scatter | solution.py:330
  1030.4 1249.3 %reduce-scatter.23.cloned.1.call-start = ((), (), s32[]{:S(2)}) async-start(), calls=%async_computation.28 | async-start | bytes 5013504 | tf_op jit(solution)/shard_map/reduce_scatter | solution.py:331
  1041.8 80.9 %copy-start.79 = (f32[262,16]{0,1:T(8,128)S(1)}, f32[262,16]{0,1:T(8,128)}, u32[]{:S(2)}) copy-start(f32[262,16]{0,1:T(8,128)} %copy-done.78) | copy-start | bytes 50308
  (134 other events, 846.6 us)
Sparse Core Ops, SparseCore 0:
  122.8 11.7 all-gather.7
  137.9 192.6 all-gather.9
  340.3 7.2 all-gather.11
  350.1 59.0 all-gather.13
  411.7 58.9 all-gather.15
  472.9 17.9 all-reduce.20
  496.5 20.3 all-reduce.22
  519.8 63.4 all-gather.17
  586.1 61.0 all-gather.19
  650.7 18.0 all-reduce.24
  677.2 19.6 all-reduce.26
  708.6 19.6 all-reduce.28
  741.6 9.6 reduce-scatter.8
  763.4 9.7 reduce-scatter.10
  783.0 688.6 reduce-scatter.12
  1477.6 129.0 reduce-scatter.18
  1613.1 107.2 all-reduce.30
  1726.6 129.7 reduce-scatter.14
  1862.9 132.5 reduce-scatter.16
  2001.9 136.3 reduce-scatter.20
  2144.0 135.6 reduce-scatter.22
where the time goes:
time: 2300 us; the launch traced here: 2290 us
  waiting for transfers between devices  1610 us (70%)
  matrix products  247 us (11%)
  blocking collectives  171 us (7%)
  local copies, waits for them, and re-layouts  141 us (6%)
  other arithmetic  97.2 us (4%)
    reduce_scatter x1, waiting for transfers between devices, per_device(): lax.psum_scatter(highway_stacked, 'wide', scatter_dimension=1, tiled=True)  301 us
    all_gather x1, waiting for transfers between devices, per_device(): lax.all_gather(own_shards[0], 'wide', axis=1, tiled=True)  196 us
    reduce_scatter x1, waiting for transfers between devices, per_device(): lax.psum_scatter(up_grad_local, 'wide', scatter_dimension=0, tiled=True)  143 us
    reduce_scatter x1, waiting for transfers between devices, per_device(): lax.psum_scatter(down_grad_local, 'wide', scatter_dimension=1, tiled=True)  141 us
    reduce_scatter x1, waiting for transfers between devices, per_device(): lax.psum_scatter(qkv_grad_local, 'wide', scatter_dimension=0, tiled=True)  139 us
    reduce_scatter x1, waiting for transfers between devices, per_device(): lax.psum_scatter(proj_grad_local, 'wide', scatter_dimension=1, tiled=True)  136 us
    reduce_scatter x1, waiting for transfers between devices, per_device(): lax.psum_scatter(out_grad_local, 'wide', scatter_dimension=1, tiled=True)  130 us
    psum x1, waiting for transfers between devices, per_device(): lax.psum((grad_filter, grad_conv_bias, highway_bias_local, bias_qv, bias_...  114 us
  transfers between devices with their start and end apart: 21, of which 20 were waited for; matrix products, arithmetic and copies ran while one was open for 13% of the time, Pallas kernels for 0%

commit v1 on v0

v1 whole, which is shorter than its diff:
```python
from functools import partial, reduce

import jax
import jax.numpy as jnp
from jax import lax
from jax.experimental import pallas as pl
from jax.experimental.pallas import tpu as pltpu
from jax.sharding import PartitionSpec as P

HEAD_DIM = 64
FILTERS = 2048
CHAR_DIM = 16
CHAR_VOCAB = 262
CHARS_MAX = 50
TAPS = 7
HW_LAYERS = 2
TILE = 16
CHUNK = 8
SLOTS = 64
IDS = 272
LANES = 128
BLOCK = 256
LOG2E = 1.4426950408889634
LENGTH = 128


BOUNDS = ((1, 2), (3, 4), (7, 8), (15, 16), (31, 32), (63, 64))
EPSILON = 1e-06


def channel_widths(first_channel, count):
    channels = first_channel + jnp.arange(count, dtype=jnp.int32)
    widths = jnp.full((count,), TAPS, jnp.int32)
    for numerator, denominator in BOUNDS:
        widths = widths - (channels >= FILTERS * numerator // denominator).astype(jnp.int32)
    return widths


def gelu_exact(values):
    return jax.nn.gelu(values, approximate=False)


def layer_norm(values, gain_row, bias_row):
    center = jnp.mean(values, axis=-1, keepdims=True)
    spread = jnp.mean(jnp.square(values - center), axis=-1, keepdims=True)
    return (values - center) * lax.rsqrt(spread + EPSILON) * gain_row + bias_row


def highway_mix(mixed_pre, carried):
    gate_value = jax.nn.sigmoid(mixed_pre[:, 1])
    return gate_value * carried + (1.0 - gate_value) * gelu_exact(mixed_pre[:, 0])


def word_order(lengths):
    words = lengths.shape[0]
    sequences = words // LENGTH
    spots = jnp.arange(words, dtype=jnp.int32)
    keys = lengths * LENGTH + (LENGTH - 1 - spots % LENGTH)
    same = spots[:, None] // LENGTH == spots[None, :] // LENGTH
    ranks = jnp.sum((same & (keys[None, :] > keys[:, None])).astype(jnp.int32), axis=1)
    places = ranks // 8 * (8 * sequences) + spots // LENGTH * 8 + ranks % 8
    return (places[None, :] == spots[:, None]).astype(jnp.float32)


def spot_chars(ids_row, table_t):
    ids = lax.broadcasted_iota(jnp.int32, (IDS, LANES), 0)
    marks = (ids == ids_row).astype(jnp.float32).astype(jnp.bfloat16)
    return jnp.dot(table_t, marks, preferred_element_type=jnp.float32).T.astype(jnp.bfloat16)


def tap_rows(table_ref, start, tile, tap_lanes):
    rows = pl.ds(pl.multiple_of(tile * TILE, TILE), TILE)
    taken = None
    for tap in range(TAPS):
        piece = table_ref[pl.ds(start + tap, CHUNK), rows, :] * tap_lanes[tap][None]
        taken = piece if taken is None else taken + piece
    return taken.reshape(CHUNK * TILE, LANES)


def window_counts(lens_ref, widths_ref, tile):
    rows = pl.ds(pl.multiple_of(tile * TILE, TILE), TILE)
    return jnp.maximum(lens_ref[rows, :1] - widths_ref[...] + 1.0, 1.0)


def pool_kernel(
    tile_ref, ids_ref, table_ref, lanes_ref, filters_ref, scale_ref, bias_ref, lens_ref, widths_ref,
    embed_ref, pooled_ref, shift_ref, conv_ref, count_ref, top_ref,
):
    channels = filters_ref.shape[1]
    chunks_all = SLOTS // CHUNK
    tap_lanes = [lanes_ref[tap : tap + 1, :].astype(jnp.bfloat16) for tap in range(TAPS)]
    blocks = [slice(first, first + BLOCK) for first in range(0, channels, BLOCK)]

    def one_tile(tile, _):
        rows = pl.ds(pl.multiple_of(tile * TILE, TILE), TILE)
        chunks = tile_ref[tile]

        def embed(chunk, _):
            found = spot_chars(ids_ref[pl.ds(tile * chunks_all + chunk, 1), :], table_ref[...])
            embed_ref[pl.ds(chunk * CHUNK, CHUNK), rows, :] = found.reshape(CHUNK, TILE, LANES)
            return 0

        lax.fori_loop(0, chunks, embed, 0)
        embed_ref[pl.ds(chunks * CHUNK, CHUNK), rows, :] = jnp.zeros(
            (CHUNK, TILE, LANES), jnp.bfloat16
        )
        count_ref[...] = window_counts(lens_ref, widths_ref, tile)
        top_ref[...] = jnp.full(top_ref.shape, -1e30, jnp.float32)

        def convolve(chunk, _):
            columns = tap_rows(embed_ref, chunk * CHUNK, tile, tap_lanes)
            first = (chunk * CHUNK).astype(jnp.float32)
            for block in blocks:
                convolved = jnp.dot(
                    columns, filters_ref[:, block], preferred_element_type=jnp.float32
                )
                conv_ref[chunk, :, block] = convolved
                counts = count_ref[:, block] - first
                top = top_ref[:, block]
                for place in range(CHUNK):
                    row = convolved[place * TILE : (place + 1) * TILE]
                    top = jnp.maximum(top, jnp.where(counts > float(place), row, -1e30))
                top_ref[:, block] = top
            return 0

        lax.fori_loop(0, chunks, convolve, 0)
        pooled_ref[rows, :] = jnp.zeros((TILE, channels), jnp.float32)

        def weigh(chunk, _):
            first = (chunk * CHUNK).astype(jnp.float32)
            for block in blocks:
                counts = count_ref[:, block] - first
                scale = scale_ref[:, block] * LOG2E
                offset = top_ref[:, block] * scale
                total = pooled_ref[rows, block]
                for place in range(CHUNK):
                    row = conv_ref[chunk, place * TILE : (place + 1) * TILE, block]
                    weight = jnp.exp2(row * scale - offset)
                    total = total + jnp.where(counts > float(place), weight, 0.0)
                pooled_ref[rows, block] = total
            return 0

        lax.fori_loop(0, chunks, weigh, 0)
        top = top_ref[...] * scale_ref[...]
        log_total = jnp.log(pooled_ref[rows, :])
        pooled_ref[rows, :] = top + bias_ref[...] + log_total - jnp.log(count_ref[...])
        shift_ref[rows, :] = (top + log_total) * -LOG2E
        return 0

    lax.fori_loop(0, tile_ref.shape[0], one_tile, 0)


def pool_back_kernel(
    tile_ref, ids_ref, lanes_ref, filters_ref, scale_ref, lens_ref, widths_ref, embed_ref, shift_ref,
    grad_ref, filter_grad_ref, char_grad_ref, conv_grad_ref, column_ref, count_ref,
):
    channels = filters_ref.shape[1]
    chunks_all = SLOTS // CHUNK
    tap_lanes = [lanes_ref[tap : tap + 1, :].astype(jnp.bfloat16) for tap in range(TAPS)]
    lane_taps = lax.broadcasted_iota(jnp.int32, (1, 1, LANES), 2) // CHAR_DIM
    blocks = [slice(first, first + BLOCK) for first in range(0, channels, BLOCK)]
    filter_grad_ref[...] = jnp.zeros(filter_grad_ref.shape, jnp.float32)
    char_grad_ref[...] = jnp.zeros(char_grad_ref.shape, jnp.float32)
    column_ref[:CHUNK] = jnp.zeros((CHUNK, TILE, LANES), jnp.float32)

    def one_tile(tile, _):
        rows = pl.ds(pl.multiple_of(tile * TILE, TILE), TILE)
        chunks = tile_ref[tile]
        count_ref[...] = window_counts(lens_ref, widths_ref, tile)

        def one_chunk(chunk, _):
            columns = tap_rows(embed_ref, chunk * CHUNK, tile, tap_lanes)
            columns_t = columns.astype(jnp.float32).T.astype(jnp.bfloat16)
            first = (chunk * CHUNK).astype(jnp.float32)
            grad_columns = None
            for block in blocks:
                filters = filters_ref[:, block]
                convolved = jnp.dot(columns, filters, preferred_element_type=jnp.float32)
                counts = count_ref[:, block] - first
                scale = scale_ref[:, block]
                scale2 = scale * LOG2E
                shift = shift_ref[rows, block]
                grad = grad_ref[rows, block] * scale
                for place in range(CHUNK):
                    row = convolved[place * TILE : (place + 1) * TILE]
                    share = jnp.exp2(row * scale2 + shift)
                    conv_grad_ref[place * TILE : (place + 1) * TILE, block] = jnp.where(
                        counts > float(place), share * grad, 0.0
                    ).astype(jnp.bfloat16)
                conv_grad = conv_grad_ref[:, block]
                filter_grad_ref[:, block] += jnp.dot(
                    columns_t, conv_grad, preferred_element_type=jnp.float32
                )
                piece = lax.dot_general(
                    conv_grad, filters, (((1,), (1,)), ((), ())), preferred_element_type=jnp.float32
                )
                grad_columns = piece if grad_columns is None else grad_columns + piece
            column_ref[pl.ds(chunk * CHUNK + CHUNK, CHUNK)] = grad_columns.reshape(
                CHUNK, TILE, LANES
            )
            return 0

        lax.fori_loop(0, chunks, one_chunk, 0)

        def fold(chunk, _):
            moved = None
            for tap in range(TAPS):
                piece = column_ref[pl.ds(chunk * CHUNK + CHUNK - tap, CHUNK)]
                moved = piece if moved is None else jnp.where(lane_taps == tap, piece, moved)
            moved = moved.reshape(CHUNK * TILE, LANES)
            high = moved.astype(jnp.bfloat16)
            low = (moved - high.astype(jnp.float32)).astype(jnp.bfloat16)
            ids = lax.broadcasted_iota(jnp.int32, (IDS, LANES), 0)
            ids_row = ids_ref[pl.ds(tile * chunks_all + chunk, 1), :]
            marks = (ids == ids_row).astype(jnp.float32).astype(jnp.bfloat16)
            char_grad_ref[...] += jnp.dot(
                marks, jnp.concatenate([high, low], axis=1), preferred_element_type=jnp.float32
            )
            return 0

        lax.fori_loop(0, chunks, fold, 0)
        return 0

    lax.fori_loop(0, tile_ref.shape[0], one_tile, 0)


def conv_calls(words, channels):
    vmem = pl.BlockSpec(memory_space=pltpu.VMEM)
    smem = pl.BlockSpec(memory_space=pltpu.SMEM)
    shape = partial(jax.ShapeDtypeStruct, dtype=jnp.float32)
    params = pltpu.CompilerParams(vmem_limit_bytes=40 * 1024 * 1024)
    pool = pl.pallas_call(
        pool_kernel,
        out_shape=[
            jax.ShapeDtypeStruct((SLOTS, words, LANES), jnp.bfloat16),
            shape((words, channels)),
            shape((words, channels)),
        ],
        in_specs=[smem] + [vmem] * 8,
        out_specs=[vmem] * 3,
        scratch_shapes=[
            pltpu.VMEM((SLOTS // CHUNK, CHUNK * TILE, channels), jnp.float32),
            pltpu.VMEM((TILE, channels), jnp.float32),
            pltpu.VMEM((TILE, channels), jnp.float32),
        ],
        compiler_params=params,
        cost_estimate=pl.CostEstimate(
            flops=5_000_000_000, bytes_accessed=8_000_000, transcendentals=5_000_000
        ),
    )
    back = pl.pallas_call(
        pool_back_kernel,
        out_shape=[shape((LANES, channels)), shape((IDS, 2 * LANES))],
        in_specs=[smem] + [vmem] * 9,
        out_specs=[vmem] * 2,
        scratch_shapes=[
            pltpu.VMEM((CHUNK * TILE, channels), jnp.bfloat16),
            pltpu.VMEM((SLOTS + CHUNK, TILE, LANES), jnp.float32),
            pltpu.VMEM((TILE, channels), jnp.float32),
        ],
        compiler_params=params,
        cost_estimate=pl.CostEstimate(
            flops=10_000_000_000, bytes_accessed=10_000_000, transcendentals=5_000_000
        ),
    )
    return pool, back


STEPS = {
    "x": [(i, i ^ 1) for i in range(16)],
    "y": [(i, i ^ 2) for i in range(16)],
    "z": [(i, (i + 4) % 16) for i in range(16)],
}
PLACE = {"z": 0, "y": 1, "x": 2}
CHIPS = 16
SWAP = [(0, 1), (1, 0)]


def step(value, axis):
    return lax.ppermute(value, "wide", STEPS[axis])


def swap(value):
    return lax.ppermute(value, "narrow", SWAP)


def joined(pieces):
    return pieces[0] if len(pieces) == 1 else jnp.concatenate(pieces, axis=0)


def blocks_after(axes):
    blocks = [(0, 0, 0)]
    for axis in axes:
        place = PLACE[axis]
        count = 4 if axis == "z" else 2
        blocks = [
            block[:place] + (away,) + block[place + 1 :] for away in range(count) for block in blocks
        ]
    return blocks


def owners(axes, here):
    z, y, x = here // 4, (here // 2) % 2, here % 2
    return jnp.stack(
        [
            ((z - dz) % 4) * 4 + (y + dy) % 2 * 2 + (x + dx) % 2
            for dz, dy, dx in blocks_after(axes)
        ]
    ).astype(jnp.int32)


def gather_blocks(shard, axes):
    pieces = [shard]
    for axis in axes:
        pieces = [joined(pieces)]
        for _ in range(3 if axis == "z" else 1):
            pieces.append(step(pieces[-1], axis))
    return pieces


def add(one, other):
    return one.astype(jnp.float32) + other.astype(jnp.float32)


def scatter_blocks(pieces, axes, dtype=jnp.bfloat16):
    for place in reversed(range(len(axes))):
        axis = axes[place]
        travelling = pieces[1].astype(dtype)
        for later in pieces[2:]:
            travelling = add(later, step(travelling, axis)).astype(dtype)
        total = add(pieces[0], step(travelling, axis))
        if place:
            count = 4 if axes[place - 1] == "z" else 2
            pieces = jnp.split(total.astype(dtype), count, axis=0)
    return total


def reorder(rows, old, new):
    height = rows.shape[0] // len(old)
    if old == new:
        return rows
    return joined([rows[old.index(block) * height :][:height] for block in new])


def pair_sum(partial_value):
    return partial_value + swap(partial_value)


def pair_grad_sum(partial_value):
    low = partial_value.astype(jnp.bfloat16)
    return add(low, swap(low))


def permute_kernel(order_ref, own_ref, other_ref, *out_refs):
    count = own_ref.shape[1] // 128
    for part, out_ref in enumerate(out_refs):
        for block in range(2 * count):
            source = order_ref[part, block]
            offset = pl.multiple_of((source % count) * 128, 128)
            target = slice(block * 128, block * 128 + 128)

            @pl.when(source < count)
            def _():
                out_ref[:, target] = own_ref[:, pl.ds(offset, 128)]

            @pl.when(source >= count)
            def _():
                out_ref[:, target] = other_ref[:, pl.ds(offset, 128)]


def permute_channels(order, own, other):
    shape = jax.ShapeDtypeStruct((own.shape[0], 2 * own.shape[1]), own.dtype)
    vmem = pl.BlockSpec(memory_space=pltpu.VMEM)
    return pl.pallas_call(
        permute_kernel,
        out_shape=[shape] * order.shape[0],
        in_specs=[pl.BlockSpec(memory_space=pltpu.SMEM), vmem, vmem],
        out_specs=[vmem] * order.shape[0],
    )(order, own, other)


def take_kernel(order_ref, rows_ref, out_ref):
    for block in range(out_ref.shape[0]):
        out_ref[block] = rows_ref[order_ref[block]]


def take_blocks(order, rows):
    blocks = rows.reshape(CHIPS, -1, rows.shape[1])
    vmem = pl.BlockSpec(memory_space=pltpu.VMEM)
    return pl.pallas_call(
        take_kernel,
        out_shape=jax.ShapeDtypeStruct(blocks.shape, blocks.dtype),
        in_specs=[pl.BlockSpec(memory_space=pltpu.SMEM), vmem],
        out_specs=vmem,
    )(order, blocks).reshape(rows.shape)


def unpermute_kernel(order_ref, first_ref, second_ref, own_ref, other_ref, total_ref):
    count = own_ref.shape[1] // 128
    for block in range(2 * count):
        offset = pl.multiple_of(order_ref[0, block] * 128, 128)
        total_ref[:, pl.ds(offset, 128)] = first_ref[:, block * 128 : block * 128 + 128]
    for block in range(2 * count):
        offset = pl.multiple_of(order_ref[1, block] * 128, 128)
        total_ref[:, pl.ds(offset, 128)] += second_ref[:, block * 128 : block * 128 + 128]
    own_ref[...] = total_ref[:, : count * 128]
    other_ref[...] = total_ref[:, count * 128 :].astype(other_ref.dtype)


def unpermute_sum(order, first, second):
    words, channels = first.shape
    vmem = pl.BlockSpec(memory_space=pltpu.VMEM)
    return pl.pallas_call(
        unpermute_kernel,
        out_shape=[
            jax.ShapeDtypeStruct((words, channels // 2), jnp.float32),
            jax.ShapeDtypeStruct((words, channels // 2), jnp.bfloat16),
        ],
        in_specs=[pl.BlockSpec(memory_space=pltpu.SMEM), vmem, vmem],
        out_specs=[vmem] * 2,
        scratch_shapes=[pltpu.VMEM((words, channels), jnp.float32)],
        compiler_params=pltpu.CompilerParams(vmem_limit_bytes=32 * 1024 * 1024),
    )(order, first, second)


FIRST_AXES = "xzy"
SECOND_AXES = "yzx"
HIGHWAY_AXES = (("xzy", "yzx"), ("zxy", "zyx"))
SMALL_AXES = "zxy"


def times_pieces(values, pieces):
    columns = jnp.split(values, len(pieces), axis=1)
    return reduce(
        jnp.add,
        [
            jnp.dot(column, piece, preferred_element_type=jnp.float32)
            for column, piece in zip(columns, pieces)
        ],
    )


def sum_over_wide(values, routed):
    if not routed:
        return lax.psum(values, "wide")
    flat = [value.reshape(-1) for value in values]
    flat = [jnp.pad(value, (0, -value.shape[0] % 128)).reshape(-1, 128) for value in flat]
    rows = jnp.concatenate(flat, axis=0)
    used = rows.shape[0]
    rows = jnp.pad(rows, ((0, -used % (8 * CHIPS)), (0, 0)))
    order = owners(SMALL_AXES, lax.axis_index("wide"))
    spots = jnp.arange(CHIPS, dtype=jnp.int32)
    places = jnp.sum(jnp.where(order[None, :] == spots[:, None], spots[None, :], 0), axis=1)
    rows = take_blocks(order, rows)
    own = scatter_blocks(jnp.split(rows, 2, axis=0), SMALL_AXES, jnp.float32)
    rows = take_blocks(places, joined(gather_blocks(own, SMALL_AXES)))
    totals = []
    first = 0
    for value, piece in zip(values, flat):
        totals.append(rows[first : first + piece.shape[0]].reshape(-1)[: value.size].reshape(value.shape))
        first += piece.shape[0]
    return totals


def per_device(
    char_ids,
    char_mask,
    word_lengths,
    char_table,
    conv_weight,
    conv_bias,
    highway_weight,
    highway_bias,
    proj_weight,
    qkv_weight,
    qv_bias,
    out_weight,
    up_weight,
    up_bias,
    down_weight,
    vector_biases,
    norm_gains,
    cotangent,
):
    f32 = jnp.float32
    bf16 = jnp.bfloat16
    own_filters = conv_weight.shape[1]
    widths = channel_widths(lax.axis_index("narrow") * own_filters, own_filters)
    tap_rows = jnp.arange(TAPS * CHAR_DIM, dtype=jnp.int32) // CHAR_DIM
    tap_mask = (tap_rows[:, None] < widths[None, :]).astype(bf16)
    tap_pad = ((0, LANES - TAPS * CHAR_DIM), (0, 0))
    masked_filters = jnp.pad(conv_weight * tap_mask, tap_pad)
    chan_scale = jnp.sqrt(TAPS / widths.astype(f32))
    word_count = char_ids.shape[0]
    seq_count = word_count // LENGTH
    places = jnp.arange(CHARS_MAX, dtype=jnp.int32)
    alive = (char_mask > 0) & (places[None, :] < word_lengths[:, None])
    picks = word_order(word_lengths)
    picks_low = picks.astype(bf16)
    told = jnp.concatenate(
        [jnp.where(alive, char_ids, -1), word_lengths[:, None]], axis=1
    ).astype(f32)
    told = jnp.dot(picks, told, precision=lax.Precision.HIGHEST)
    lens = told[:, CHARS_MAX:]
    tile_count = word_count // TILE
    longest = jnp.max(lens.astype(jnp.int32).reshape(tile_count, TILE), axis=1)
    tile_chunks = (longest + CHUNK - 1) // CHUNK
    spread_ids = jnp.pad(
        told[:, :CHARS_MAX].astype(jnp.int32),
        ((0, 0), (0, SLOTS - CHARS_MAX)),
        constant_values=-1,
    )
    spread_ids = spread_ids.reshape(tile_count, TILE, SLOTS // CHUNK, CHUNK)
    spread_ids = spread_ids.transpose(0, 2, 3, 1).reshape(-1, CHUNK * TILE)
    table_t = jnp.pad(
        jnp.tile(char_table.T, (TAPS, 1)), (tap_pad[0], (0, IDS - CHAR_VOCAB))
    )
    tap_lanes = (
        jnp.arange(LANES, dtype=jnp.int32)[None, :] // CHAR_DIM
        == jnp.arange(8, dtype=jnp.int32)[:, None]
    ).astype(f32)
    scale_row, bias_row = chan_scale[None, :], conv_bias[None, :]
    width_row = widths.astype(f32)[None, :]
    pool, pool_back = conv_calls(word_count, own_filters)
    embedded, pooled, pool_shift = pool(
        tile_chunks, spread_ids, table_t, tap_lanes, masked_filters, scale_row, bias_row, lens,
        width_row,
    )
    current = gelu_exact(pooled).astype(bf16)
    here = lax.axis_index("wide")
    core = lax.axis_index("narrow")
    routed = lax.axis_size("wide") == CHIPS
    width_proj, width_qkv, width_out = own_filters, 3 * qkv_weight.shape[2], out_weight.shape[0]
    width_up, width_down = up_weight.shape[1], down_weight.shape[0]
    feature_rows = qkv_weight.shape[0]
    first_rows = jnp.concatenate(
        [proj_weight.T, qkv_weight.reshape(feature_rows, width_qkv), out_weight.T], axis=1
    )
    second_rows = jnp.concatenate([up_weight, down_weight.T], axis=1)

    def whole_rows(shard, axes):
        if routed:
            return gather_blocks(shard, axes)
        return [lax.all_gather(shard, "wide", axis=0, tiled=True)]

    def own_rows(pieces, axes):
        if routed:
            return scatter_blocks(pieces, axes)
        return lax.psum_scatter(
            joined(pieces).astype(f32), "wide", scatter_dimension=0, tiled=True
        )

    def halves(rows):
        return jnp.split(rows, 2, axis=0) if routed else [rows]

    highway_full = [
        [whole_rows(highway_weight[layer, :, part], HIGHWAY_AXES[layer][part]) for part in range(2)]
        for layer in range(HW_LAYERS)
    ]
    first_full = joined(whole_rows(first_rows, FIRST_AXES))
    second_full = joined(whole_rows(second_rows, SECOND_AXES))
    if routed:
        second_full = reorder(second_full, blocks_after(SECOND_AXES), blocks_after(FIRST_AXES))
        feature_order = owners(FIRST_AXES, here)
    else:
        feature_order = jnp.arange(lax.axis_size("wide"), dtype=jnp.int32)
    proj_t, qkv_full, out_t = jnp.split(
        first_full, [width_proj, width_proj + width_qkv], axis=1
    )
    qkv_full = qkv_full.reshape(-1, 3, qkv_weight.shape[2])
    up_full, down_t = jnp.split(second_full, [width_up], axis=1)
    feature_count = proj_t.shape[0]
    feature_picks = (
        feature_order[:, None] == jnp.arange(feature_order.shape[0], dtype=jnp.int32)[None, :]
    ).astype(f32)
    feature_places = (
        feature_order[:, None] * feature_rows + jnp.arange(feature_rows, dtype=jnp.int32)[None, :]
    ).reshape(-1)
    feature_moves = (
        feature_places[:, None] == jnp.arange(feature_count, dtype=jnp.int32)[None, :]
    ).astype(bf16)

    def pick_features(rows, picks):
        blocked = rows.reshape(rows.shape[0], -1, feature_rows)
        return jnp.einsum(
            "kwr,bw->kbr", blocked, picks, precision=lax.Precision.HIGHEST
        ).reshape(rows.shape)

    vector_biases = pick_features(vector_biases, feature_picks)
    norm_gains = pick_features(norm_gains, feature_picks)
    grad_output = jnp.dot(cotangent, feature_moves.T, preferred_element_type=f32).astype(bf16)
    grad_output = jnp.dot(picks_low, grad_output, preferred_element_type=f32)
    kept_layers = []
    for layer_index in range(HW_LAYERS):
        if routed:
            order = jnp.stack([owners(axes, here) for axes in HIGHWAY_AXES[layer_index]])
            order = (order - core * (CHIPS // 2)) % CHIPS
            whole_input = permute_channels(order, current, swap(current))
        else:
            order = None
            whole_input = [lax.all_gather(current, "narrow", axis=1, tiled=True)] * 2
        mixed_pre = (
            jnp.stack(
                [
                    times_pieces(whole_input[part], highway_full[layer_index][part])
                    for part in range(2)
                ],
                axis=1,
            )
            + highway_bias[layer_index]
        )
        carried = current.astype(f32)
        kept_layers.append((whole_input, mixed_pre, carried, order))
        current = highway_mix(mixed_pre, carried).astype(bf16)
    start_rows = (
        pair_sum(jnp.dot(current, proj_t.T, preferred_element_type=f32)) + vector_biases[0]
    )
    start_low = start_rows.astype(bf16)
    qkv_bias = jnp.stack([qv_bias[0], jnp.zeros_like(qv_bias[0]), qv_bias[1]])
    projected = (
        jnp.einsum("wd,dgc->wgc", start_low, qkv_full, preferred_element_type=f32) + qkv_bias
    ).astype(bf16)
    heads_here = qkv_full.shape[2] // HEAD_DIM
    head_shape = (word_count, heads_here, HEAD_DIM)
    query = projected[:, 0].reshape(head_shape)
    keys_here = projected[:, 1].reshape(head_shape)
    values_here = projected[:, 2].reshape(head_shape)
    attn_scale = HEAD_DIM ** (-0.5)
    sequence = jnp.arange(word_count, dtype=jnp.int32) // 8 % seq_count
    together = (sequence[:, None] == sequence[None, :])[None]
    scores = jnp.einsum("qhe,khe->hqk", query, keys_here, preferred_element_type=f32) * attn_scale
    scores = jnp.where(together, scores, -1e30)
    weights = jnp.exp(scores - jnp.max(scores, axis=-1, keepdims=True))
    probs = weights / jnp.sum(weights, axis=-1, keepdims=True)
    probs_low = probs.astype(bf16)
    context = (
        jnp.einsum("hqk,khe->qhe", probs_low, values_here, preferred_element_type=f32)
        .reshape(word_count, -1)
        .astype(bf16)
    )
    attended = pair_sum(jnp.dot(context, out_t.T, preferred_element_type=f32)) + vector_biases[1]
    before_one = start_rows + attended
    normed_one = layer_norm(before_one, norm_gains[0], vector_biases[3])
    normed_low = normed_one.astype(bf16)
    hidden_pre = jnp.dot(normed_low, up_full, preferred_element_type=f32) + up_bias
    hidden_low = gelu_exact(hidden_pre).astype(bf16)
    lowered = (
        pair_sum(jnp.dot(hidden_low, down_t.T, preferred_element_type=f32)) + vector_biases[2]
    )
    before_two = normed_one + lowered
    encoded = layer_norm(before_two, norm_gains[1], vector_biases[4]).astype(bf16)
    encoded = jnp.dot(encoded, feature_moves, preferred_element_type=f32).astype(bf16)
    encoded = jnp.dot(picks_low.T, encoded, preferred_element_type=f32).astype(bf16)
    ln_two_back = jax.vjp(layer_norm, before_two, norm_gains[1], vector_biases[4])[1]
    grad_before_two, gain_two, bias_two = ln_two_back(grad_output)
    grad_lowered = grad_before_two.astype(bf16)
    down_grad_local = jnp.dot(grad_lowered.T, hidden_low, preferred_element_type=f32)
    bias_down = jnp.sum(grad_lowered.astype(f32), axis=0)
    grad_hidden = jnp.dot(grad_lowered, down_t, preferred_element_type=f32)
    grad_hidden_pre = jax.vjp(gelu_exact, hidden_pre)[1](grad_hidden)[0].astype(bf16)
    up_grad_local = jnp.dot(normed_low.T, grad_hidden_pre, preferred_element_type=f32)
    bias_up = jnp.sum(grad_hidden_pre.astype(f32), axis=0)
    grad_normed_one = grad_before_two + pair_grad_sum(
        jnp.dot(grad_hidden_pre, up_full.T, preferred_element_type=f32)
    )
    ln_one_back = jax.vjp(layer_norm, before_one, norm_gains[0], vector_biases[3])[1]
    grad_before_one, gain_one, bias_one = ln_one_back(grad_normed_one)
    grad_attended = grad_before_one.astype(bf16)
    out_grad_local = jnp.dot(grad_attended.T, context, preferred_element_type=f32)
    bias_attended = jnp.sum(grad_attended.astype(f32), axis=0)
    grad_context = (
        jnp.dot(grad_attended, out_t, preferred_element_type=f32)
        .astype(bf16)
        .reshape(head_shape)
    )
    grad_probs = jnp.einsum(
        "qhe,khe->hqk", grad_context, values_here, preferred_element_type=f32
    )
    grad_value = jnp.einsum("hqk,qhe->khe", probs_low, grad_context, preferred_element_type=f32)
    grad_scores = (
        probs * (grad_probs - jnp.sum(probs * grad_probs, axis=-1, keepdims=True))
    ).astype(bf16)
    grad_query = (
        jnp.einsum("hqk,khe->qhe", grad_scores, keys_here, preferred_element_type=f32) * attn_scale
    )
    grad_key = (
        jnp.einsum("hqk,qhe->khe", grad_scores, query, preferred_element_type=f32) * attn_scale
    )
    grad_projected = jnp.stack(
        [
            grad_query.reshape(word_count, -1),
            grad_key.reshape(word_count, -1),
            grad_value.reshape(word_count, -1),
        ],
        axis=1,
    ).astype(bf16)
    qkv_grad_local = jnp.einsum(
        "wd,wgc->dgc", start_low, grad_projected, preferred_element_type=f32
    )
    bias_qv = jnp.sum(grad_projected[:, 0::2].astype(f32), axis=0)
    grad_start = grad_before_one + pair_grad_sum(
        jnp.einsum("wgc,dgc->wd", grad_projected, qkv_full, preferred_element_type=f32)
    )
    grad_start_low = grad_start.astype(bf16)
    proj_grad_local = jnp.dot(grad_start_low.T, current, preferred_element_type=f32)
    bias_start = jnp.sum(grad_start_low.astype(f32), axis=0)
    grad_current = jnp.dot(grad_start_low, proj_t, preferred_element_type=f32)
    first_grad_local = jnp.concatenate(
        [proj_grad_local, qkv_grad_local.reshape(feature_count, width_qkv), out_grad_local], axis=1
    ).astype(bf16)
    second_grad_local = jnp.concatenate([up_grad_local, down_grad_local], axis=1).astype(bf16)
    if routed:
        second_grad_local = reorder(
            second_grad_local, blocks_after(FIRST_AXES), blocks_after(SECOND_AXES)
        )
    second_grad = own_rows(halves(second_grad_local), SECOND_AXES)
    first_grad = own_rows(halves(first_grad_local), FIRST_AXES)
    highway_grads = []
    highway_bias_grads = []
    for layer_index in reversed(range(HW_LAYERS)):
        whole_input, mixed_pre, carried, order = kept_layers[layer_index]
        mix_back = jax.vjp(highway_mix, mixed_pre, carried)[1]
        grad_mixed, grad_carried = mix_back(grad_current)
        grad_mixed_low = grad_mixed.astype(bf16)
        part_grads = []
        grad_whole = []
        for part in range(2):
            part_mixed = grad_mixed_low[:, part]
            pieces = highway_full[layer_index][part]
            part_grads.append(
                own_rows(
                    [
                        jnp.dot(columns.T, part_mixed, preferred_element_type=f32).astype(bf16)
                        for columns in jnp.split(whole_input[part], len(pieces), axis=1)
                    ],
                    HIGHWAY_AXES[layer_index][part],
                )
            )
            grad_whole.append(
                jnp.concatenate(
                    [
                        jnp.dot(part_mixed, piece.T, preferred_element_type=f32)
                        for piece in pieces
                    ],
                    axis=1,
                )
            )
        highway_grads.insert(0, jnp.stack(part_grads, axis=1))
        highway_bias_grads.insert(0, jnp.sum(grad_mixed_low.astype(f32), axis=0))
        if routed:
            grad_own, grad_other = unpermute_sum(order, *grad_whole)
            grad_current = grad_carried + add(grad_own, swap(grad_other))
        else:
            grad_current = grad_carried + lax.psum_scatter(
                add(*grad_whole).astype(bf16), "narrow", scatter_dimension=1, tiled=True
            ).astype(f32)
    highway_grad = jnp.stack(highway_grads)
    highway_bias_local = jnp.stack(highway_bias_grads)
    grad_pooled = jax.vjp(gelu_exact, pooled)[1](grad_current)[0]
    grad_filter, grad_marks = pool_back(
        tile_chunks, spread_ids, tap_lanes, masked_filters, scale_row, lens, width_row, embedded,
        pool_shift, grad_pooled,
    )
    grad_filter = grad_filter[: TAPS * CHAR_DIM]
    grad_conv_bias = jnp.sum(grad_pooled, axis=0)
    grad_marks = grad_marks[:CHAR_VOCAB, :LANES] + grad_marks[:CHAR_VOCAB, LANES:]
    grad_chars = jnp.sum(
        grad_marks[:, : TAPS * CHAR_DIM].reshape(CHAR_VOCAB, TAPS, CHAR_DIM), axis=1
    )
    grad_filter = grad_filter * tap_mask.astype(f32)
    proj_grad, qkv_grad, out_grad = jnp.split(
        first_grad, [width_proj, width_proj + width_qkv], axis=1
    )
    up_grad, down_grad = jnp.split(second_grad, [width_up], axis=1)
    proj_grad, out_grad, down_grad = proj_grad.T, out_grad.T, down_grad.T
    qkv_grad = qkv_grad.reshape(qkv_weight.shape)
    bias_local = pick_features(
        jnp.stack([bias_start, bias_attended, bias_down, bias_one, bias_two]), feature_picks.T
    )
    gain_local = pick_features(jnp.stack([gain_one, gain_two]), feature_picks.T)
    (
        conv_grad,
        conv_bias_grad,
        highway_bias_grad,
        qv_bias_grad,
        up_bias_grad,
        bias_grads,
        gain_grads,
        char_grad,
    ) = sum_over_wide(
        (
            grad_filter,
            grad_conv_bias,
            highway_bias_local,
            bias_qv,
            bias_up,
            bias_local,
            gain_local,
            pair_sum(grad_chars),
        ),
        routed,
    )
    return (
        encoded,
        char_grad,
        conv_grad,
        conv_bias_grad,
        highway_grad,
        highway_bias_grad,
        proj_grad,
        qkv_grad,
        qv_bias_grad,
        out_grad,
        up_grad,
        up_bias_grad,
        down_grad,
        bias_grads,
        gain_grads,
    )


def solution(mesh):
    placed = (
        P("wide", None),
        P("wide", None),
        P("wide"),
        P(),
        P(None, "narrow"),
        P("narrow"),
        P(None, "wide", None, "narrow"),
        P(None, None, "narrow"),
        P("narrow", "wide"),
        P("wide", None, "narrow"),
        P(None, "narrow"),
        P("narrow", "wide"),
        P("wide", "narrow"),
        P("narrow"),
        P("narrow", "wide"),
        P(),
        P(),
        P("wide", None),
    )
    return jax.shard_map(
        per_device,
        mesh=mesh,
        in_specs=placed,
        out_specs=(
            P("wide", None),
            P(),
            P(None, "narrow"),
            P("narrow"),
            P(None, "wide", None, "narrow"),
            P(None, None, "narrow"),
            P("narrow", "wide"),
            P("wide", None, "narrow"),
            P(None, "narrow"),
            P("narrow", "wide"),
            P("wide", "narrow"),
            P("narrow"),
            P("narrow", "wide"),
            P(),
            P(),
        ),
        check_vma=False,
    )
```

time: 2300 us -> 908 us (0.39)
  waiting for transfers between devices: 1610 us -> 470 us
  blocking collectives: 171 us -> 0 us
  matrix products: 247 us -> 104 us
  Pallas kernels: 0 us -> 67.6 us
  starting transfers between devices: 1.65 us -> 58.1 us
  local copies, waits for them, and re-layouts: 141 us -> 116 us
    reduce_scatter x8 -> x0, waiting for transfers between devices: 1000 us -> none  [the longest x1 301 us: per_device(): lax.psum_scatter(highway_stacked, 'wide', scatter_dimension=1, tiled=True)]
    ppermute x0 -> x80, waiting for transfers between devices: none -> 470 us  [the longest x70 470 us: step(): return lax.ppermute(value, 'wide', STEPS[axis])]
    all_gather x7 -> x0, waiting for transfers between devices: 400 us -> none  [the longest x1 196 us: per_device(): lax.all_gather(own_shards[0], 'wide', axis=1, tiled=True)]
    psum x6 -> x0, waiting for transfers between devices: 210 us -> none  [the longest x1 114 us: per_device(): lax.psum((grad_filter, grad_conv_bias, highway_bias_local, bias_qv, bias_...]
    psum x2 -> x0, blocking collectives: 127 us -> none  [the longest x1 79.5 us: per_device(): lax.psum((grad_filter, grad_conv_bias, highway_bias_local, bias_qv, bias_...]
    div x8 -> x0, matrix products: 80.8 us -> none  [pool_windows(): return (pooled, weights / totals[:, None, :])]
    pallas_call x0 -> x8, Pallas kernels: none -> 67.6 us  [the longest x1 32.9 us: per_device(): pool_back(tile_chunks, spread_ids, tap_lanes, masked_filters, scale_row,...]
    dot_general x71 -> x47, matrix products: 151 us -> 89.6 us  [the longest x8 19.5 us: per_device(): jnp.dot(part_mixed, piece.T, preferred_element_type=f32)]
  transfers between devices with their start and end apart: 21 -> 80, of which waited for: 20 -> 41; matrix products, arithmetic and copies ran while one was open for 13% -> 26% of each run, Pallas kernels for 0% -> 8%
where the time goes in v1:
time: 908 us; the launch traced here: 897 us
  waiting for transfers between devices  470 us (52%)
  local copies, waits for them, and re-layouts  116 us (13%)
  matrix products  104 us (11%)
  other arithmetic  76.3 us (8%)
  Pallas kernels  67.6 us (7%)
  starting transfers between devices  58.1 us (6%)
    ppermute x70, waiting for transfers between devices, step(): return lax.ppermute(value, 'wide', STEPS[axis])  470 us
    unnamed x309, local copies, waits for them, and re-layouts  60.3 us
    ppermute x70, starting transfers between devices, step(): return lax.ppermute(value, 'wide', STEPS[axis])  56 us
    pallas_call x1, Pallas kernels, per_device(): pool_back(tile_chunks, spread_ids, tap_lanes, masked_filters, scale_row,...  32.9 us
    pallas_call x1, Pallas kernels, per_device(): pool(tile_chunks, spread_ids, table_t, tap_lanes, masked_filters, scale_r...  20.7 us
    dot_general x8, matrix products, per_device(): jnp.dot(part_mixed, piece.T, preferred_element_type=f32)  19.5 us
    convert_element_type x12, other arithmetic, scatter_blocks(): pieces = jnp.split(total.astype(dtype), count, axis=0)  19.3 us
    dot_general x8, matrix products, times_pieces(): jnp.dot(column, piece, preferred_element_type=jnp.float32)  18.8 us
  transfers between devices with their start and end apart: 80, of which 41 were waited for; matrix products, arithmetic and copies ran while one was open for 26% of the time, Pallas kernels for 8%

profile of v1, /device:TPU:0, one launch (start us, length us, event | category | flops | bytes accessed | tf_op | source)
XLA Modules:
  0.0 896.8 jit_solution(4004600765961559008)
XLA Ops:
  16.1 20.7 %shard_map.289 = (bf16[64,256,128]{2,1,0:T(8,128)(2,1)S(1)}, f32[256,1024]{1,0:T(8,128)S(1)}, f32[256,1024]{1,0:T(8,128)S(1)}) custom-call(s32[16]{0:T(128)S(1)} %and_select_fusion.4.tile_ref, s32[128,128]{1,0:T(8,128)S(1)} %reshape.707.ids_ref, bf16[128,272]{1,0:T(8,128)(2,1)S(1)} %pad.33.table_ref, f32[8,128]{1,0:T(8,128)S(1)} %fusion.219.lanes_ref, ...), custom_call_target="tpu_custom_call" | custom-call | flops 5000000000 | bytes 8000000 | tf_op jit(solution)/shard_map/pallas_call | solution.py:525
  85.2 21.4 %collective-permute-done.18 = bf16[128,1024]{1,0:T(8,128)(2,1)} collective-permute-done((bf16[128,1024]{1,0:T(8,128)(2,1)S(1)}, bf16[128,1024]{1,0:T(8,128)(2,1)}, u32[]{:S(2)}, u32[]{:S(2)}) %collective-permute-start.18) | collective-permute-done | bytes 262176 | tf_op jit(solution)/shard_map/ppermute | solution.py:280
  123.6 18.3 %collective-permute-done.19 = bf16[128,1024]{1,0:T(8,128)(2,1)} collective-permute-done((bf16[128,1024]{1,0:T(8,128)(2,1)}, bf16[128,1024]{1,0:T(8,128)(2,1)}, u32[]{:S(2)}, u32[]{:S(2)}) %collective-permute-start.19) | collective-permute-done | bytes 262176 | tf_op jit(solution)/shard_map/ppermute | solution.py:280
  149.4 8.6 collective-permute-done.24
  161.5 7.6 collective-permute-done.8
  169.2 11.1 %collective-permute-done.3 = bf16[256,1024]{1,0:T(8,128)(2,1)S(1)} collective-permute-done((bf16[256,1024]{1,0:T(8,128)(2,1)}, bf16[256,1024]{1,0:T(8,128)(2,1)S(1)}, u32[]{:S(2)}, u32[]{:S(2)}) %collective-permute-start.3) | collective-permute-done | bytes 524320 | tf_op jit(solution)/shard_map/ppermute | solution.py:280
  180.4 10.5 %collective-permute-done.25 = bf16[96,2560]{1,0:T(8,128)(2,1)S(1)} collective-permute-done((bf16[96,2560]{1,0:T(8,128)(2,1)S(1)}, bf16[96,2560]{1,0:T(8,128)(2,1)S(1)}, u32[]{:S(2)}, u32[]{:S(2)}) %collective-permute-start.25) | collective-permute-done | bytes 491552 | tf_op jit(solution)/shard_map/ppermute | solution.py:280
  193.9 20.9 %collective-permute-done.9 = bf16[256,1024]{1,0:T(8,128)(2,1)S(1)} collective-permute-done((bf16[256,1024]{1,0:T(8,128)(2,1)S(1)}, bf16[256,1024]{1,0:T(8,128)(2,1)S(1)}, u32[]{:S(2)}, u32[]{:S(2)}) %collective-permute-start.9) | collective-permute-done | bytes 524320 | tf_op jit(solution)/shard_map/ppermute | solution.py:280
  219.9 5.6 collective-permute-done.4
  233.9 51.0 %collective-permute-done.15 = bf16[512,1024]{1,0:T(8,128)(2,1)S(1)} collective-permute-done((bf16[512,1024]{1,0:T(8,128)(2,1)S(1)}, bf16[512,1024]{1,0:T(8,128)(2,1)S(1)}, u32[]{:S(2)}, u32[]{:S(2)}) %collective-permute-start.15) | collective-permute-done | bytes 1048608 | tf_op jit(solution)/shard_map/ppermute | solution.py:280
  307.1 5.5 fusion.43
  312.6 68.8 %collective-permute-done.33 = bf16[384,3072]{1,0:T(8,128)(2,1)} collective-permute-done((bf16[384,3072]{1,0:T(8,128)(2,1)}, bf16[384,3072]{1,0:T(8,128)(2,1)}, u32[]{:S(2)}, u32[]{:S(2)}) %collective-permute-start.33) | collective-permute-done | bytes 2359328 | tf_op jit(solution)/shard_map/ppermute | solution.py:280
  430.8 7.2 multiply_convert_fusion.1
  543.2 32.9 %shard_map.294 = (f32[128,1024]{1,0:T(8,128)S(1)}, f32[272,256]{1,0:T(8,128)S(1)}) custom-call(s32[16]{0:T(128)S(1)} %and_select_fusion.4.tile_ref, s32[128,128]{1,0:T(8,128)S(1)} %reshape.707.ids_ref, f32[8,128]{1,0:T(8,128)S(1)} %fusion.219.lanes_ref, bf16[128,1024]{1,0:T(8,128)(2,1)S(1)} %pad.34.filters_ref, f32[1,1024]{1,0:T(1,128)S(1)} %divide_sqrt_fusion.scale_ref, ...), custom_call_target="tpu_custom_call" | custom-call | flops 10000000000 | bytes 10000000 | tf_op jit(solution)/shard_map/pallas_call | solution.py:760
  582.4 4.8 collective-permute-start.40
  588.9 20.5 %collective-permute-done.40 = f32[576,128]{1,0:T(8,128)S(1)} collective-permute-done((f32[576,128]{1,0:T(8,128)S(1)}, f32[576,128]{1,0:T(8,128)S(1)}, u32[]{:S(2)}, u32[]{:S(2)}) %collective-permute-start.40) | collective-permute-done | bytes 294944 | tf_op jit(solution)/shard_map/ppermute | solution.py:280
  639.8 5.7 collective-permute-done.46
  645.6 5.7 collective-permute-done.47
  651.9 25.6 %collective-permute-done.48 = f32[288,128]{1,0:T(8,128)S(1)} collective-permute-done((f32[288,128]{1,0:T(8,128)S(1)}, f32[288,128]{1,0:T(8,128)S(1)}, u32[]{:S(2)}, u32[]{:S(2)}) %collective-permute-start.48) | collective-permute-done | bytes 147488 | tf_op jit(solution)/shard_map/ppermute | solution.py:280
  696.3 36.3 %collective-permute-done.49 = f32[576,128]{1,0:T(8,128)S(1)} collective-permute-done((f32[576,128]{1,0:T(8,128)S(1)}, f32[576,128]{1,0:T(8,128)S(1)}, u32[]{:S(2)}, u32[]{:S(2)}) %collective-permute-start.49) | collective-permute-done | bytes 294944 | tf_op jit(solution)/shard_map/ppermute | solution.py:280
  757.1 8.5 collective-permute-done.77
  765.8 10.4 %collective-permute-done.72 = bf16[96,2560]{1,0:T(8,128)(2,1)S(1)} collective-permute-done((bf16[96,2560]{1,0:T(8,128)(2,1)S(1)}, bf16[96,2560]{1,0:T(8,128)(2,1)S(1)}, u32[]{:S(2)}, u32[]{:S(2)}) %collective-permute-start.72) | collective-permute-done | bytes 491552 | tf_op jit(solution)/shard_map/ppermute | solution.py:280
  780.2 7.2 collective-permute-done.56
  787.7 11.0 %collective-permute-done.51 = bf16[256,1024]{1,0:T(8,128)(2,1)S(1)} collective-permute-done((bf16[256,1024]{1,0:T(8,128)(2,1)S(1)}, bf16[256,1024]{1,0:T(8,128)(2,1)S(1)}, u32[]{:S(2)}, u32[]{:S(2)}) %collective-permute-start.51) | collective-permute-done | bytes 524320 | tf_op jit(solution)/shard_map/ppermute | solution.py:280
  798.9 12.4 %collective-permute-done.78 = bf16[96,3072]{1,0:T(8,128)(2,1)S(1)} collective-permute-done((bf16[96,3072]{1,0:T(8,128)(2,1)S(1)}, bf16[96,3072]{1,0:T(8,128)(2,1)S(1)}, u32[]{:S(2)}, u32[]{:S(2)}) %collective-permute-start.78) | collective-permute-done | bytes 589856 | tf_op jit(solution)/shard_map/ppermute | solution.py:280
  811.5 16.0 %collective-permute-done.67 = bf16[128,1024]{1,0:T(8,128)(2,1)S(1)} collective-permute-done((bf16[128,1024]{1,0:T(8,128)(2,1)S(1)}, bf16[128,1024]{1,0:T(8,128)(2,1)S(1)}, u32[]{:S(2)}, u32[]{:S(2)}) %collective-permute-start.67) | collective-permute-done | bytes 262176 | tf_op jit(solution)/shard_map/ppermute | solution.py:280
  827.8 5.3 collective-permute-done.62
  835.6 25.6 %collective-permute-done.68 = bf16[128,1024]{1,0:T(8,128)(2,1)S(1)} collective-permute-done((bf16[128,1024]{1,0:T(8,128)(2,1)S(1)}, bf16[128,1024]{1,0:T(8,128)(2,1)S(1)}, u32[]{:S(2)}, u32[]{:S(2)}) %collective-permute-start.68) | collective-permute-done | bytes 262176 | tf_op jit(solution)/shard_map/ppermute | solution.py:280
  861.3 5.5 collective-permute-done.63
  875.2 5.5 collective-permute-done.58
  881.2 5.1 collective-permute-done.53
  887.4 5.5 collective-permute-done.54
  (731 shorter events, 385.8 us)
Async XLA Ops:
  2.8 79.0 %collective-permute-start.29 = (bf16[48,3072]{1,0:T(8,128)(2,1)}, bf16[48,3072]{1,0:T(8,128)(2,1)S(1)}, u32[]{:S(2)}, u32[]{:S(2)}) collective-permute-start(bf16[48,3072]{1,0:T(8,128)(2,1)} %get-tuple-element.167), channel_id=1, source_target_pairs={{0,4},{2,6},{4,0},{6,2},{8,12},{10,14},{12,8},{14,10},{16,20},{18,... | collective-permute-start | bytes 884744 | tf_op jit(solution)/shard_map/ppermute | solution.py:280
  8.6 52.6 %collective-permute-start.22 = (bf16[48,2560]{1,0:T(8,128)(2,1)}, bf16[48,2560]{1,0:T(8,128)(2,1)}, u32[]{:S(2)}, u32[]{:S(2)}) collective-permute-start(bf16[48,2560]{1,0:T(8,128)(2,1)} %get-tuple-element.176), channel_id=1, source_target_pairs={{0,2},{2,0},{4,6},{6,4},{8,10},{10,8},{12,14},{14,12},{16,18},{18,... | collective-permute-start | bytes 737288 | tf_op jit(solution)/shard_map/ppermute | solution.py:280
  13.5 54.6 %collective-permute-start.6 = (bf16[128,1024]{1,0:T(8,128)(2,1)}, bf16[128,1024]{1,0:T(8,128)(2,1)S(1)}, u32[]{:S(2)}, u32[]{:S(2)}) collective-permute-start(bf16[128,1024]{1,0:T(8,128)(2,1)} %get-tuple-element.143), channel_id=1, source_target_pairs={{0,4},{2,6},{4,0},{6,2},{8,12},{10,14},{12,8},{14,10},{16,20},{18,... | collective-permute-start | bytes 786440 | tf_op jit(solution)/shard_map/ppermute | solution.py:280
  43.0 70.0 %collective-permute-start = (bf16[256,1024]{1,0:T(8,128)(2,1)}, bf16[256,1024]{1,0:T(8,128)(2,1)}, u32[]{:S(2)}, u32[]{:S(2)}) collective-permute-start(bf16[256,1024]{1,0:T(8,128)(2,1)} %multiply_convert_fusion.2.own_ref), channel_id=1, source_target_pairs={{0,1},{1,0},{2,3},{3,2},{4,5},{5,4},{6,7},{7,6},{8,9},{9,8},{10,11... | collective-permute-start | bytes 1572872 | tf_op jit(solution)/shard_map/ppermute | solution.py:284
  70.5 47.8 %collective-permute-start.23 = (bf16[96,2560]{1,0:T(8,128)(2,1)}, bf16[96,2560]{1,0:T(8,128)(2,1)}, u32[]{:S(2)}, u32[]{:S(2)}) collective-permute-start(bf16[96,2560]{1,0:T(8,128)(2,1)} %pad_maximum_fusion.12), channel_id=1, source_target_pairs={{0,8},{2,10},{4,12},{6,14},{8,16},{10,18},{12,20},{14,22},{16,24},... | collective-permute-start | bytes 1474568 | tf_op jit(solution)/shard_map/ppermute | solution.py:280
  112.2 47.7 %collective-permute-start.30 = (bf16[96,3072]{1,0:T(8,128)(2,1)}, bf16[96,3072]{1,0:T(8,128)(2,1)S(1)}, u32[]{:S(2)}, u32[]{:S(2)}) collective-permute-start(bf16[96,3072]{1,0:T(8,128)(2,1)} %pad_maximum_fusion.8), channel_id=1, source_target_pairs={{0,8},{2,10},{4,12},{6,14},{8,16},{10,18},{12,20},{14,22},{16,24},... | collective-permute-start | bytes 1769480 | tf_op jit(solution)/shard_map/ppermute | solution.py:280
  143.3 87.8 %collective-permute-start.20 = (bf16[512,1024]{1,0:T(8,128)(2,1)S(1)}, bf16[512,1024]{1,0:T(8,128)(2,1)S(1)}, u32[]{:S(2)}, u32[]{:S(2)}) collective-permute-start(bf16[512,1024]{1,0:T(8,128)(2,1)S(1)} %pad_maximum_fusion.7), channel_id=1, source_target_pairs={{0,4},{2,6},{4,0},{6,2},{8,12},{10,14},{12,8},{14,10},{16,20},{18,... | collective-permute-start | bytes 3145736 | tf_op jit(solution)/shard_map/ppermute | solution.py:280
  159.8 68.2 %collective-permute-start.31 = (bf16[96,3072]{1,0:T(8,128)(2,1)S(1)}, bf16[96,3072]{1,0:T(8,128)(2,1)S(1)}, u32[]{:S(2)}, u32[]{:S(2)}) collective-permute-start(bf16[96,3072]{1,0:T(8,128)(2,1)S(1)} %collective-permute-done.30), channel_id=1, source_target_pairs={{0,8},{2,10},{4,12},{6,14},{8,16},{10,18},{12,20},{14,22},{16,24},... | collective-permute-start | bytes 1769480 | tf_op jit(solution)/shard_map/ppermute | solution.py:280
  191.0 98.7 %collective-permute-start.26 = (bf16[384,2560]{1,0:T(8,128)(2,1)S(1)}, bf16[384,2560]{1,0:T(8,128)(2,1)S(1)}, u32[]{:S(2)}, u32[]{:S(2)}) collective-permute-start(bf16[384,2560]{1,0:T(8,128)(2,1)S(1)} %get-tuple-element.161), channel_id=1, source_target_pairs={{0,4},{2,6},{4,0},{6,2},{8,12},{10,14},{12,8},{14,10},{16,20},{18,... | collective-permute-start | bytes 5898248 | tf_op jit(solution)/shard_map/ppermute | solution.py:280
  215.6 81.7 %collective-permute-start.10 = (bf16[1024,1024]{1,0:T(8,128)(2,1)}, bf16[1024,1024]{1,0:T(8,128)(2,1)}, u32[]{:S(2)}, u32[]{:S(2)}) collective-permute-start(bf16[1024,1024]{1,0:T(8,128)(2,1)} %constant_dynamic-update-slice_fusion.5), channel_id=1, source_target_pairs={{0,2},{2,0},{4,6},{6,4},{8,10},{10,8},{12,14},{14,12},{16,18},{18,... | collective-permute-start | bytes 6291464 | tf_op jit(solution)/shard_map/ppermute | solution.py:280
  225.5 59.4 %collective-permute-start.15 = (bf16[512,1024]{1,0:T(8,128)(2,1)S(1)}, bf16[512,1024]{1,0:T(8,128)(2,1)S(1)}, u32[]{:S(2)}, u32[]{:S(2)}) collective-permute-start(bf16[512,1024]{1,0:T(8,128)(2,1)S(1)} %pad_maximum_fusion.6), channel_id=1, source_target_pairs={{0,2},{2,0},{4,6},{6,4},{8,10},{10,8},{12,14},{14,12},{16,18},{18,... | collective-permute-start | bytes 3145736 | tf_op jit(solution)/shard_map/ppermute | solution.py:280
  228.1 71.7 %collective-permute-start.5 = (bf16[1024,1024]{1,0:T(8,128)(2,1)}, bf16[1024,1024]{1,0:T(8,128)(2,1)}, u32[]{:S(2)}, u32[]{:S(2)}) collective-permute-start(bf16[1024,1024]{1,0:T(8,128)(2,1)} %constant_dynamic-update-slice_fusion), channel_id=1, source_target_pairs={{0,4},{2,6},{4,0},{6,2},{8,12},{10,14},{12,8},{14,10},{16,20},{18,... | collective-permute-start | bytes 6291464 | tf_op jit(solution)/shard_map/ppermute | solution.py:280
  231.1 56.6 %collective-permute-start.32 = (bf16[96,3072]{1,0:T(8,128)(2,1)S(1)}, bf16[96,3072]{1,0:T(8,128)(2,1)S(1)}, u32[]{:S(2)}, u32[]{:S(2)}) collective-permute-start(bf16[96,3072]{1,0:T(8,128)(2,1)S(1)} %collective-permute-done.31), channel_id=1, source_target_pairs={{0,8},{2,10},{4,12},{6,14},{8,16},{10,18},{12,20},{14,22},{16,24},... | collective-permute-start | bytes 1769480 | tf_op jit(solution)/shard_map/ppermute | solution.py:280
  284.9 114.8 %collective-permute-start.21 = (bf16[1024,1024]{1,0:T(8,128)(2,1)}, bf16[1024,1024]{1,0:T(8,128)(2,1)}, u32[]{:S(2)}, u32[]{:S(2)}) collective-permute-start(bf16[1024,1024]{1,0:T(8,128)(2,1)} %constant_dynamic-update-slice_fusion.15), channel_id=1, source_target_pairs={{0,2},{2,0},{4,6},{6,4},{8,10},{10,8},{12,14},{14,12},{16,18},{18,... | collective-permute-start | bytes 6291464 | tf_op jit(solution)/shard_map/ppermute | solution.py:280
  287.7 117.0 %collective-permute-start.16 = (bf16[1024,1024]{1,0:T(8,128)(2,1)}, bf16[1024,1024]{1,0:T(8,128)(2,1)}, u32[]{:S(2)}, u32[]{:S(2)}) collective-permute-start(bf16[1024,1024]{1,0:T(8,128)(2,1)} %constant_dynamic-update-slice_fusion.10), channel_id=1, source_target_pairs={{0,4},{2,6},{4,0},{6,2},{8,12},{10,14},{12,8},{14,10},{16,20},{18,... | collective-permute-start | bytes 6291464 | tf_op jit(solution)/shard_map/ppermute | solution.py:280
  289.7 91.8 %collective-permute-start.33 = (bf16[384,3072]{1,0:T(8,128)(2,1)}, bf16[384,3072]{1,0:T(8,128)(2,1)}, u32[]{:S(2)}, u32[]{:S(2)}) collective-permute-start(bf16[384,3072]{1,0:T(8,128)(2,1)} %constant_dynamic-update-slice_fusion.31), channel_id=1, source_target_pairs={{0,2},{2,0},{4,6},{6,4},{8,10},{10,8},{12,14},{14,12},{16,18},{18,... | collective-permute-start | bytes 7077896 | tf_op jit(solution)/shard_map/ppermute | solution.py:280
  312.6 82.8 %collective-permute-start.11 = (bf16[256,1024]{1,0:T(8,128)(2,1)S(1)}, bf16[256,1024]{1,0:T(8,128)(2,1)S(1)}, u32[]{:S(2)}, u32[]{:S(2)}) collective-permute-start(bf16[256,1024]{1,0:T(8,128)(2,1)S(1)} %get-tuple-element.138.own_ref), channel_id=1, source_target_pairs={{0,1},{1,0},{2,3},{3,2},{4,5},{5,4},{6,7},{7,6},{8,9},{9,8},{10,11... | collective-permute-start | bytes 1572872 | tf_op jit(solution)/shard_map/ppermute | solution.py:284
  463.0 170.8 %collective-permute-start.75 = (bf16[384,3072]{1,0:T(8,128)(2,1)}, bf16[384,3072]{1,0:T(8,128)(2,1)}, u32[]{:S(2)}, u32[]{:S(2)}) collective-permute-start(bf16[384,3072]{1,0:T(8,128)(2,1)} %copy-done.103), channel_id=1, source_target_pairs={{0,2},{2,0},{4,6},{6,4},{8,10},{10,8},{12,14},{14,12},{16,18},{18,... | collective-permute-start | bytes 7077896 | tf_op jit(solution)/shard_map/ppermute | solution.py:280
  509.7 171.2 %collective-permute-start.65 = (bf16[1024,1024]{1,0:T(8,128)(2,1)}, bf16[1024,1024]{1,0:T(8,128)(2,1)}, u32[]{:S(2)}, u32[]{:S(2)}) collective-permute-start(bf16[1024,1024]{1,0:T(8,128)(2,1)} %convolution_convert_fusion.2), channel_id=1, source_target_pairs={{0,2},{2,0},{4,6},{6,4},{8,10},{10,8},{12,14},{14,12},{16,18},{18,... | collective-permute-start | bytes 6291464 | tf_op jit(solution)/shard_map/ppermute | solution.py:280
  513.5 172.3 %collective-permute-start.60 = (bf16[1024,1024]{1,0:T(8,128)(2,1)}, bf16[1024,1024]{1,0:T(8,128)(2,1)}, u32[]{:S(2)}, u32[]{:S(2)}) collective-permute-start(bf16[1024,1024]{1,0:T(8,128)(2,1)} %convolution_convert_fusion.3), channel_id=1, source_target_pairs={{0,4},{2,6},{4,0},{6,2},{8,12},{10,14},{12,8},{14,10},{16,20},{18,... | collective-permute-start | bytes 6291464 | tf_op jit(solution)/shard_map/ppermute | solution.py:280
  535.0 142.8 %collective-permute-start.70 = (bf16[384,2560]{1,0:T(8,128)(2,1)}, bf16[384,2560]{1,0:T(8,128)(2,1)}, u32[]{:S(2)}, u32[]{:S(2)}) collective-permute-start(bf16[384,2560]{1,0:T(8,128)(2,1)} %split.310), channel_id=1, source_target_pairs={{0,4},{2,6},{4,0},{6,2},{8,12},{10,14},{12,8},{14,10},{16,20},{18,... | collective-permute-start | bytes 5898248 | tf_op jit(solution)/shard_map/ppermute | solution.py:280
  632.2 116.7 %collective-permute-start.55 = (bf16[1024,1024]{1,0:T(8,128)(2,1)}, bf16[1024,1024]{1,0:T(8,128)(2,1)}, u32[]{:S(2)}, u32[]{:S(2)}) collective-permute-start(bf16[1024,1024]{1,0:T(8,128)(2,1)} %convolution_convert_fusion.4), channel_id=1, source_target_pairs={{0,2},{2,0},{4,6},{6,4},{8,10},{10,8},{12,14},{14,12},{16,18},{18,... | collective-permute-start | bytes 6291464 | tf_op jit(solution)/shard_map/ppermute | solution.py:280
  677.5 74.9 %collective-permute-start.50 = (bf16[1024,1024]{1,0:T(8,128)(2,1)}, bf16[1024,1024]{1,0:T(8,128)(2,1)}, u32[]{:S(2)}, u32[]{:S(2)}) collective-permute-start(bf16[1024,1024]{1,0:T(8,128)(2,1)} %convolution_convert_fusion.5), channel_id=1, source_target_pairs={{0,4},{2,6},{4,0},{6,2},{8,12},{10,14},{12,8},{14,10},{16,20},{18,... | collective-permute-start | bytes 6291464 | tf_op jit(solution)/shard_map/ppermute | solution.py:280
  681.4 51.2 %collective-permute-start.49 = (f32[576,128]{1,0:T(8,128)S(1)}, f32[576,128]{1,0:T(8,128)S(1)}, u32[]{:S(2)}, u32[]{:S(2)}) collective-permute-start(f32[576,128]{1,0:T(8,128)S(1)} %get-tuple-element.177), channel_id=1, source_target_pairs={{0,4},{2,6},{4,0},{6,2},{8,12},{10,14},{12,8},{14,10},{16,20},{18,... | collective-permute-start | bytes 884744 | tf_op jit(solution)/shard_map/ppermute | solution.py:280
  685.8 61.8 %collective-permute-start.71 = (bf16[96,2560]{1,0:T(8,128)(2,1)}, bf16[96,2560]{1,0:T(8,128)(2,1)}, u32[]{:S(2)}, u32[]{:S(2)}) collective-permute-start(bf16[96,2560]{1,0:T(8,128)(2,1)} %split.314), channel_id=1, source_target_pairs={{0,8},{2,10},{4,12},{6,14},{8,16},{10,18},{12,20},{14,22},{16,24},... | collective-permute-start | bytes 1474568 | tf_op jit(solution)/shard_map/ppermute | solution.py:280
  694.8 81.6 %collective-permute-start.66 = (bf16[512,1024]{1,0:T(8,128)(2,1)}, bf16[512,1024]{1,0:T(8,128)(2,1)S(1)}, u32[]{:S(2)}, u32[]{:S(2)}) collective-permute-start(bf16[512,1024]{1,0:T(8,128)(2,1)} %split.304), channel_id=1, source_target_pairs={{0,4},{2,6},{4,0},{6,2},{8,12},{10,14},{12,8},{14,10},{16,20},{18,... | collective-permute-start | bytes 3145736 | tf_op jit(solution)/shard_map/ppermute | solution.py:280
  732.6 46.5 %collective-permute-start.61 = (bf16[512,1024]{1,0:T(8,128)(2,1)}, bf16[512,1024]{1,0:T(8,128)(2,1)S(1)}, u32[]{:S(2)}, u32[]{:S(2)}) collective-permute-start(bf16[512,1024]{1,0:T(8,128)(2,1)} %split.298), channel_id=1, source_target_pairs={{0,2},{2,0},{4,6},{6,4},{8,10},{10,8},{12,14},{14,12},{16,18},{18,... | collective-permute-start | bytes 3145736 | tf_op jit(solution)/shard_map/ppermute | solution.py:280
  777.4 55.8 %collective-permute-start.73 = (bf16[96,2560]{1,0:T(8,128)(2,1)S(1)}, bf16[96,2560]{1,0:T(8,128)(2,1)S(1)}, u32[]{:S(2)}, u32[]{:S(2)}) collective-permute-start(bf16[96,2560]{1,0:T(8,128)(2,1)S(1)} %add_convert_fusion.21), channel_id=1, source_target_pairs={{0,8},{2,10},{4,12},{6,14},{8,16},{10,18},{12,20},{14,22},{16,24},... | collective-permute-start | bytes 1474568 | tf_op jit(solution)/shard_map/ppermute | solution.py:280
  779.1 48.4 %collective-permute-start.67 = (bf16[128,1024]{1,0:T(8,128)(2,1)S(1)}, bf16[128,1024]{1,0:T(8,128)(2,1)S(1)}, u32[]{:S(2)}, u32[]{:S(2)}) collective-permute-start(bf16[128,1024]{1,0:T(8,128)(2,1)S(1)} %split.308), channel_id=1, source_target_pairs={{0,8},{2,10},{4,12},{6,14},{8,16},{10,18},{12,20},{14,22},{16,24},... | collective-permute-start | bytes 786440 | tf_op jit(solution)/shard_map/ppermute | solution.py:280
  787.5 45.6 %collective-permute-start.62 = (bf16[128,1024]{1,0:T(8,128)(2,1)S(1)}, bf16[128,1024]{1,0:T(8,128)(2,1)S(1)}, u32[]{:S(2)}, u32[]{:S(2)}) collective-permute-start(bf16[128,1024]{1,0:T(8,128)(2,1)S(1)} %split.302), channel_id=1, source_target_pairs={{0,8},{2,10},{4,12},{6,14},{8,16},{10,18},{12,20},{14,22},{16,24},... | collective-permute-start | bytes 786440 | tf_op jit(solution)/shard_map/ppermute | solution.py:280
  798.7 68.3 %collective-permute-start.57 = (bf16[256,1024]{1,0:T(8,128)(2,1)S(1)}, bf16[256,1024]{1,0:T(8,128)(2,1)S(1)}, u32[]{:S(2)}, u32[]{:S(2)}) collective-permute-start(bf16[256,1024]{1,0:T(8,128)(2,1)S(1)} %add_convert_fusion.16), channel_id=1, source_target_pairs={{0,8},{2,10},{4,12},{6,14},{8,16},{10,18},{12,20},{14,22},{16,24},... | collective-permute-start | bytes 1572872 | tf_op jit(solution)/shard_map/ppermute | solution.py:280
  811.3 55.9 %collective-permute-start.52 = (bf16[256,1024]{1,0:T(8,128)(2,1)S(1)}, bf16[256,1024]{1,0:T(8,128)(2,1)S(1)}, u32[]{:S(2)}, u32[]{:S(2)}) collective-permute-start(bf16[256,1024]{1,0:T(8,128)(2,1)S(1)} %add_convert_fusion.19), channel_id=1, source_target_pairs={{0,8},{2,10},{4,12},{6,14},{8,16},{10,18},{12,20},{14,22},{16,24},... | collective-permute-start | bytes 1572872 | tf_op jit(solution)/shard_map/ppermute | solution.py:280
  (179 other events, 2695.3 us)

commit v2 on v1

--- a/solution.py
+++ b/solution.py
@@ -270,8 +270,9 @@
     "x": [(i, i ^ 1) for i in range(16)],
     "y": [(i, i ^ 2) for i in range(16)],
     "z": [(i, (i + 4) % 16) for i in range(16)],
+    "near": [(i, i ^ 4) for i in range(16)],
+    "far": [(i, i ^ 8) for i in range(16)],
 }
-PLACE = {"z": 0, "y": 1, "x": 2}
 CHIPS = 16
 SWAP = [(0, 1), (1, 0)]
 
@@ -288,58 +289,256 @@
     return pieces[0] if len(pieces) == 1 else jnp.concatenate(pieces, axis=0)
 
 
-def blocks_after(axes):
-    blocks = [(0, 0, 0)]
-    for axis in axes:
-        place = PLACE[axis]
-        count = 4 if axis == "z" else 2
-        blocks = [
-            block[:place] + (away,) + block[place + 1 :] for away in range(count) for block in blocks
-        ]
+def add(one, other):
+    return one.astype(jnp.float32) + other.astype(jnp.float32)
+
+
+FIRST = {"a": "x", "b": "y"}
+LAST = {"a": "y", "b": "x"}
+
+
+def moves_of(kind):
+    moves = {}
+    if kind == "Q":
+        for turn in (1, 2, 3):
+            moves["z", turn] = ("z", 2, [("z", turn - 1)] if turn > 1 else [])
+    for part in "ab":
+        if kind == "P":
+            moves[part, "first"] = (FIRST[part], 1, [])
+            for turn in (1, 2, 3):
+                before = (part, "z", turn - 1) if turn > 1 else (part, "first")
+                moves[part, "z", turn] = ("z", 2, [before])
+            for half in (0, 1):
+                moves[part, "last", half] = (LAST[part], 4, [(part, "z", 1 + 2 * half)])
+        else:
+            for half in (0, 1):
+                moves[part, "first", half] = (FIRST[part], 2, [("z", 1 + 2 * half)])
+                moves[part, "last", half] = (LAST[part], 4, [(part, "first", half)])
+    return moves
+
+
+def back_moves_of(kind):
+    moves = {}
+    for part in "ab":
+        for half in (0, 1):
+            moves[part, "last", half] = (LAST[part], 4, [])
+        if kind == "P":
+            moves[part, "z", 1] = ("z", 2, [(part, "last", 0)])
+            moves[part, "z", 2] = ("z", 2, [(part, "z", 1), (part, "last", 1)])
+            moves[part, "z", 3] = ("z", 2, [(part, "z", 2)])
+            moves[part, "first"] = (FIRST[part], 1, [(part, "z", 3)])
+        else:
+            for half in (0, 1):
+                moves[part, "first", half] = (FIRST[part], 2, [(part, "last", half)])
+    if kind == "Q":
+        moves["z", 1] = ("z", 2, [("a", "first", 0), ("b", "first", 0)])
+        moves["z", 2] = ("z", 2, [("z", 1), ("a", "first", 1), ("b", "first", 1)])
+        moves["z", 3] = ("z", 2, [("z", 2)])
+    return moves
+
+
+def ordered_moves(moves, ready, lag=0.5):
+    ended, free, order = {}, {"x": 0.0, "y": 0.0, "z": 0.0}, []
+    ranks = {name: rank for rank, name in enumerate(moves)}
+    waiting = dict(moves)
+    while waiting:
+        best = None
+        for name, (axis, size, needs) in waiting.items():
+            if all(need in ended for need in needs):
+                start = max([ready.get(name[0], 0.0), free[axis]] + [ended[need] + lag for need in needs])
+                if best is None or (start, ranks[name]) < best[:2]:
+                    best = (start, ranks[name], name)
+        start, _, name = best
+        axis, size, _ = waiting.pop(name)
+        ended[name] = free[axis] = start + size
+        order.append(name)
+    return order
+
+
+class Links:
+    def __init__(self):
+        self.sent = {"x": [], "y": [], "z": []}
+
+    def send(self, value, axis, way=None):
+        sent = self.sent[axis]
+        if len(sent) > 1:
+            value, _ = lax.optimization_barrier((value, sent[-2]))
+        sent.append(step(value, way or axis))
+        return sent[-1]
+
+
+def blocks_of(kind, part):
+    blocks = []
+    for last in (0, 1):
+        for half in (0, 1):
+            turns = (2 * half, 2 * half + 1)
+            if kind == "P":
+                pairs = [(turn, first) for turn in turns for first in (0, 1)]
+            else:
+                pairs = [(turn, first) for first in (0, 1) for turn in turns]
+            for turn, first in pairs:
+                blocks.append((turn, first, last) if part == "b" else (turn, last, first))
     return blocks
 
 
-def owners(axes, here):
+def owners(blocks, here):
     z, y, x = here // 4, (here // 2) % 2, here % 2
     return jnp.stack(
-        [
-            ((z - dz) % 4) * 4 + (y + dy) % 2 * 2 + (x + dx) % 2
-            for dz, dy, dx in blocks_after(axes)
-        ]
+        [((z - dz) % 4) * 4 + (y + dy) % 2 * 2 + (x + dx) % 2 for dz, dy, dx in blocks]
     ).astype(jnp.int32)
 
 
-def gather_blocks(shard, axes):
-    pieces = [shard]
-    for axis in axes:
-        pieces = [joined(pieces)]
-        for _ in range(3 if axis == "z" else 1):
-            pieces.append(step(pieces[-1], axis))
-    return pieces
-
-
-def add(one, other):
-    return one.astype(jnp.float32) + other.astype(jnp.float32)
-
-
-def scatter_blocks(pieces, axes, dtype=jnp.bfloat16):
-    for place in reversed(range(len(axes))):
-        axis = axes[place]
-        travelling = pieces[1].astype(dtype)
-        for later in pieces[2:]:
-            travelling = add(later, step(travelling, axis)).astype(dtype)
-        total = add(pieces[0], step(travelling, axis))
-        if place:
-            count = 4 if axes[place - 1] == "z" else 2
-            pieces = jnp.split(total.astype(dtype), count, axis=0)
-    return total
-
-
-def reorder(rows, old, new):
-    height = rows.shape[0] // len(old)
-    if old == new:
-        return rows
-    return joined([rows[old.index(block) * height :][:height] for block in new])
+def gather_matrices(shards, kinds):
+    moves = {}
+    for name, kind in kinds.items():
+        for move, (axis, size, needs) in moves_of(kind).items():
+            moves[(name,) + move] = (axis, size, [(name,) + need for need in needs])
+    links, got, sent = Links(), {}, {}
+    for move in ordered_moves(moves, {}):
+        name, kind = move[0], kinds[move[0]]
+        parts = dict(zip("ab", shards[name]))
+        if kind == "P":
+            part, stage = move[1:3]
+            if stage == "first":
+                value = parts[part]
+            elif stage == "z":
+                if move[3] == 1:
+                    sent[name, part, "pair"] = joined([parts[part], got[name, part, "first"]])
+                    value = sent[name, part, "pair"]
+                else:
+                    value = got[name, part, "z", move[3] - 1]
+            else:
+                pairs = [sent[name, part, "pair"]] + [got[name, part, "z", turn] for turn in (1, 2, 3) if turn <= 1 + 2 * move[3]]
+                value = joined(pairs[2 * move[3] :])
+        elif move[1] == "z":
+            value = joined_lanes(shards[name]) if move[2] == 1 else got[name, "z", move[2] - 1]
+        else:
+            part, stage, half = move[1:]
+            if stage == "first":
+                width = parts["a"].shape[1]
+                lanes = slice(0, width) if part == "a" else slice(width, None)
+                rows = [
+                    got[name, "z", turn][:, lanes] if turn else parts[part]
+                    for turn in (2 * half, 2 * half + 1)
+                ]
+                value = joined(rows)
+            else:
+                value = joined([sent[name, part, "first", half], got[name, part, "first", half]])
+        sent[move] = value
+        got[move] = links.send(value, moves[move][0])
+    full = {
+        (name, part): [held[name, part, "last", half] for held in (sent, got) for half in (0, 1)]
+        for name in kinds
+        for part in "ab"
+    }
+    return full, got
+
+
+def joined_lanes(pieces):
+    return jnp.concatenate(pieces, axis=1)
+
+
+SMALL_MOVES = {
+    ("small", "x"): ("x", 1, []),
+    ("small", "y"): ("y", 1, [("small", "x")]),
+    ("small", "near"): ("z", 1, [("small", "y")]),
+    ("small", "far"): ("z", 2, [("small", "near")]),
+}
+
+
+def scatter_matrices(grads, kinds, small, ready):
+    low = jnp.bfloat16
+    moves = {}
+    for name, kind in kinds.items():
+        for move, (axis, size, needs) in back_moves_of(kind).items():
+            moves[(name,) + move] = (axis, size, [(name,) + need for need in needs])
+    moves = {**SMALL_MOVES, **moves}
+    links, got, held = Links(), {}, {}
+
+    def kept(name, part, half):
+        key = (name, part, half)
+        if key not in held:
+            held[key] = add(grads[name, part][half], got[name, part, "last", half]).astype(low)
+        return held[key]
+
+    def pair(name, part, turn):
+        rows = kept(name, part, turn // 2)
+        height = rows.shape[0] // 2
+        return rows[(turn % 2) * height :][:height]
+
+    def both(name, turn):
+        rows = []
+        for part in "ab":
+            half = turn // 2
+            key = (name, part, "both", half)
+            if key not in held:
+                own = kept(name, part, half)
+                held[key] = add(own[: own.shape[0] // 2], got[name, part, "first", half])
+            height = held[key].shape[0] // 2
+            rows.append(held[key][(turn % 2) * height :][:height])
+        return joined_lanes(rows)
+
+    for move in ordered_moves(moves, ready):
+        if move in SMALL_MOVES:
+            small = small.astype(low)
+            small = add(small, links.send(small, moves[move][0], move[1]))
+            continue
+        name, kind = move[0], kinds[move[0]]
+        if "last" in move:
+            value = grads[name, move[1]][2 + move[3]]
+        elif kind == "P" and move[2] == "z":
+            part, turn = move[1], move[3]
+            value = pair(name, part, turn)
+            if turn > 1:
+                value = add(value, got[name, part, "z", turn - 1]).astype(low)
+        elif kind == "P":
+            part = move[1]
+            total = add(pair(name, part, 0), got[name, part, "z", 3])
+            held[name, part, "own"] = total[: total.shape[0] // 2]
+            value = total[total.shape[0] // 2 :].astype(low)
+        elif move[1] == "z":
+            turn = move[2]
+            value = both(name, turn)
+            if turn > 1:
+                value = add(value, got[name, "z", turn - 1])
+            value = value.astype(low)
+        else:
+            part, half = move[1], move[3]
+            own = kept(name, part, half)
+            value = own[own.shape[0] // 2 :]
+        got[move] = links.send(value, moves[move][0])
+    sums = {}
+    for name, kind in kinds.items():
+        if kind == "P":
+            sums[name] = joined_lanes(
+                [add(held[name, part, "own"], got[name, part, "first"]) for part in "ab"]
+            )
+        else:
+            sums[name] = add(both(name, 0), got[name, "z", 3])
+    return sums, small
+
+
+def moved_blocks(buffers, old, new, count):
+    rows, width = buffers[0].shape
+    height = rows * len(buffers) // len(old)
+    per_source, per_target = len(old) // len(buffers), len(new) // count
+
+    def kernel(*refs):
+        sources, targets = refs[: len(buffers)], refs[len(buffers) :]
+        for spot, block in enumerate(new):
+            place = old.index(block)
+            source, target = sources[place // per_source], targets[spot // per_target]
+            first, place = spot % per_target * height, place % per_source * height
+            target[first : first + height] = source[place : place + height]
+
+    vmem = pl.BlockSpec(memory_space=pltpu.VMEM)
+    return pl.pallas_call(
+        kernel,
+        out_shape=[jax.ShapeDtypeStruct((height * per_target, width), buffers[0].dtype)] * count,
+        in_specs=[vmem] * len(buffers),
+        out_specs=[vmem] * count,
+        compiler_params=pltpu.CompilerParams(vmem_limit_bytes=24 * 1024 * 1024),
+    )(*buffers)
 
 
 def pair_sum(partial_value):
@@ -377,22 +576,6 @@
         in_specs=[pl.BlockSpec(memory_space=pltpu.SMEM), vmem, vmem],
         out_specs=[vmem] * order.shape[0],
     )(order, own, other)
-
-
-def take_kernel(order_ref, rows_ref, out_ref):
-    for block in range(out_ref.shape[0]):
-        out_ref[block] = rows_ref[order_ref[block]]
-
-
-def take_blocks(order, rows):
-    blocks = rows.reshape(CHIPS, -1, rows.shape[1])
-    vmem = pl.BlockSpec(memory_space=pltpu.VMEM)
-    return pl.pallas_call(
-        take_kernel,
-        out_shape=jax.ShapeDtypeStruct(blocks.shape, blocks.dtype),
-        in_specs=[pl.BlockSpec(memory_space=pltpu.SMEM), vmem],
-        out_specs=vmem,
-    )(order, blocks).reshape(rows.shape)
 
 
 def unpermute_kernel(order_ref, first_ref, second_ref, own_ref, other_ref, total_ref):
@@ -423,10 +606,10 @@
     )(order, first, second)
 
 
-FIRST_AXES = "xzy"
-SECOND_AXES = "yzx"
-HIGHWAY_AXES = (("xzy", "yzx"), ("zxy", "zyx"))
-SMALL_AXES = "zxy"
+READY = {"highway1": 12.0, "highway0": 16.0, "small": 24.0}
+CONV_AFTER = [("highway0", "b", "z", 1)]
+GATHER_KINDS = {"highway0": "P", "highway1": "Q", "encoder": "P"}
+SCATTER_KINDS = {"encoder": "P", "highway1": "P", "highway0": "Q"}
 
 
 def times_pieces(values, pieces):
@@ -440,25 +623,22 @@
     )
 
 
-def sum_over_wide(values, routed):
-    if not routed:
-        return lax.psum(values, "wide")
+def packed(values):
+    width = 1024
     flat = [value.reshape(-1) for value in values]
-    flat = [jnp.pad(value, (0, -value.shape[0] % 128)).reshape(-1, 128) for value in flat]
+    flat = [jnp.pad(value, (0, -value.shape[0] % width)).reshape(-1, width) for value in flat]
     rows = jnp.concatenate(flat, axis=0)
-    used = rows.shape[0]
-    rows = jnp.pad(rows, ((0, -used % (8 * CHIPS)), (0, 0)))
-    order = owners(SMALL_AXES, lax.axis_index("wide"))
-    spots = jnp.arange(CHIPS, dtype=jnp.int32)
-    places = jnp.sum(jnp.where(order[None, :] == spots[:, None], spots[None, :], 0), axis=1)
-    rows = take_blocks(order, rows)
-    own = scatter_blocks(jnp.split(rows, 2, axis=0), SMALL_AXES, jnp.float32)
-    rows = take_blocks(places, joined(gather_blocks(own, SMALL_AXES)))
+    return jnp.pad(rows, ((0, -rows.shape[0] % 16), (0, 0)))
+
+
+def unpacked(rows, values):
     totals = []
     first = 0
-    for value, piece in zip(values, flat):
-        totals.append(rows[first : first + piece.shape[0]].reshape(-1)[: value.size].reshape(value.shape))
-        first += piece.shape[0]
+    for value in values:
+        count = -(-value.size // rows.shape[1])
+        taken = rows[first : first + count].reshape(-1)
+        totals.append(taken[: value.size].reshape(value.shape))
+        first += count
     return totals
 
 
@@ -522,11 +702,6 @@
     scale_row, bias_row = chan_scale[None, :], conv_bias[None, :]
     width_row = widths.astype(f32)[None, :]
     pool, pool_back = conv_calls(word_count, own_filters)
-    embedded, pooled, pool_shift = pool(
-        tile_chunks, spread_ids, table_t, tap_lanes, masked_filters, scale_row, bias_row, lens,
-        width_row,
-    )
-    current = gelu_exact(pooled).astype(bf16)
     here = lax.axis_index("wide")
     core = lax.axis_index("narrow")
     routed = lax.axis_size("wide") == CHIPS
@@ -538,36 +713,53 @@
     )
     second_rows = jnp.concatenate([up_weight, down_weight.T], axis=1)
 
-    def whole_rows(shard, axes):
-        if routed:
-            return gather_blocks(shard, axes)
-        return [lax.all_gather(shard, "wide", axis=0, tiled=True)]
-
-    def own_rows(pieces, axes):
-        if routed:
-            return scatter_blocks(pieces, axes)
-        return lax.psum_scatter(
-            joined(pieces).astype(f32), "wide", scatter_dimension=0, tiled=True
+    def whole_rows(shard):
+        return lax.all_gather(shard, "wide", axis=0, tiled=True)
+
+    def own_rows(terms):
+        return lax.psum_scatter(terms.astype(f32), "wide", scatter_dimension=0, tiled=True)
+
+    arrived = {}
+
+    def after(value, moves):
+        ended = [arrived[move] for move in moves if move in arrived]
+        return lax.optimization_barrier((value, *ended))[0] if ended else value
+
+    if routed:
+        full, arrived = gather_matrices(
+            {
+                "highway0": [highway_weight[0, :, part] for part in range(2)],
+                "highway1": [highway_weight[1, :, part] for part in range(2)],
+                "encoder": [first_rows, second_rows],
+            },
+            GATHER_KINDS,
         )
-
-    def halves(rows):
-        return jnp.split(rows, 2, axis=0) if routed else [rows]
-
-    highway_full = [
-        [whole_rows(highway_weight[layer, :, part], HIGHWAY_AXES[layer][part]) for part in range(2)]
-        for layer in range(HW_LAYERS)
-    ]
-    first_full = joined(whole_rows(first_rows, FIRST_AXES))
-    second_full = joined(whole_rows(second_rows, SECOND_AXES))
-    if routed:
-        second_full = reorder(second_full, blocks_after(SECOND_AXES), blocks_after(FIRST_AXES))
-        feature_order = owners(FIRST_AXES, here)
+        highway_full = [
+            [full[f"highway{layer}", part] for part in "ab"] for layer in range(HW_LAYERS)
+        ]
+        gathered_blocks = {part: blocks_of(GATHER_KINDS["encoder"], part) for part in "ab"}
+        scattered_blocks = {part: blocks_of(SCATTER_KINDS["encoder"], part) for part in "ab"}
+        features = gathered_blocks["a"]
+        first_full, second_full = [
+            moved_blocks(full["encoder", part], gathered_blocks[part], features, 1)[0]
+            for part in "ab"
+        ]
+        feature_order = owners(features, here)
     else:
+        highway_full = [
+            [[whole_rows(highway_weight[layer, :, part])] for part in range(2)]
+            for layer in range(HW_LAYERS)
+        ]
+        first_full, second_full = whole_rows(first_rows), whole_rows(second_rows)
         feature_order = jnp.arange(lax.axis_size("wide"), dtype=jnp.int32)
+    embedded, pooled, pool_shift = pool(
+        after(tile_chunks, CONV_AFTER), spread_ids, table_t, tap_lanes, masked_filters, scale_row, bias_row, lens,
+        width_row,
+    )
+    current = gelu_exact(pooled).astype(bf16)
     proj_t, qkv_full, out_t = jnp.split(
         first_full, [width_proj, width_proj + width_qkv], axis=1
     )
-    qkv_full = qkv_full.reshape(-1, 3, qkv_weight.shape[2])
     up_full, down_t = jnp.split(second_full, [width_up], axis=1)
     feature_count = proj_t.shape[0]
     feature_picks = (
@@ -593,12 +785,20 @@
     kept_layers = []
     for layer_index in range(HW_LAYERS):
         if routed:
-            order = jnp.stack([owners(axes, here) for axes in HIGHWAY_AXES[layer_index]])
-            order = (order - core * (CHIPS // 2)) % CHIPS
-            whole_input = permute_channels(order, current, swap(current))
+            name = f"highway{layer_index}"
+            orders = {}
+            for kind in (GATHER_KINDS[name], SCATTER_KINDS[name]):
+                order = jnp.stack([owners(blocks_of(kind, part), here) for part in "ab"])
+                orders[kind] = (order - core * (CHIPS // 2)) % CHIPS
+            order = orders[GATHER_KINDS[name]]
+            whole_input = permute_channels(
+                jnp.concatenate(list(orders.values())), current, swap(current)
+            )
+            grad_input = whole_input[-2:]
         else:
             order = None
             whole_input = [lax.all_gather(current, "narrow", axis=1, tiled=True)] * 2
+            grad_input = whole_input
         mixed_pre = (
             jnp.stack(
                 [
@@ -610,21 +810,20 @@
             + highway_bias[layer_index]
         )
         carried = current.astype(f32)
-        kept_layers.append((whole_input, mixed_pre, carried, order))
+        kept_layers.append((grad_input, mixed_pre, carried, order))
         current = highway_mix(mixed_pre, carried).astype(bf16)
     start_rows = (
         pair_sum(jnp.dot(current, proj_t.T, preferred_element_type=f32)) + vector_biases[0]
     )
     start_low = start_rows.astype(bf16)
-    qkv_bias = jnp.stack([qv_bias[0], jnp.zeros_like(qv_bias[0]), qv_bias[1]])
+    qkv_bias = jnp.concatenate([qv_bias[0], jnp.zeros_like(qv_bias[0]), qv_bias[1]])
     projected = (
-        jnp.einsum("wd,dgc->wgc", start_low, qkv_full, preferred_element_type=f32) + qkv_bias
+        jnp.dot(start_low, qkv_full, preferred_element_type=f32) + qkv_bias
     ).astype(bf16)
-    heads_here = qkv_full.shape[2] // HEAD_DIM
-    head_shape = (word_count, heads_here, HEAD_DIM)
-    query = projected[:, 0].reshape(head_shape)
-    keys_here = projected[:, 1].reshape(head_shape)
-    values_here = projected[:, 2].reshape(head_shape)
+    head_shape = (word_count, -1, HEAD_DIM)
+    query, keys_here, values_here = [
+        part.reshape(head_shape) for part in jnp.split(projected, 3, axis=1)
+    ]
     attn_scale = HEAD_DIM ** (-0.5)
     sequence = jnp.arange(word_count, dtype=jnp.int32) // 8 % seq_count
     together = (sequence[:, None] == sequence[None, :])[None]
@@ -686,39 +885,32 @@
     grad_key = (
         jnp.einsum("hqk,qhe->khe", grad_scores, query, preferred_element_type=f32) * attn_scale
     )
-    grad_projected = jnp.stack(
-        [
-            grad_query.reshape(word_count, -1),
-            grad_key.reshape(word_count, -1),
-            grad_value.reshape(word_count, -1),
-        ],
+    grad_projected = jnp.concatenate(
+        [grad.reshape(word_count, -1).astype(bf16) for grad in (grad_query, grad_key, grad_value)],
         axis=1,
-    ).astype(bf16)
-    qkv_grad_local = jnp.einsum(
-        "wd,wgc->dgc", start_low, grad_projected, preferred_element_type=f32
-    )
-    bias_qv = jnp.sum(grad_projected[:, 0::2].astype(f32), axis=0)
+    )
+    qkv_grad_local = jnp.dot(start_low.T, grad_projected, preferred_element_type=f32)
+    bias_qkv = jnp.sum(grad_projected.astype(f32), axis=0).reshape(3, -1)
+    bias_qv = bias_qkv[0::2]
     grad_start = grad_before_one + pair_grad_sum(
-        jnp.einsum("wgc,dgc->wd", grad_projected, qkv_full, preferred_element_type=f32)
+        jnp.dot(grad_projected, qkv_full.T, preferred_element_type=f32)
     )
     grad_start_low = grad_start.astype(bf16)
     proj_grad_local = jnp.dot(grad_start_low.T, current, preferred_element_type=f32)
     bias_start = jnp.sum(grad_start_low.astype(f32), axis=0)
     grad_current = jnp.dot(grad_start_low, proj_t, preferred_element_type=f32)
     first_grad_local = jnp.concatenate(
-        [proj_grad_local, qkv_grad_local.reshape(feature_count, width_qkv), out_grad_local], axis=1
+        [proj_grad_local, qkv_grad_local, out_grad_local], axis=1
     ).astype(bf16)
     second_grad_local = jnp.concatenate([up_grad_local, down_grad_local], axis=1).astype(bf16)
+    terms = {}
     if routed:
-        second_grad_local = reorder(
-            second_grad_local, blocks_after(FIRST_AXES), blocks_after(SECOND_AXES)
-        )
-    second_grad = own_rows(halves(second_grad_local), SECOND_AXES)
-    first_grad = own_rows(halves(first_grad_local), FIRST_AXES)
+        for part, local in (("a", first_grad_local), ("b", second_grad_local)):
+            terms["encoder", part] = moved_blocks([local], features, scattered_blocks[part], 4)
     highway_grads = []
     highway_bias_grads = []
     for layer_index in reversed(range(HW_LAYERS)):
-        whole_input, mixed_pre, carried, order = kept_layers[layer_index]
+        grad_input, mixed_pre, carried, order = kept_layers[layer_index]
         mix_back = jax.vjp(highway_mix, mixed_pre, carried)[1]
         grad_mixed, grad_carried = mix_back(grad_current)
         grad_mixed_low = grad_mixed.astype(bf16)
@@ -728,13 +920,10 @@
             part_mixed = grad_mixed_low[:, part]
             pieces = highway_full[layer_index][part]
             part_grads.append(
-                own_rows(
-                    [
-                        jnp.dot(columns.T, part_mixed, preferred_element_type=f32).astype(bf16)
-                        for columns in jnp.split(whole_input[part], len(pieces), axis=1)
-                    ],
-                    HIGHWAY_AXES[layer_index][part],
-                )
+                [
+                    jnp.dot(columns.T, part_mixed, preferred_element_type=f32).astype(bf16)
+                    for columns in jnp.split(grad_input[part], len(pieces), axis=1)
+                ]
             )
             grad_whole.append(
                 jnp.concatenate(
@@ -745,7 +934,12 @@
                     axis=1,
                 )
             )
-        highway_grads.insert(0, jnp.stack(part_grads, axis=1))
+        if routed:
+            terms.update(zip([(f"highway{layer_index}", part) for part in "ab"], part_grads))
+        else:
+            highway_grads.insert(
+                0, jnp.stack([own_rows(joined(pieces)) for pieces in part_grads], axis=1)
+            )
         highway_bias_grads.insert(0, jnp.sum(grad_mixed_low.astype(f32), axis=0))
         if routed:
             grad_own, grad_other = unpermute_sum(order, *grad_whole)
@@ -754,7 +948,6 @@
             grad_current = grad_carried + lax.psum_scatter(
                 add(*grad_whole).astype(bf16), "narrow", scatter_dimension=1, tiled=True
             ).astype(f32)
-    highway_grad = jnp.stack(highway_grads)
     highway_bias_local = jnp.stack(highway_bias_grads)
     grad_pooled = jax.vjp(gelu_exact, pooled)[1](grad_current)[0]
     grad_filter, grad_marks = pool_back(
@@ -768,16 +961,37 @@
         grad_marks[:, : TAPS * CHAR_DIM].reshape(CHAR_VOCAB, TAPS, CHAR_DIM), axis=1
     )
     grad_filter = grad_filter * tap_mask.astype(f32)
+    bias_local = pick_features(
+        jnp.stack([bias_start, bias_attended, bias_down, bias_one, bias_two]), feature_picks.T
+    )
+    gain_local = pick_features(jnp.stack([gain_one, gain_two]), feature_picks.T)
+    locals_small = (
+        grad_filter,
+        grad_conv_bias,
+        highway_bias_local,
+        bias_qv,
+        bias_up,
+        bias_local,
+        gain_local,
+        pair_sum(grad_chars),
+    )
+    if routed:
+        sums, small = scatter_matrices(terms, SCATTER_KINDS, packed(locals_small), READY)
+        small_sums = unpacked(small, locals_small)
+        highway_grads = [
+            sums[f"highway{layer}"].reshape(highway_weight.shape[1:]) for layer in range(HW_LAYERS)
+        ]
+        first_grad, second_grad = jnp.split(sums["encoder"], [first_rows.shape[1]], axis=1)
+    else:
+        first_grad, second_grad = own_rows(first_grad_local), own_rows(second_grad_local)
+        small_sums = lax.psum(locals_small, "wide")
+    highway_grad = jnp.stack(highway_grads)
     proj_grad, qkv_grad, out_grad = jnp.split(
         first_grad, [width_proj, width_proj + width_qkv], axis=1
     )
     up_grad, down_grad = jnp.split(second_grad, [width_up], axis=1)
     proj_grad, out_grad, down_grad = proj_grad.T, out_grad.T, down_grad.T
     qkv_grad = qkv_grad.reshape(qkv_weight.shape)
-    bias_local = pick_features(
-        jnp.stack([bias_start, bias_attended, bias_down, bias_one, bias_two]), feature_picks.T
-    )
-    gain_local = pick_features(jnp.stack([gain_one, gain_two]), feature_picks.T)
     (
         conv_grad,
         conv_bias_grad,
@@ -787,19 +1001,7 @@
         bias_grads,
         gain_grads,
         char_grad,
-    ) = sum_over_wide(
-        (
-            grad_filter,
-            grad_conv_bias,
-            highway_bias_local,
-            bias_qv,
-            bias_up,
-            bias_local,
-            gain_local,
-            pair_sum(grad_chars),
-        ),
-        routed,
-    )
+    ) = small_sums
     return (
         encoded,
         char_grad,

time: 908 us -> 660 us (0.73)
  waiting for transfers between devices: 470 us -> 265 us
  local copies, waits for them, and re-layouts: 116 us -> 53.6 us
  Pallas kernels: 67.6 us -> 80.6 us
  starting transfers between devices: 58.1 us -> 68.1 us
    ppermute x70 -> x74, waiting for transfers between devices: 470 us -> 263 us  [step(): return lax.ppermute(value, 'wide', STEPS[axis])]
    unnamed x309 -> x427, local copies, waits for them, and re-layouts: 60.3 us -> 24.4 us
    ppermute x70 -> x74, starting transfers between devices: 56 us -> 66.9 us  [step(): return lax.ppermute(value, 'wide', STEPS[axis])]
    split x18 -> x4, local copies, waits for them, and re-layouts: 11.3 us -> 0.5 us  [per_device(): jnp.split(projected, 3, axis=1)]
    pallas_call x3 -> x5, Pallas kernels: 24.7 us -> 30.4 us  [the longest x1 23.1 us: per_device(): pool(after(tile_chunks, CONV_AFTER), spread_ids, table_t, tap_lanes, mask...]
    convert_element_type x24 -> x18, other arithmetic: 22.9 us -> 17.4 us  [the longest x5 8.97 us: kept(): add(grads[name, part][half], got[name, part, 'last', half]).astype(low)]
    dot_general x8 -> x16, matrix products: 17.6 us -> 22.2 us  [per_device(): jnp.dot(columns.T, part_mixed, preferred_element_type=f32).astype(bf16)]
    dot_general x8 -> x16, matrix products: 19.5 us -> 15.7 us  [per_device(): jnp.dot(part_mixed, piece.T, preferred_element_type=f32)]
  transfers between devices with their start and end apart: 80 -> 84, of which waited for: 41 -> 35; matrix products, arithmetic and copies ran while one was open for 26% -> 28% of each run, Pallas kernels for 8% -> 12%
where the time goes in v2:
time: 660 us; the launch traced here: 651 us
  waiting for transfers between devices  265 us (40%)
  matrix products  96.5 us (15%)
  other arithmetic  82.1 us (12%)
  Pallas kernels  80.6 us (12%)
  starting transfers between devices  68.1 us (10%)
  local copies, waits for them, and re-layouts  53.6 us (8%)
    ppermute x74, waiting for transfers between devices, step(): return lax.ppermute(value, 'wide', STEPS[axis])  263 us
    ppermute x74, starting transfers between devices, step(): return lax.ppermute(value, 'wide', STEPS[axis])  66.9 us
    pallas_call x1, Pallas kernels, per_device(): pool_back(tile_chunks, spread_ids, tap_lanes, masked_filters, scale_row,...  37 us
    unnamed x427, local copies, waits for them, and re-layouts  24.4 us
    pallas_call x1, Pallas kernels, per_device(): pool(after(tile_chunks, CONV_AFTER), spread_ids, table_t, tap_lanes, mask...  23.1 us
    dot_general x16, matrix products, per_device(): jnp.dot(columns.T, part_mixed, preferred_element_type=f32).astype(bf16)  22.2 us
    dot_general x16, matrix products, times_pieces(): jnp.dot(column, piece, preferred_element_type=jnp.float32)  17 us
    dot_general x16, matrix products, per_device(): jnp.dot(part_mixed, piece.T, preferred_element_type=f32)  15.7 us
  transfers between devices with their start and end apart: 84, of which 35 were waited for; matrix products, arithmetic and copies ran while one was open for 28% of the time, Pallas kernels for 12%

profile of v2, /device:TPU:0, one launch (start us, length us, event | category | flops | bytes accessed | tf_op | source)
XLA Modules:
  0.0 651.1 jit_solution(13133029859160373924)
XLA Ops:
  34.9 7.3 %collective-permute-done.5 = bf16[256,1024]{1,0:T(8,128)(2,1)S(1)} collective-permute-done((bf16[256,1024]{1,0:T(8,128)(2,1)S(1)}, bf16[256,1024]{1,0:T(8,128)(2,1)S(1)}, u32[]{:S(2)}, u32[]{:S(2)}) %collective-permute-start.5) | collective-permute-done | bytes 524320 | tf_op jit(solution)/shard_map/ppermute | solution.py:281
  44.8 8.6 %collective-permute-done.2 = bf16[256,1024]{1,0:T(8,128)(2,1)S(1)} collective-permute-done((bf16[256,1024]{1,0:T(8,128)(2,1)S(1)}, bf16[256,1024]{1,0:T(8,128)(2,1)S(1)}, u32[]{:S(2)}, u32[]{:S(2)}) %collective-permute-start.2) | collective-permute-done | bytes 524320 | tf_op jit(solution)/shard_map/ppermute | solution.py:281
  53.5 23.1 %shard_map.289 = (bf16[64,256,128]{2,1,0:T(8,128)(2,1)S(1)}, f32[256,1024]{1,0:T(8,128)S(1)}, f32[256,1024]{1,0:T(8,128)S(1)}) custom-call(s32[16]{0:T(128)S(1)} %and_select_fusion.4.tile_ref, s32[128,128]{1,0:T(8,128)S(1)} %reshape.729.ids_ref, bf16[128,272]{1,0:T(8,128)(2,1)S(1)} %pad.54.table_ref, f32[8,128]{1,0:T(8,128)S(1)} %fusion.231.lanes_ref, ...), custom_call_target="tpu_custom_call" | custom-call | flops 5000000000 | bytes 8000000 | tf_op jit(solution)/shard_map/pallas_call | solution.py:755
  87.5 5.2 shard_map.290
  102.8 10.6 %collective-permute-done.12 = bf16[256,1024]{1,0:T(8,128)(2,1)S(1)} collective-permute-done((bf16[256,1024]{1,0:T(8,128)(2,1)}, bf16[256,1024]{1,0:T(8,128)(2,1)S(1)}, u32[]{:S(2)}, u32[]{:S(2)}) %collective-permute-start.12) | collective-permute-done | bytes 524320 | tf_op jit(solution)/shard_map/ppermute | solution.py:281
  115.0 16.3 %collective-permute-done.14 = bf16[512,1024]{1,0:T(8,128)(2,1)} collective-permute-done((bf16[512,1024]{1,0:T(8,128)(2,1)}, bf16[512,1024]{1,0:T(8,128)(2,1)}, u32[]{:S(2)}, u32[]{:S(2)}) %collective-permute-start.14) | collective-permute-done | bytes 1048608 | tf_op jit(solution)/shard_map/ppermute | solution.py:281
  134.8 4.5 collective-permute-start.29
  141.4 9.8 %collective-permute-done.21 = bf16[128,2048]{1,0:T(8,128)(2,1)S(1)} collective-permute-done((bf16[128,2048]{1,0:T(8,128)(2,1)S(1)}, bf16[128,2048]{1,0:T(8,128)(2,1)S(1)}, u32[]{:S(2)}, u32[]{:S(2)}) %collective-permute-start.21) | collective-permute-done | bytes 524320 | tf_op jit(solution)/shard_map/ppermute | solution.py:281
  153.8 7.9 %collective-permute-done.29 = bf16[96,2560]{1,0:T(8,128)(2,1)S(1)} collective-permute-done((bf16[96,2560]{1,0:T(8,128)(2,1)S(1)}, bf16[96,2560]{1,0:T(8,128)(2,1)S(1)}, u32[]{:S(2)}, u32[]{:S(2)}) %collective-permute-start.29) | collective-permute-done | bytes 491552 | tf_op jit(solution)/shard_map/ppermute | solution.py:281
  165.1 5.5 fusion.58
  180.8 4.1 collective-permute-done.30
  188.6 5.1 shard_map.291
  203.3 25.2 %collective-permute-done.31.refs_3_ = bf16[192,2560]{1,0:T(8,128)(2,1)} collective-permute-done((bf16[192,2560]{1,0:T(8,128)(2,1)}, bf16[192,2560]{1,0:T(8,128)(2,1)}, u32[]{:S(2)}, u32[]{:S(2)}) %collective-permute-start.31) | collective-permute-done | bytes 983072 | tf_op jit(solution)/shard_map/ppermute | solution.py:281
  251.6 18.7 %collective-permute-done.38.refs_3_ = bf16[192,3072]{1,0:T(8,128)(2,1)} collective-permute-done((bf16[192,3072]{1,0:T(8,128)(2,1)}, bf16[192,3072]{1,0:T(8,128)(2,1)}, u32[]{:S(2)}, u32[]{:S(2)}) %collective-permute-start.38) | collective-permute-done | bytes 1179680 | tf_op jit(solution)/shard_map/ppermute | solution.py:281
  275.7 5.7 multiply_convert_fusion.1
  410.1 37.0 %shard_map.296 = (f32[128,1024]{1,0:T(8,128)S(1)}, f32[272,256]{1,0:T(8,128)S(1)}) custom-call(s32[16]{0:T(128)S(1)} %copy-done.24, s32[128,128]{1,0:T(8,128)S(1)} %copy-done.21, f32[8,128]{1,0:T(8,128)S(1)} %fusion.231.lanes_ref, bf16[128,1024]{1,0:T(8,128)(2,1)S(1)} %copy-done.19, f32[1,1024]{1,0:T(1,128)S(1)} %divide_sqrt_fusion.scale_ref, ...), custom_call_target="tpu_custom_call" | custom-call | flops 10000000000 | bytes 10000000 | tf_op jit(solution)/shard_map/pallas_call | solution.py:953
  455.7 14.5 %collective-permute-done.56 = bf16[96,2560]{1,0:T(8,128)(2,1)S(1)} collective-permute-done((bf16[96,2560]{1,0:T(8,128)(2,1)S(1)}, bf16[96,2560]{1,0:T(8,128)(2,1)S(1)}, u32[]{:S(2)}, u32[]{:S(2)}) %collective-permute-start.56) | collective-permute-done | bytes 491552 | tf_op jit(solution)/shard_map/ppermute | solution.py:281
  476.1 6.8 %collective-permute-done.65 = bf16[96,3072]{1,0:T(8,128)(2,1)S(1)} collective-permute-done((bf16[96,3072]{1,0:T(8,128)(2,1)S(1)}, bf16[96,3072]{1,0:T(8,128)(2,1)S(1)}, u32[]{:S(2)}, u32[]{:S(2)}) %collective-permute-start.65) | collective-permute-done | bytes 589856 | tf_op jit(solution)/shard_map/ppermute | solution.py:281
  485.2 8.3 %collective-permute-done.57 = bf16[96,2560]{1,0:T(8,128)(2,1)S(1)} collective-permute-done((bf16[96,2560]{1,0:T(8,128)(2,1)S(1)}, bf16[96,2560]{1,0:T(8,128)(2,1)S(1)}, u32[]{:S(2)}, u32[]{:S(2)}) %collective-permute-start.57) | collective-permute-done | bytes 491552 | tf_op jit(solution)/shard_map/ppermute | solution.py:281
  493.7 11.2 %collective-permute-done.74 = bf16[48,3072]{1,0:T(8,128)(2,1)S(1)} collective-permute-done((bf16[48,3072]{1,0:T(8,128)(2,1)S(1)}, bf16[48,3072]{1,0:T(8,128)(2,1)S(1)}, u32[]{:S(2)}, u32[]{:S(2)}) %collective-permute-start.74) | collective-permute-done | bytes 294944 | tf_op jit(solution)/shard_map/ppermute | solution.py:281
  510.0 3.5 collective-permute-done.70
  521.0 9.2 %collective-permute-done.67 = bf16[256,1024]{1,0:T(8,128)(2,1)S(1)} collective-permute-done((bf16[256,1024]{1,0:T(8,128)(2,1)S(1)}, bf16[256,1024]{1,0:T(8,128)(2,1)S(1)}, u32[]{:S(2)}, u32[]{:S(2)}) %collective-permute-start.67) | collective-permute-done | bytes 524320 | tf_op jit(solution)/shard_map/ppermute | solution.py:281
  530.4 5.1 collective-permute-done.52
  536.2 5.2 collective-permute-done.59
  541.7 11.0 %collective-permute-done.68 = bf16[256,1024]{1,0:T(8,128)(2,1)S(1)} collective-permute-done((bf16[256,1024]{1,0:T(8,128)(2,1)S(1)}, bf16[256,1024]{1,0:T(8,128)(2,1)S(1)}, u32[]{:S(2)}, u32[]{:S(2)}) %collective-permute-start.68) | collective-permute-done | bytes 524320 | tf_op jit(solution)/shard_map/ppermute | solution.py:281
  557.2 3.6 collective-permute-done.79
  560.9 5.3 collective-permute-done.72
  570.3 25.4 %collective-permute-done.76 = bf16[128,1024]{1,0:T(8,128)(2,1)S(1)} collective-permute-done((bf16[128,1024]{1,0:T(8,128)(2,1)S(1)}, bf16[128,1024]{1,0:T(8,128)(2,1)S(1)}, u32[]{:S(2)}, u32[]{:S(2)}) %collective-permute-start.76) | collective-permute-done | bytes 262176 | tf_op jit(solution)/shard_map/ppermute | solution.py:281
  605.9 4.3 collective-permute-done.80
  611.3 4.5 collective-permute-done.81
  621.7 11.2 %collective-permute-done.82 = bf16[128,2048]{1,0:T(8,128)(2,1)} collective-permute-done((bf16[128,2048]{1,0:T(8,128)(2,1)}, bf16[128,2048]{1,0:T(8,128)(2,1)}, u32[]{:S(2)}, u32[]{:S(2)}) %collective-permute-start.82) | collective-permute-done | bytes 524320 | tf_op jit(solution)/shard_map/ppermute | solution.py:281
  638.8 7.4 %collective-permute-done.83 = bf16[128,2048]{1,0:T(8,128)(2,1)} collective-permute-done((bf16[128,2048]{1,0:T(8,128)(2,1)}, bf16[128,2048]{1,0:T(8,128)(2,1)}, u32[]{:S(2)}, u32[]{:S(2)}) %collective-permute-start.83) | collective-permute-done | bytes 524320 | tf_op jit(solution)/shard_map/ppermute | solution.py:281
  (880 shorter events, 315.0 us)
Async XLA Ops:
  31.8 50.4 %collective-permute-start.15 = (bf16[256,1024]{1,0:T(8,128)(2,1)S(1)}, bf16[256,1024]{1,0:T(8,128)(2,1)S(1)}, u32[]{:S(2)}, u32[]{:S(2)}) collective-permute-start(bf16[256,1024]{1,0:T(8,128)(2,1)S(1)} %pad_maximum_fusion.22), channel_id=1, source_target_pairs={{0,4},{2,6},{4,0},{6,2},{8,12},{10,14},{12,8},{14,10},{16,20},{18,... | collective-permute-start | bytes 1572872 | tf_op jit(solution)/shard_map/ppermute | solution.py:281
  33.4 45.5 %collective-permute-start.13 = (bf16[256,1024]{1,0:T(8,128)(2,1)S(1)}, bf16[256,1024]{1,0:T(8,128)(2,1)S(1)}, u32[]{:S(2)}, u32[]{:S(2)}) collective-permute-start(bf16[256,1024]{1,0:T(8,128)(2,1)S(1)} %pad_maximum_fusion.21), channel_id=1, source_target_pairs={{0,2},{2,0},{4,6},{6,4},{8,10},{10,8},{12,14},{14,12},{16,18},{18,... | collective-permute-start | bytes 1572872 | tf_op jit(solution)/shard_map/ppermute | solution.py:281
  42.2 38.2 %collective-permute-start.6 = (bf16[256,1024]{1,0:T(8,128)(2,1)S(1)}, bf16[256,1024]{1,0:T(8,128)(2,1)}, u32[]{:S(2)}, u32[]{:S(2)}) collective-permute-start(bf16[256,1024]{1,0:T(8,128)(2,1)S(1)} %collective-permute-done.5), channel_id=1, source_target_pairs={{0,8},{2,10},{4,12},{6,14},{8,16},{10,18},{12,20},{14,22},{16,24},... | collective-permute-start | bytes 1572872 | tf_op jit(solution)/shard_map/ppermute | solution.py:281
  43.3 54.4 %collective-permute-start.9 = (bf16[512,1024]{1,0:T(8,128)(2,1)}, bf16[512,1024]{1,0:T(8,128)(2,1)}, u32[]{:S(2)}, u32[]{:S(2)}) collective-permute-start(bf16[512,1024]{1,0:T(8,128)(2,1)} %pad_maximum_fusion.8), channel_id=1, source_target_pairs={{0,4},{2,6},{4,0},{6,2},{8,12},{10,14},{12,8},{14,10},{16,20},{18,... | collective-permute-start | bytes 3145736 | tf_op jit(solution)/shard_map/ppermute | solution.py:281
  53.4 32.5 %collective-permute-start.11 = (bf16[256,1024]{1,0:T(8,128)(2,1)S(1)}, bf16[256,1024]{1,0:T(8,128)(2,1)S(1)}, u32[]{:S(2)}, u32[]{:S(2)}) collective-permute-start(bf16[256,1024]{1,0:T(8,128)(2,1)S(1)} %collective-permute-done.2), channel_id=1, source_target_pairs={{0,8},{2,10},{4,12},{6,14},{8,16},{10,18},{12,20},{14,22},{16,24},... | collective-permute-start | bytes 1572872 | tf_op jit(solution)/shard_map/ppermute | solution.py:281
  83.3 31.1 %collective-permute-start.17 = (bf16[512,1024]{1,0:T(8,128)(2,1)}, bf16[512,1024]{1,0:T(8,128)(2,1)}, u32[]{:S(2)}, u32[]{:S(2)}) collective-permute-start(bf16[512,1024]{1,0:T(8,128)(2,1)} %pad_maximum_fusion.10), channel_id=1, source_target_pairs={{0,2},{2,0},{4,6},{6,4},{8,10},{10,8},{12,14},{14,12},{16,18},{18,... | collective-permute-start | bytes 3145736 | tf_op jit(solution)/shard_map/ppermute | solution.py:281
  85.9 54.5 %collective-permute-start.23 = (bf16[512,1024]{1,0:T(8,128)(2,1)}, bf16[512,1024]{1,0:T(8,128)(2,1)}, u32[]{:S(2)}, u32[]{:S(2)}) collective-permute-start(bf16[512,1024]{1,0:T(8,128)(2,1)} %pad_maximum_fusion.11), channel_id=1, source_target_pairs={{0,4},{2,6},{4,0},{6,2},{8,12},{10,14},{12,8},{14,10},{16,20},{18,... | collective-permute-start | bytes 3145736 | tf_op jit(solution)/shard_map/ppermute | solution.py:281
  86.0 45.2 %collective-permute-start.14 = (bf16[512,1024]{1,0:T(8,128)(2,1)}, bf16[512,1024]{1,0:T(8,128)(2,1)}, u32[]{:S(2)}, u32[]{:S(2)}) collective-permute-start(bf16[512,1024]{1,0:T(8,128)(2,1)} %pad_maximum_fusion.9), channel_id=1, source_target_pairs={{0,2},{2,0},{4,6},{6,4},{8,10},{10,8},{12,14},{14,12},{16,18},{18,... | collective-permute-start | bytes 3145736 | tf_op jit(solution)/shard_map/ppermute | solution.py:281
  97.7 36.7 %collective-permute-start.20 = (bf16[128,2048]{1,0:T(8,128)(2,1)}, bf16[128,2048]{1,0:T(8,128)(2,1)S(1)}, u32[]{:S(2)}, u32[]{:S(2)}) collective-permute-start(bf16[128,2048]{1,0:T(8,128)(2,1)} %collective-permute-done.1), channel_id=1, source_target_pairs={{0,8},{2,10},{4,12},{6,14},{8,16},{10,18},{12,20},{14,22},{16,24},... | collective-permute-start | bytes 1572872 | tf_op jit(solution)/shard_map/ppermute | solution.py:281
  113.5 38.3 %collective-permute-start.10 = (bf16[512,1024]{1,0:T(8,128)(2,1)S(1)}, bf16[512,1024]{1,0:T(8,128)(2,1)S(1)}, u32[]{:S(2)}, u32[]{:S(2)}) collective-permute-start(bf16[512,1024]{1,0:T(8,128)(2,1)S(1)} %constant_dynamic-update-slice_fusion), channel_id=1, source_target_pairs={{0,4},{2,6},{4,0},{6,2},{8,12},{10,14},{12,8},{14,10},{16,20},{18,... | collective-permute-start | bytes 3145736 | tf_op jit(solution)/shard_map/ppermute | solution.py:281
  131.2 32.3 %collective-permute-start.18 = (bf16[512,1024]{1,0:T(8,128)(2,1)S(1)}, bf16[512,1024]{1,0:T(8,128)(2,1)S(1)}, u32[]{:S(2)}, u32[]{:S(2)}) collective-permute-start(bf16[512,1024]{1,0:T(8,128)(2,1)S(1)} %constant_dynamic-update-slice_fusion.2), channel_id=1, source_target_pairs={{0,2},{2,0},{4,6},{6,4},{8,10},{10,8},{12,14},{14,12},{16,18},{18,... | collective-permute-start | bytes 3145736 | tf_op jit(solution)/shard_map/ppermute | solution.py:281
  140.4 38.0 %collective-permute-start.25 = (bf16[192,2560]{1,0:T(8,128)(2,1)S(1)}, bf16[192,2560]{1,0:T(8,128)(2,1)S(1)}, u32[]{:S(2)}, u32[]{:S(2)}) collective-permute-start(bf16[192,2560]{1,0:T(8,128)(2,1)S(1)} %pad_maximum_fusion.15.refs_0_), channel_id=1, source_target_pairs={{0,4},{2,6},{4,0},{6,2},{8,12},{10,14},{12,8},{14,10},{16,20},{18,... | collective-permute-start | bytes 2949128 | tf_op jit(solution)/shard_map/ppermute | solution.py:281
  179.4 62.4 %collective-permute-start.37 = (bf16[192,3072]{1,0:T(8,128)(2,1)S(1)}, bf16[192,3072]{1,0:T(8,128)(2,1)}, u32[]{:S(2)}, u32[]{:S(2)}) collective-permute-start(bf16[192,3072]{1,0:T(8,128)(2,1)S(1)} %pad_maximum_fusion.7.refs_0_), channel_id=1, source_target_pairs={{0,2},{2,0},{4,6},{6,4},{8,10},{10,8},{12,14},{14,12},{16,18},{18,... | collective-permute-start | bytes 3538952 | tf_op jit(solution)/shard_map/ppermute | solution.py:281
  184.9 45.3 %collective-permute-start.26 = (bf16[512,1024]{1,0:T(8,128)(2,1)}, bf16[512,1024]{1,0:T(8,128)(2,1)}, u32[]{:S(2)}, u32[]{:S(2)}) collective-permute-start(bf16[512,1024]{1,0:T(8,128)(2,1)} %pad_maximum_fusion.12), channel_id=1, source_target_pairs={{0,4},{2,6},{4,0},{6,2},{8,12},{10,14},{12,8},{14,10},{16,20},{18,... | collective-permute-start | bytes 3145736 | tf_op jit(solution)/shard_map/ppermute | solution.py:281
  187.5 41.0 %collective-permute-start.31 = (bf16[192,2560]{1,0:T(8,128)(2,1)}, bf16[192,2560]{1,0:T(8,128)(2,1)}, u32[]{:S(2)}, u32[]{:S(2)}) collective-permute-start(bf16[192,2560]{1,0:T(8,128)(2,1)} %constant_dynamic-update-slice_fusion.4.refs_1_), channel_id=1, source_target_pairs={{0,4},{2,6},{4,0},{6,2},{8,12},{10,14},{12,8},{14,10},{16,20},{18,... | collective-permute-start | bytes 2949128 | tf_op jit(solution)/shard_map/ppermute | solution.py:281
  199.5 41.4 %collective-permute-start.36 = (bf16[96,3072]{1,0:T(8,128)(2,1)}, bf16[96,3072]{1,0:T(8,128)(2,1)S(1)}, u32[]{:S(2)}, u32[]{:S(2)}) collective-permute-start(bf16[96,3072]{1,0:T(8,128)(2,1)} %collective-permute-done.35), channel_id=1, source_target_pairs={{0,8},{2,10},{4,12},{6,14},{8,16},{10,18},{12,20},{14,22},{16,24},... | collective-permute-start | bytes 1769480 | tf_op jit(solution)/shard_map/ppermute | solution.py:281
  241.8 28.5 %collective-permute-start.38 = (bf16[192,3072]{1,0:T(8,128)(2,1)}, bf16[192,3072]{1,0:T(8,128)(2,1)}, u32[]{:S(2)}, u32[]{:S(2)}) collective-permute-start(bf16[192,3072]{1,0:T(8,128)(2,1)} %constant_dynamic-update-slice_fusion.6.refs_1_), channel_id=1, source_target_pairs={{0,2},{2,0},{4,6},{6,4},{8,10},{10,8},{12,14},{14,12},{16,18},{18,... | collective-permute-start | bytes 3538952 | tf_op jit(solution)/shard_map/ppermute | solution.py:281
  305.7 57.8 %collective-permute-start.45 = (bf16[192,3072]{1,0:T(8,128)(2,1)}, bf16[192,3072]{1,0:T(8,128)(2,1)}, u32[]{:S(2)}, u32[]{:S(2)}) collective-permute-start(bf16[192,3072]{1,0:T(8,128)(2,1)} %get-tuple-element.147), channel_id=1, source_target_pairs={{0,2},{2,0},{4,6},{6,4},{8,10},{10,8},{12,14},{14,12},{16,18},{18,... | collective-permute-start | bytes 3538952 | tf_op jit(solution)/shard_map/ppermute | solution.py:281
  306.5 59.8 %collective-permute-start.62 = (bf16[192,3072]{1,0:T(8,128)(2,1)}, bf16[192,3072]{1,0:T(8,128)(2,1)}, u32[]{:S(2)}, u32[]{:S(2)}) collective-permute-start(bf16[192,3072]{1,0:T(8,128)(2,1)} %get-tuple-element.168), channel_id=1, source_target_pairs={{0,2},{2,0},{4,6},{6,4},{8,10},{10,8},{12,14},{14,12},{16,18},{18,... | collective-permute-start | bytes 3538952 | tf_op jit(solution)/shard_map/ppermute | solution.py:281
  355.7 43.6 %collective-permute-start.49 = (bf16[192,2560]{1,0:T(8,128)(2,1)}, bf16[192,2560]{1,0:T(8,128)(2,1)}, u32[]{:S(2)}, u32[]{:S(2)}) collective-permute-start(bf16[192,2560]{1,0:T(8,128)(2,1)} %get-tuple-element.153), channel_id=1, source_target_pairs={{0,4},{2,6},{4,0},{6,2},{8,12},{10,14},{12,8},{14,10},{16,20},{18,... | collective-permute-start | bytes 2949128 | tf_op jit(solution)/shard_map/ppermute | solution.py:281
  356.6 44.6 %collective-permute-start.53 = (bf16[192,2560]{1,0:T(8,128)(2,1)}, bf16[192,2560]{1,0:T(8,128)(2,1)}, u32[]{:S(2)}, u32[]{:S(2)}) collective-permute-start(bf16[192,2560]{1,0:T(8,128)(2,1)} %get-tuple-element.157), channel_id=1, source_target_pairs={{0,4},{2,6},{4,0},{6,2},{8,12},{10,14},{12,8},{14,10},{16,20},{18,... | collective-permute-start | bytes 2949128 | tf_op jit(solution)/shard_map/ppermute | solution.py:281
  366.2 29.3 %collective-permute-start.63 = (bf16[96,3072]{1,0:T(8,128)(2,1)}, bf16[96,3072]{1,0:T(8,128)(2,1)}, u32[]{:S(2)}, u32[]{:S(2)}) collective-permute-start(bf16[96,3072]{1,0:T(8,128)(2,1)} %slice.415), channel_id=1, source_target_pairs={{0,8},{2,10},{4,12},{6,14},{8,16},{10,18},{12,20},{14,22},{16,24},... | collective-permute-start | bytes 1769480 | tf_op jit(solution)/shard_map/ppermute | solution.py:281
  366.2 83.1 %collective-permute-start.46 = (bf16[512,1024]{1,0:T(8,128)(2,1)}, bf16[512,1024]{1,0:T(8,128)(2,1)}, u32[]{:S(2)}, u32[]{:S(2)}) collective-permute-start(bf16[512,1024]{1,0:T(8,128)(2,1)} %convolution_convert_fusion.18), channel_id=1, source_target_pairs={{0,2},{2,0},{4,6},{6,4},{8,10},{10,8},{12,14},{14,12},{16,18},{18,... | collective-permute-start | bytes 3145736 | tf_op jit(solution)/shard_map/ppermute | solution.py:281
  397.6 56.6 %collective-permute-start.64 = (bf16[96,3072]{1,0:T(8,128)(2,1)}, bf16[96,3072]{1,0:T(8,128)(2,1)}, u32[]{:S(2)}, u32[]{:S(2)}) collective-permute-start(bf16[96,3072]{1,0:T(8,128)(2,1)} %add_convert_fusion.16), channel_id=1, source_target_pairs={{0,8},{2,10},{4,12},{6,14},{8,16},{10,18},{12,20},{14,22},{16,24},... | collective-permute-start | bytes 1769480 | tf_op jit(solution)/shard_map/ppermute | solution.py:281
  403.5 47.9 %collective-permute-start.55 = (bf16[96,2560]{1,0:T(8,128)(2,1)}, bf16[96,2560]{1,0:T(8,128)(2,1)}, u32[]{:S(2)}, u32[]{:S(2)}) collective-permute-start(bf16[96,2560]{1,0:T(8,128)(2,1)} %slice.409), channel_id=1, source_target_pairs={{0,8},{2,10},{4,12},{6,14},{8,16},{10,18},{12,20},{14,22},{16,24},... | collective-permute-start | bytes 1474568 | tf_op jit(solution)/shard_map/ppermute | solution.py:281
  403.5 67.0 %collective-permute-start.54 = (bf16[512,1024]{1,0:T(8,128)(2,1)}, bf16[512,1024]{1,0:T(8,128)(2,1)}, u32[]{:S(2)}, u32[]{:S(2)}) collective-permute-start(bf16[512,1024]{1,0:T(8,128)(2,1)} %convolution_convert_fusion.13), channel_id=1, source_target_pairs={{0,4},{2,6},{4,0},{6,2},{8,12},{10,14},{12,8},{14,10},{16,20},{18,... | collective-permute-start | bytes 3145736 | tf_op jit(solution)/shard_map/ppermute | solution.py:281
  451.3 54.4 %collective-permute-start.47 = (bf16[512,1024]{1,0:T(8,128)(2,1)S(1)}, bf16[512,1024]{1,0:T(8,128)(2,1)S(1)}, u32[]{:S(2)}, u32[]{:S(2)}) collective-permute-start(bf16[512,1024]{1,0:T(8,128)(2,1)S(1)} %copy-done.132), channel_id=1, source_target_pairs={{0,2},{2,0},{4,6},{6,4},{8,10},{10,8},{12,14},{14,12},{16,18},{18,... | collective-permute-start | bytes 3145736 | tf_op jit(solution)/shard_map/ppermute | solution.py:281
  474.1 45.4 %collective-permute-start.51 = (bf16[512,1024]{1,0:T(8,128)(2,1)S(1)}, bf16[512,1024]{1,0:T(8,128)(2,1)S(1)}, u32[]{:S(2)}, u32[]{:S(2)}) collective-permute-start(bf16[512,1024]{1,0:T(8,128)(2,1)S(1)} %copy-done.134), channel_id=1, source_target_pairs={{0,4},{2,6},{4,0},{6,2},{8,12},{10,14},{12,8},{14,10},{16,20},{18,... | collective-permute-start | bytes 3145736 | tf_op jit(solution)/shard_map/ppermute | solution.py:281
  505.8 29.9 %collective-permute-start.75 = (bf16[512,1024]{1,0:T(8,128)(2,1)S(1)}, bf16[512,1024]{1,0:T(8,128)(2,1)S(1)}, u32[]{:S(2)}, u32[]{:S(2)}) collective-permute-start(bf16[512,1024]{1,0:T(8,128)(2,1)S(1)} %copy-done.133), channel_id=1, source_target_pairs={{0,4},{2,6},{4,0},{6,2},{8,12},{10,14},{12,8},{14,10},{16,20},{18,... | collective-permute-start | bytes 3145736 | tf_op jit(solution)/shard_map/ppermute | solution.py:281
  517.4 35.7 %collective-permute-start.71 = (bf16[512,1024]{1,0:T(8,128)(2,1)S(1)}, bf16[512,1024]{1,0:T(8,128)(2,1)S(1)}, u32[]{:S(2)}, u32[]{:S(2)}) collective-permute-start(bf16[512,1024]{1,0:T(8,128)(2,1)S(1)} %copy-done.131), channel_id=1, source_target_pairs={{0,2},{2,0},{4,6},{6,4},{8,10},{10,8},{12,14},{14,12},{16,18},{18,... | collective-permute-start | bytes 3145736 | tf_op jit(solution)/shard_map/ppermute | solution.py:281
  566.3 34.3 %collective-permute-start.78 = (bf16[512,1024]{1,0:T(8,128)(2,1)S(1)}, bf16[512,1024]{1,0:T(8,128)(2,1)S(1)}, u32[]{:S(2)}, u32[]{:S(2)}) collective-permute-start(bf16[512,1024]{1,0:T(8,128)(2,1)S(1)} %copy-done.130), channel_id=1, source_target_pairs={{0,2},{2,0},{4,6},{6,4},{8,10},{10,8},{12,14},{14,12},{16,18},{18,... | collective-permute-start | bytes 3145736 | tf_op jit(solution)/shard_map/ppermute | solution.py:281
  569.0 28.6 %collective-permute-start.61 = (bf16[144,1024]{1,0:T(8,128)(2,1)S(1)}, bf16[144,1024]{1,0:T(8,128)(2,1)S(1)}, u32[]{:S(2)}, u32[]{:S(2)}) collective-permute-start(bf16[144,1024]{1,0:T(8,128)(2,1)S(1)} %add_convert_fusion.26), channel_id=1, source_target_pairs={{0,8},{2,10},{4,12},{6,14},{8,0},{10,2},{12,4},{14,6},{16,24},{18,... | collective-permute-start | bytes 884744 | tf_op jit(solution)/shard_map/ppermute | solution.py:281
  (258 other events, 3325.7 us)

commit v3 on v2

--- a/solution.py
+++ b/solution.py
@@ -1,4 +1,5 @@
-from functools import partial, reduce
+import math
+from functools import partial
 
 import jax
 import jax.numpy as jnp
@@ -46,11 +47,6 @@
     return (values - center) * lax.rsqrt(spread + EPSILON) * gain_row + bias_row
 
 
-def highway_mix(mixed_pre, carried):
-    gate_value = jax.nn.sigmoid(mixed_pre[:, 1])
-    return gate_value * carried + (1.0 - gate_value) * gelu_exact(mixed_pre[:, 0])
-
-
 def word_order(lengths):
     words = lengths.shape[0]
     sequences = words // LENGTH
@@ -152,15 +148,16 @@
 
 def pool_back_kernel(
     tile_ref, ids_ref, lanes_ref, filters_ref, scale_ref, lens_ref, widths_ref, embed_ref, shift_ref,
-    grad_ref, filter_grad_ref, char_grad_ref, conv_grad_ref, column_ref, count_ref,
+    grad_ref, filter_before_ref, char_before_ref, filter_grad_ref, char_grad_ref, conv_grad_ref,
+    column_ref, count_ref,
 ):
     channels = filters_ref.shape[1]
     chunks_all = SLOTS // CHUNK
     tap_lanes = [lanes_ref[tap : tap + 1, :].astype(jnp.bfloat16) for tap in range(TAPS)]
     lane_taps = lax.broadcasted_iota(jnp.int32, (1, 1, LANES), 2) // CHAR_DIM
     blocks = [slice(first, first + BLOCK) for first in range(0, channels, BLOCK)]
-    filter_grad_ref[...] = jnp.zeros(filter_grad_ref.shape, jnp.float32)
-    char_grad_ref[...] = jnp.zeros(char_grad_ref.shape, jnp.float32)
+    filter_grad_ref[...] = filter_before_ref[...]
+    char_grad_ref[...] = char_before_ref[...]
     column_ref[:CHUNK] = jnp.zeros((CHUNK, TILE, LANES), jnp.float32)
 
     def one_tile(tile, _):
@@ -245,13 +242,13 @@
         ],
         compiler_params=params,
         cost_estimate=pl.CostEstimate(
-            flops=5_000_000_000, bytes_accessed=8_000_000, transcendentals=5_000_000
+            flops=2_000_000_000, bytes_accessed=8_000_000, transcendentals=5_000_000
         ),
     )
     back = pl.pallas_call(
         pool_back_kernel,
         out_shape=[shape((LANES, channels)), shape((IDS, 2 * LANES))],
-        in_specs=[smem] + [vmem] * 9,
+        in_specs=[smem] + [vmem] * 11,
         out_specs=[vmem] * 2,
         scratch_shapes=[
             pltpu.VMEM((CHUNK * TILE, channels), jnp.bfloat16),
@@ -260,7 +257,7 @@
         ],
         compiler_params=params,
         cost_estimate=pl.CostEstimate(
-            flops=10_000_000_000, bytes_accessed=10_000_000, transcendentals=5_000_000
+            flops=4_000_000_000, bytes_accessed=10_000_000, transcendentals=5_000_000
         ),
     )
     return pool, back
@@ -295,17 +292,24 @@
 
 FIRST = {"a": "x", "b": "y"}
 LAST = {"a": "y", "b": "x"}
+TURNS = (1, 2, 3)
+SMALL_MOVES = {
+    ("small", "x"): ("x", 1, []),
+    ("small", "y"): ("y", 1, [("small", "x")]),
+    ("small", "near"): ("z", 1, [("small", "y")]),
+    ("small", "far"): ("z", 2, [("small", "near")]),
+}
 
 
 def moves_of(kind):
     moves = {}
     if kind == "Q":
-        for turn in (1, 2, 3):
+        for turn in TURNS:
             moves["z", turn] = ("z", 2, [("z", turn - 1)] if turn > 1 else [])
     for part in "ab":
         if kind == "P":
             moves[part, "first"] = (FIRST[part], 1, [])
-            for turn in (1, 2, 3):
+            for turn in TURNS:
                 before = (part, "z", turn - 1) if turn > 1 else (part, "first")
                 moves[part, "z", turn] = ("z", 2, [before])
             for half in (0, 1):
@@ -337,34 +341,70 @@
     return moves
 
 
-def ordered_moves(moves, ready, lag=0.5):
-    ended, free, order = {}, {"x": 0.0, "y": 0.0, "z": 0.0}, []
-    ranks = {name: rank for rank, name in enumerate(moves)}
-    waiting = dict(moves)
-    while waiting:
-        best = None
-        for name, (axis, size, needs) in waiting.items():
-            if all(need in ended for need in needs):
-                start = max([ready.get(name[0], 0.0), free[axis]] + [ended[need] + lag for need in needs])
-                if best is None or (start, ranks[name]) < best[:2]:
-                    best = (start, ranks[name], name)
-        start, _, name = best
-        axis, size, _ = waiting.pop(name)
-        ended[name] = free[axis] = start + size
-        order.append(name)
-    return order
-
-
-class Links:
-    def __init__(self):
-        self.sent = {"x": [], "y": [], "z": []}
-
-    def send(self, value, axis, way=None):
+class Schedule:
+    def __init__(self, kinds, moves_of_kind, ready, extra, ranks, lag=0.7):
+        moves = dict(extra)
+        for name, kind in kinds.items():
+            for move, (axis, load, needs) in moves_of_kind(kind).items():
+                moves[(name,) + move] = (axis, load, [(name,) + need for need in needs])
+        self.moves, self.got, self.sent = moves, {}, {"x": [], "y": [], "z": []}
+        self.values = {}
+        users = {move: [] for move in moves}
+        for move, (_, _, needs) in moves.items():
+            for need in needs:
+                users[need].append(move)
+        tails = {}
+
+        def tail(move):
+            if move not in tails:
+                tails[move] = moves[move][1] + lag + max(map(tail, users[move]), default=0.0)
+            return tails[move]
+
+        places = {move: place for place, move in enumerate(moves)}
+        free, waiting = {"x": 0.0, "y": 0.0, "z": 0.0}, dict(moves)
+        self.starts, self.ends = {}, {}
+        while waiting:
+            best = None
+            for move, (axis, load, needs) in waiting.items():
+                if all(need in self.ends for need in needs):
+                    start = max(
+                        [ready.get(move[:2], ready.get(move[0], 0.0)), free[axis]]
+                        + [self.ends[need] + lag for need in needs]
+                    )
+                    rank = ranks.get(move[:2], ranks.get(move[0], 0))
+                    key = (start, rank - tail(move), places[move])
+                    if best is None or key < best[0]:
+                        best = (key, start, move)
+            _, start, move = best
+            axis, load, _ = waiting.pop(move)
+            self.starts[move] = start
+            self.ends[move] = free[axis] = start + load
+        self.order = list(self.starts)
+
+    def after(self, value, time):
+        known = []
+        for axis in "xyz":
+            for times, arrays in ((self.ends, self.got), (self.starts, self.values)):
+                past = [m for m in arrays if self.moves[m][0] == axis and times[m] <= time]
+                if past:
+                    known.append(arrays[max(past, key=times.get)])
+        return lax.optimization_barrier((value, *known))[0] if known else value
+
+    def after_all(self, value, *names):
+        return self.after(
+            value, max(end for move, end in self.ends.items() if move[: len(names)] == names)
+        )
+
+    def send(self, move, value, way):
+        axis = self.moves[move][0]
         sent = self.sent[axis]
         if len(sent) > 1:
-            value, _ = lax.optimization_barrier((value, sent[-2]))
-        sent.append(step(value, way or axis))
-        return sent[-1]
+            value = lax.optimization_barrier((value, sent[-2]))[0]
+        value = self.after(value, self.starts[move] - SLACK)
+        self.values[move] = value
+        self.got[move] = step(value, way)
+        sent.append(self.got[move])
+        return self.got[move]
 
 
 def blocks_of(kind, part):
@@ -389,133 +429,122 @@
 
 
 def gather_matrices(shards, kinds):
-    moves = {}
-    for name, kind in kinds.items():
-        for move, (axis, size, needs) in moves_of(kind).items():
-            moves[(name,) + move] = (axis, size, [(name,) + need for need in needs])
-    links, got, sent = Links(), {}, {}
-    for move in ordered_moves(moves, {}):
+    plan = Schedule(kinds, moves_of, {}, {}, GATHER_RANKS)
+    got, sent = plan.got, {}
+    for move in plan.order:
         name, kind = move[0], kinds[move[0]]
         parts = dict(zip("ab", shards[name]))
-        if kind == "P":
+        way = plan.moves[move][0]
+        if "z" in move:
+            turn = move[-1]
+            if turn > 1:
+                value = got[move[:-1] + (turn - 1,)]
+            elif kind == "P":
+                part = move[1]
+                value = joined([parts[part], got[name, part, "first"]])
+                sent[name, part, "pair"] = value
+            else:
+                value = joined_lanes(shards[name])
+        else:
             part, stage = move[1:3]
-            if stage == "first":
+            turns = (2 * move[3], 2 * move[3] + 1) if len(move) == 4 else ()
+            if kind == "P" and stage == "first":
                 value = parts[part]
-            elif stage == "z":
-                if move[3] == 1:
-                    sent[name, part, "pair"] = joined([parts[part], got[name, part, "first"]])
-                    value = sent[name, part, "pair"]
-                else:
-                    value = got[name, part, "z", move[3] - 1]
-            else:
-                pairs = [sent[name, part, "pair"]] + [got[name, part, "z", turn] for turn in (1, 2, 3) if turn <= 1 + 2 * move[3]]
-                value = joined(pairs[2 * move[3] :])
-        elif move[1] == "z":
-            value = joined_lanes(shards[name]) if move[2] == 1 else got[name, "z", move[2] - 1]
-        else:
-            part, stage, half = move[1:]
-            if stage == "first":
+            elif kind == "P":
+                value = joined(
+                    [got[name, part, "z", turn] if turn else sent[name, part, "pair"] for turn in turns]
+                )
+            elif stage == "first":
                 width = parts["a"].shape[1]
                 lanes = slice(0, width) if part == "a" else slice(width, None)
-                rows = [
-                    got[name, "z", turn][:, lanes] if turn else parts[part]
-                    for turn in (2 * half, 2 * half + 1)
-                ]
-                value = joined(rows)
+                value = joined(
+                    [got[name, "z", turn][:, lanes] if turn else parts[part] for turn in turns]
+                )
             else:
-                value = joined([sent[name, part, "first", half], got[name, part, "first", half]])
+                value = joined([sent[name, part, "first", move[3]], got[name, part, "first", move[3]]])
         sent[move] = value
-        got[move] = links.send(value, moves[move][0])
+        plan.send(move, value, way)
     full = {
         (name, part): [held[name, part, "last", half] for held in (sent, got) for half in (0, 1)]
         for name in kinds
         for part in "ab"
     }
-    return full, got
+    return full, plan
 
 
 def joined_lanes(pieces):
     return jnp.concatenate(pieces, axis=1)
 
 
-SMALL_MOVES = {
-    ("small", "x"): ("x", 1, []),
-    ("small", "y"): ("y", 1, [("small", "x")]),
-    ("small", "near"): ("z", 1, [("small", "y")]),
-    ("small", "far"): ("z", 2, [("small", "near")]),
-}
-
-
-def scatter_matrices(grads, kinds, small, ready):
-    low = jnp.bfloat16
-    moves = {}
-    for name, kind in kinds.items():
-        for move, (axis, size, needs) in back_moves_of(kind).items():
-            moves[(name,) + move] = (axis, size, [(name,) + need for need in needs])
-    moves = {**SMALL_MOVES, **moves}
-    links, got, held = Links(), {}, {}
-
-    def kept(name, part, half):
+class Scatter:
+    def __init__(self, kinds, ready):
+        self.kinds, self.terms, self.held, self.small = kinds, {}, {}, None
+        self.plan = Schedule(kinds, back_moves_of, ready, SMALL_MOVES, SCATTER_RANKS)
+        self.left = list(self.plan.order)
+
+    def kept(self, name, part, half):
         key = (name, part, half)
-        if key not in held:
-            held[key] = add(grads[name, part][half], got[name, part, "last", half]).astype(low)
-        return held[key]
-
-    def pair(name, part, turn):
-        rows = kept(name, part, turn // 2)
+        if key not in self.held:
+            got = self.plan.got[name, part, "last", half]
+            self.held[key] = add(self.terms[name, part][half], got).astype(jnp.bfloat16)
+        return self.held[key]
+
+    def pair(self, name, part, turn):
+        rows = self.kept(name, part, turn // 2)
         height = rows.shape[0] // 2
         return rows[(turn % 2) * height :][:height]
 
-    def both(name, turn):
-        rows = []
-        for part in "ab":
-            half = turn // 2
-            key = (name, part, "both", half)
-            if key not in held:
-                own = kept(name, part, half)
-                held[key] = add(own[: own.shape[0] // 2], got[name, part, "first", half])
-            height = held[key].shape[0] // 2
-            rows.append(held[key][(turn % 2) * height :][:height])
-        return joined_lanes(rows)
-
-    for move in ordered_moves(moves, ready):
-        if move in SMALL_MOVES:
-            small = small.astype(low)
-            small = add(small, links.send(small, moves[move][0], move[1]))
-            continue
-        name, kind = move[0], kinds[move[0]]
-        if "last" in move:
-            value = grads[name, move[1]][2 + move[3]]
-        elif kind == "P" and move[2] == "z":
-            part, turn = move[1], move[3]
-            value = pair(name, part, turn)
-            if turn > 1:
-                value = add(value, got[name, part, "z", turn - 1]).astype(low)
-        elif kind == "P":
-            part = move[1]
-            total = add(pair(name, part, 0), got[name, part, "z", 3])
-            held[name, part, "own"] = total[: total.shape[0] // 2]
-            value = total[total.shape[0] // 2 :].astype(low)
-        elif move[1] == "z":
-            turn = move[2]
-            value = both(name, turn)
-            if turn > 1:
-                value = add(value, got[name, "z", turn - 1])
-            value = value.astype(low)
-        else:
-            part, half = move[1], move[3]
-            own = kept(name, part, half)
-            value = own[own.shape[0] // 2 :]
-        got[move] = links.send(value, moves[move][0])
-    sums = {}
-    for name, kind in kinds.items():
-        if kind == "P":
-            sums[name] = joined_lanes(
-                [add(held[name, part, "own"], got[name, part, "first"]) for part in "ab"]
-            )
-        else:
-            sums[name] = add(both(name, 0), got[name, "z", 3])
-    return sums, small
+    def crossed(self, name, part, turn):
+        half = turn // 2
+        key = (name, part, "crossed", half)
+        if key not in self.held:
+            own = self.kept(name, part, half)
+            got = self.plan.got[name, part, "first", half]
+            self.held[key] = add(own[: own.shape[0] // 2], got).astype(jnp.bfloat16)
+        height = self.held[key].shape[0] // 2
+        return self.held[key][(turn % 2) * height :][:height]
+
+    def both(self, name, turn):
+        return joined_lanes([self.crossed(name, part, turn) for part in "ab"])
+
+    def advance(self, time):
+        got = self.plan.got
+        while self.left and self.plan.starts[self.left[0]] < time:
+            move = self.left.pop(0)
+            name, way = move[0], self.plan.moves[move][0]
+            if name == "small":
+                small = self.small.astype(jnp.bfloat16)
+                self.small = add(small, self.plan.send(move, small, move[1]))
+                continue
+            kind = self.kinds[name]
+            if "last" in move:
+                value = self.terms[name, move[1]][2 + move[3]]
+            elif "z" in move:
+                turn = move[-1]
+                value = self.pair(name, move[1], turn) if kind == "P" else self.both(name, turn)
+                if turn > 1:
+                    value = add(value, got[move[:-1] + (turn - 1,)]).astype(jnp.bfloat16)
+            elif kind == "P":
+                part = move[1]
+                total = add(self.pair(name, part, 0), got[name, part, "z", 3])
+                self.held[name, part, "own"] = total[: total.shape[0] // 2]
+                value = total[total.shape[0] // 2 :].astype(jnp.bfloat16)
+            else:
+                own = self.kept(name, move[1], move[3])
+                value = own[own.shape[0] // 2 :]
+            self.plan.send(move, value, way)
+
+    def sums(self):
+        got = self.plan.got
+        sums = {}
+        for name, kind in self.kinds.items():
+            if kind == "P":
+                sums[name] = joined_lanes(
+                    [add(self.held[name, part, "own"], got[name, part, "first"]) for part in "ab"]
+                )
+            else:
+                sums[name] = add(self.both(name, 0), got[name, "z", 3])
+        return sums, self.small
 
 
 def moved_blocks(buffers, old, new, count):
@@ -550,77 +579,234 @@
     return add(low, swap(low))
 
 
-def permute_kernel(order_ref, own_ref, other_ref, *out_refs):
-    count = own_ref.shape[1] // 128
-    for part, out_ref in enumerate(out_refs):
-        for block in range(2 * count):
-            source = order_ref[part, block]
-            offset = pl.multiple_of((source % count) * 128, 128)
-            target = slice(block * 128, block * 128 + 128)
-
-            @pl.when(source < count)
-            def _():
-                out_ref[:, target] = own_ref[:, pl.ds(offset, 128)]
-
-            @pl.when(source >= count)
-            def _():
-                out_ref[:, target] = other_ref[:, pl.ds(offset, 128)]
-
-
-def permute_channels(order, own, other):
-    shape = jax.ShapeDtypeStruct((own.shape[0], 2 * own.shape[1]), own.dtype)
+def permute_kernel(order_ref, own_ref, other_ref, a_ref, b_ref, a_t_ref, b_t_ref, both_ref):
+    half = own_ref.shape[1]
+    both_ref[:, :half] = own_ref[...]
+    both_ref[:, half:] = other_ref[...]
+    for block in range(2 * half // LANES):
+        target = slice(block * LANES, block * LANES + LANES)
+        for row, out_ref in enumerate((a_ref, b_ref, a_t_ref, b_t_ref)):
+            offset = pl.multiple_of(order_ref[row, block] * LANES, LANES)
+            taken = both_ref[:, pl.ds(offset, LANES)]
+            if row < 2:
+                out_ref[:, target] = taken
+            else:
+                out_ref[target, :] = taken.astype(jnp.float32).T.astype(taken.dtype)
+
+
+def permute_channels(orders, own, other):
+    words, channels = own.shape[0], 2 * own.shape[1]
     vmem = pl.BlockSpec(memory_space=pltpu.VMEM)
     return pl.pallas_call(
         permute_kernel,
-        out_shape=[shape] * order.shape[0],
+        out_shape=[jax.ShapeDtypeStruct((words, channels), own.dtype)] * 2
+        + [jax.ShapeDtypeStruct((channels, words), own.dtype)] * 2,
         in_specs=[pl.BlockSpec(memory_space=pltpu.SMEM), vmem, vmem],
-        out_specs=[vmem] * order.shape[0],
-    )(order, own, other)
-
-
-def unpermute_kernel(order_ref, first_ref, second_ref, own_ref, other_ref, total_ref):
-    count = own_ref.shape[1] // 128
-    for block in range(2 * count):
-        offset = pl.multiple_of(order_ref[0, block] * 128, 128)
-        total_ref[:, pl.ds(offset, 128)] = first_ref[:, block * 128 : block * 128 + 128]
-    for block in range(2 * count):
-        offset = pl.multiple_of(order_ref[1, block] * 128, 128)
-        total_ref[:, pl.ds(offset, 128)] += second_ref[:, block * 128 : block * 128 + 128]
-    own_ref[...] = total_ref[:, : count * 128]
-    other_ref[...] = total_ref[:, count * 128 :].astype(other_ref.dtype)
-
-
-def unpermute_sum(order, first, second):
-    words, channels = first.shape
-    vmem = pl.BlockSpec(memory_space=pltpu.VMEM)
+        out_specs=[vmem] * 4,
+        scratch_shapes=[pltpu.VMEM((words, channels), own.dtype)],
+        compiler_params=pltpu.CompilerParams(vmem_limit_bytes=24 * 1024 * 1024),
+    )(orders, own, other)
+
+
+def normal_share(values):
+    return 0.5 * (1.0 + lax.erf(values * 0.5**0.5))
+
+
+def load_all(sources, targets, sems):
+    return [
+        pltpu.make_async_copy(source, targets.at[place], sems.at[place])
+        for place, source in enumerate(sources)
+    ]
+
+
+ROWS = 32
+
+
+def mix_kernel(count, a_ref, b_ref, own_ref, bias_ref, *refs):
+    sources = refs[: 2 * count]
+    change_ref, gate_ref, next_ref, held, sems = refs[2 * count :]
+    copies = load_all(sources, held, sems)
+    for copy in copies:
+        copy.start()
+    width = a_ref.shape[1] // count
+    for part, (values_ref, out_ref) in enumerate(((a_ref, change_ref), (b_ref, gate_ref))):
+        for place in range(count):
+            copies[part * count + place].wait()
+            product = jnp.dot(
+                values_ref[:, place * width : (place + 1) * width],
+                held[part * count + place],
+                preferred_element_type=jnp.float32,
+            )
+            if place:
+                out_ref[...] += product
+            else:
+                out_ref[...] = product + bias_ref[part : part + 1, :]
+
+    def rows_of(step, _):
+        rows = pl.ds(pl.multiple_of(step * ROWS, ROWS), ROWS)
+        change, gate = change_ref[rows, :], jax.nn.sigmoid(gate_ref[rows, :])
+        carried = own_ref[rows, :].astype(jnp.float32)
+        mixed = gate * carried + (1.0 - gate) * (change * normal_share(change))
+        next_ref[rows, :] = mixed.astype(next_ref.dtype)
+        return 0
+
+    lax.fori_loop(0, a_ref.shape[0] // ROWS, rows_of, 0)
+
+
+def mix_layer(values, own, bias, pieces):
+    words, channels = own.shape
+    count = len(pieces) // 2
+    vmem, anywhere = [pl.BlockSpec(memory_space=space) for space in (pltpu.VMEM, pl.ANY)]
+    full = jax.ShapeDtypeStruct((words, channels), jnp.float32)
     return pl.pallas_call(
-        unpermute_kernel,
-        out_shape=[
-            jax.ShapeDtypeStruct((words, channels // 2), jnp.float32),
-            jax.ShapeDtypeStruct((words, channels // 2), jnp.bfloat16),
+        partial(mix_kernel, count),
+        out_shape=[full, full, jax.ShapeDtypeStruct((words, channels), own.dtype)],
+        in_specs=[vmem] * 4 + [anywhere] * len(pieces),
+        out_specs=[vmem] * 3,
+        scratch_shapes=[
+            pltpu.VMEM((len(pieces),) + pieces[0].shape, own.dtype),
+            pltpu.SemaphoreType.DMA((len(pieces),)),
         ],
-        in_specs=[pl.BlockSpec(memory_space=pltpu.SMEM), vmem, vmem],
-        out_specs=[vmem] * 2,
-        scratch_shapes=[pltpu.VMEM((words, channels), jnp.float32)],
+        compiler_params=pltpu.CompilerParams(vmem_limit_bytes=40 * 1024 * 1024),
+        cost_estimate=pl.CostEstimate(
+            flops=4_300_000_000, bytes_accessed=16_000_000, transcendentals=1_000_000
+        ),
+    )(*values, own, bias, *pieces)
+
+
+def mix_back_kernel(count, order_ref, grad_ref, change_ref, gate_ref, carried_ref, *refs):
+    sources = refs[: 2 * count]
+    (
+        grad_change_ref, grad_gate_ref, grad_carried_ref, bias_ref, own_ref, other_ref,
+        total_ref, held, sems,
+    ) = refs[2 * count :]
+    copies = load_all(sources, held, sems)
+    for copy in copies:
+        copy.start()
+    words, channels = grad_ref.shape
+    bias_ref[...] = jnp.zeros(bias_ref.shape, jnp.float32)
+
+    def rows_of(step, _):
+        rows = pl.ds(pl.multiple_of(step * ROWS, ROWS), ROWS)
+        grad, change = grad_ref[rows, :], change_ref[rows, :]
+        gate = jax.nn.sigmoid(gate_ref[rows, :])
+        share = normal_share(change)
+        slope = share + change * jnp.exp(change * change * -0.5) * (0.5 / math.pi) ** 0.5
+        rest = grad * (1.0 - gate)
+        grad_change = (rest * slope).astype(jnp.bfloat16)
+        grad_gate = rest * gate * (carried_ref[rows, :].astype(jnp.float32) - change * share)
+        grad_gate = grad_gate.astype(jnp.bfloat16)
+        grad_change_ref[rows, :] = grad_change
+        grad_gate_ref[rows, :] = grad_gate
+        grad_carried_ref[rows, :] = grad * gate
+        for part, piece in enumerate((grad_change, grad_gate)):
+            bias_ref[part : part + 1, :] += jnp.sum(
+                piece.astype(jnp.float32), axis=0, keepdims=True
+            )
+        return 0
+
+    lax.fori_loop(0, words // ROWS, rows_of, 0)
+    blocks = 2 * channels // LANES // count
+    for part, values_ref in enumerate((grad_change_ref, grad_gate_ref)):
+        for place in range(count):
+            copies[part * count + place].wait()
+            product = lax.dot_general(
+                values_ref[...],
+                held[part * count + place],
+                (((1,), (1,)), ((), ())),
+                preferred_element_type=jnp.float32,
+            )
+            for block in range(blocks):
+                source = order_ref[part, place * blocks + block]
+                lanes = pl.ds(pl.multiple_of(source * LANES, LANES), LANES)
+                piece = product[:, block * LANES : (block + 1) * LANES]
+                if part:
+                    total_ref[:, lanes] += piece
+                else:
+                    total_ref[:, lanes] = piece
+    own_ref[...] = total_ref[:, :channels] + grad_carried_ref[...]
+    other_ref[...] = total_ref[:, channels:].astype(other_ref.dtype)
+
+
+def mix_layer_back(order, grad, change, gate, carried, pieces):
+    words, channels = grad.shape
+    count = len(pieces) // 2
+    vmem, anywhere = [pl.BlockSpec(memory_space=space) for space in (pltpu.VMEM, pl.ANY)]
+    low = jax.ShapeDtypeStruct((words, channels), jnp.bfloat16)
+    full = jax.ShapeDtypeStruct((words, channels), jnp.float32)
+    results = pl.pallas_call(
+        partial(mix_back_kernel, count),
+        out_shape=[low, low, full, jax.ShapeDtypeStruct((2, channels), jnp.float32), full, low],
+        in_specs=[pl.BlockSpec(memory_space=pltpu.SMEM)] + [vmem] * 4 + [anywhere] * len(pieces),
+        out_specs=[vmem] * 6,
+        scratch_shapes=[
+            pltpu.VMEM((words, 2 * channels), jnp.float32),
+            pltpu.VMEM((len(pieces),) + pieces[0].shape, jnp.bfloat16),
+            pltpu.SemaphoreType.DMA((len(pieces),)),
+        ],
+        compiler_params=pltpu.CompilerParams(vmem_limit_bytes=40 * 1024 * 1024),
+        cost_estimate=pl.CostEstimate(
+            flops=4_300_000_000, bytes_accessed=16_000_000, transcendentals=1_000_000
+        ),
+    )(order, grad, change, gate, carried, *pieces)
+    return results[:2], results[3], results[4], results[5]
+
+
+def outer_kernel(count, a_t_ref, b_t_ref, grad_a_ref, grad_b_ref, *refs):
+    out_refs, (held, sems) = refs[: 2 * count], refs[2 * count :]
+    height = a_t_ref.shape[0] // count
+    copies = []
+    for part, (rows_ref, grad_ref) in enumerate(((a_t_ref, grad_a_ref), (b_t_ref, grad_b_ref))):
+        for place in range(count):
+            spot = part * count + place
+            held[spot] = jnp.dot(
+                rows_ref[place * height : (place + 1) * height, :],
+                grad_ref[...],
+                preferred_element_type=jnp.float32,
+            ).astype(held.dtype)
+            copies.append(pltpu.make_async_copy(held.at[spot], out_refs[spot], sems.at[spot]))
+            copies[-1].start()
+    for copy in copies:
+        copy.wait()
+
+
+def outer_products(rows, grads, count):
+    channels, width = rows[0].shape[0], grads[0].shape[1]
+    shape = (channels // count, width)
+    vmem, anywhere = [pl.BlockSpec(memory_space=space) for space in (pltpu.VMEM, pl.ANY)]
+    results = pl.pallas_call(
+        partial(outer_kernel, count),
+        out_shape=[jax.ShapeDtypeStruct(shape, jnp.bfloat16)] * (2 * count),
+        in_specs=[vmem] * 4,
+        out_specs=[anywhere] * (2 * count),
+        scratch_shapes=[
+            pltpu.VMEM((2 * count,) + shape, jnp.bfloat16),
+            pltpu.SemaphoreType.DMA((2 * count,)),
+        ],
         compiler_params=pltpu.CompilerParams(vmem_limit_bytes=32 * 1024 * 1024),
-    )(order, first, second)
-
-
-READY = {"highway1": 12.0, "highway0": 16.0, "small": 24.0}
-CONV_AFTER = [("highway0", "b", "z", 1)]
-GATHER_KINDS = {"highway0": "P", "highway1": "Q", "encoder": "P"}
-SCATTER_KINDS = {"encoder": "P", "highway1": "P", "highway0": "Q"}
-
-
-def times_pieces(values, pieces):
-    columns = jnp.split(values, len(pieces), axis=1)
-    return reduce(
-        jnp.add,
-        [
-            jnp.dot(column, piece, preferred_element_type=jnp.float32)
-            for column, piece in zip(columns, pieces)
-        ],
-    )
+        cost_estimate=pl.CostEstimate(
+            flops=4_300_000_000, bytes_accessed=11_000_000, transcendentals=0
+        ),
+    )(*rows, *grads)
+    return results[:count], results[count:]
+
+
+SLACK = 4.0
+GATHER_KINDS = {"highway0": "Q", "highway1": "P", "encoder": "P"}
+GATHER_RANKS = {"highway0": -8.0, ("encoder", "b"): 6.0}
+SCATTER_KINDS = {"encoder": "P", "highway1": "Q", "highway0": "Q"}
+READY = {
+    ("encoder", "b"): 0.0,
+    ("encoder", "a"): 5.0,
+    "highway1": 9.0,
+    "highway0": 13.0,
+    "small": 30.0,
+}
+SCATTER_RANKS = {"encoder": -20.0, "highway1": -10.0}
+BACK_TIMES = (9.0, 4.9)
+POOL_TIMES = (4.0, 6.0, 8.0, 10.0, 12.0, 14.0)
+POOL_BACK_TIMES = (15.0, 17.5, 20.0, 22.5, 25.0, 27.0)
+POOL_CUTS = (0, 1, 2, 3, 5, 8)
 
 
 def packed(values):
@@ -701,7 +887,6 @@
     ).astype(f32)
     scale_row, bias_row = chan_scale[None, :], conv_bias[None, :]
     width_row = widths.astype(f32)[None, :]
-    pool, pool_back = conv_calls(word_count, own_filters)
     here = lax.axis_index("wide")
     core = lax.axis_index("narrow")
     routed = lax.axis_size("wide") == CHIPS
@@ -719,14 +904,8 @@
     def own_rows(terms):
         return lax.psum_scatter(terms.astype(f32), "wide", scatter_dimension=0, tiled=True)
 
-    arrived = {}
-
-    def after(value, moves):
-        ended = [arrived[move] for move in moves if move in arrived]
-        return lax.optimization_barrier((value, *ended))[0] if ended else value
-
     if routed:
-        full, arrived = gather_matrices(
+        full, gather_plan = gather_matrices(
             {
                 "highway0": [highway_weight[0, :, part] for part in range(2)],
                 "highway1": [highway_weight[1, :, part] for part in range(2)],
@@ -741,7 +920,13 @@
         scattered_blocks = {part: blocks_of(SCATTER_KINDS["encoder"], part) for part in "ab"}
         features = gathered_blocks["a"]
         first_full, second_full = [
-            moved_blocks(full["encoder", part], gathered_blocks[part], features, 1)[0]
+            moved_blocks(
+                [gather_plan.after_all(full["encoder", part][0], "encoder", part)]
+                + full["encoder", part][1:],
+                gathered_blocks[part],
+                features,
+                1,
+            )[0]
             for part in "ab"
         ]
         feature_order = owners(features, here)
@@ -752,10 +937,21 @@
         ]
         first_full, second_full = whole_rows(first_rows), whole_rows(second_rows)
         feature_order = jnp.arange(lax.axis_size("wide"), dtype=jnp.int32)
-    embedded, pooled, pool_shift = pool(
-        after(tile_chunks, CONV_AFTER), spread_ids, table_t, tap_lanes, masked_filters, scale_row, bias_row, lens,
-        width_row,
-    )
+    cuts = [cut * tile_count // 16 for cut in POOL_CUTS] + [tile_count]
+    pool_pieces = []
+    for first, last, time in zip(cuts, cuts[1:], POOL_TIMES):
+        rows = slice(first * TILE, last * TILE)
+        id_rows = slice(first * (SLOTS // CHUNK), last * (SLOTS // CHUNK))
+        chunks = tile_chunks[first:last]
+        if routed:
+            chunks = gather_plan.after(chunks, time)
+        pool, pool_back = conv_calls((last - first) * TILE, own_filters)
+        results = pool(
+            chunks, spread_ids[id_rows], table_t, tap_lanes, masked_filters, scale_row, bias_row,
+            lens[rows], width_row,
+        )
+        pool_pieces.append((rows, id_rows, first, last, pool_back, results))
+    pooled = joined([results[1] for *_, results in pool_pieces])
     current = gelu_exact(pooled).astype(bf16)
     proj_t, qkv_full, out_t = jnp.split(
         first_full, [width_proj, width_proj + width_qkv], axis=1
@@ -783,35 +979,24 @@
     grad_output = jnp.dot(cotangent, feature_moves.T, preferred_element_type=f32).astype(bf16)
     grad_output = jnp.dot(picks_low, grad_output, preferred_element_type=f32)
     kept_layers = []
+    block_count = 2 * own_filters // LANES
     for layer_index in range(HW_LAYERS):
+        name = f"highway{layer_index}"
+        orders = [jnp.arange(block_count, dtype=jnp.int32)] * 4
         if routed:
-            name = f"highway{layer_index}"
-            orders = {}
-            for kind in (GATHER_KINDS[name], SCATTER_KINDS[name]):
-                order = jnp.stack([owners(blocks_of(kind, part), here) for part in "ab"])
-                orders[kind] = (order - core * (CHIPS // 2)) % CHIPS
-            order = orders[GATHER_KINDS[name]]
-            whole_input = permute_channels(
-                jnp.concatenate(list(orders.values())), current, swap(current)
-            )
-            grad_input = whole_input[-2:]
-        else:
-            order = None
-            whole_input = [lax.all_gather(current, "narrow", axis=1, tiled=True)] * 2
-            grad_input = whole_input
-        mixed_pre = (
-            jnp.stack(
-                [
-                    times_pieces(whole_input[part], highway_full[layer_index][part])
-                    for part in range(2)
-                ],
-                axis=1,
-            )
-            + highway_bias[layer_index]
-        )
-        carried = current.astype(f32)
-        kept_layers.append((grad_input, mixed_pre, carried, order))
-        current = highway_mix(mixed_pre, carried).astype(bf16)
+            orders = [
+                owners(blocks_of(kinds[name], part), here)
+                for kinds in (GATHER_KINDS, SCATTER_KINDS)
+                for part in "ab"
+            ]
+        order = (jnp.stack(orders) - core * (block_count // 2)) % block_count
+        *whole_input, rows_a, rows_b = permute_channels(order, current, swap(current))
+        if routed:
+            whole_input[0] = gather_plan.after_all(whole_input[0], name)
+        pieces = highway_full[layer_index][0] + highway_full[layer_index][1]
+        change, gate, mixed = mix_layer(whole_input, current, highway_bias[layer_index], pieces)
+        kept_layers.append((order[:2], change, gate, current, pieces, (rows_a, rows_b)))
+        current = mixed
     start_rows = (
         pair_sum(jnp.dot(current, proj_t.T, preferred_element_type=f32)) + vector_biases[0]
     )
@@ -850,6 +1035,8 @@
     encoded = layer_norm(before_two, norm_gains[1], vector_biases[4]).astype(bf16)
     encoded = jnp.dot(encoded, feature_moves, preferred_element_type=f32).astype(bf16)
     encoded = jnp.dot(picks_low.T, encoded, preferred_element_type=f32).astype(bf16)
+    if routed:
+        scatter = Scatter(SCATTER_KINDS, READY)
     ln_two_back = jax.vjp(layer_norm, before_two, norm_gains[1], vector_biases[4])[1]
     grad_before_two, gain_two, bias_two = ln_two_back(grad_output)
     grad_lowered = grad_before_two.astype(bf16)
@@ -903,57 +1090,39 @@
         [proj_grad_local, qkv_grad_local, out_grad_local], axis=1
     ).astype(bf16)
     second_grad_local = jnp.concatenate([up_grad_local, down_grad_local], axis=1).astype(bf16)
-    terms = {}
     if routed:
         for part, local in (("a", first_grad_local), ("b", second_grad_local)):
-            terms["encoder", part] = moved_blocks([local], features, scattered_blocks[part], 4)
+            scatter.terms["encoder", part] = moved_blocks([local], features, scattered_blocks[part], 4)
     highway_grads = []
     highway_bias_grads = []
     for layer_index in reversed(range(HW_LAYERS)):
-        grad_input, mixed_pre, carried, order = kept_layers[layer_index]
-        mix_back = jax.vjp(highway_mix, mixed_pre, carried)[1]
-        grad_mixed, grad_carried = mix_back(grad_current)
-        grad_mixed_low = grad_mixed.astype(bf16)
-        part_grads = []
-        grad_whole = []
-        for part in range(2):
-            part_mixed = grad_mixed_low[:, part]
-            pieces = highway_full[layer_index][part]
-            part_grads.append(
-                [
-                    jnp.dot(columns.T, part_mixed, preferred_element_type=f32).astype(bf16)
-                    for columns in jnp.split(grad_input[part], len(pieces), axis=1)
-                ]
-            )
-            grad_whole.append(
-                jnp.concatenate(
-                    [
-                        jnp.dot(part_mixed, piece.T, preferred_element_type=f32)
-                        for piece in pieces
-                    ],
-                    axis=1,
-                )
-            )
+        order, change, gate, carried, pieces, rows = kept_layers[layer_index]
         if routed:
-            terms.update(zip([(f"highway{layer_index}", part) for part in "ab"], part_grads))
+            scatter.advance(READY[f"highway{layer_index}"])
+            grad_current = scatter.plan.after(grad_current, BACK_TIMES[layer_index])
+        part_grads, bias_sums, grad_own, grad_other = mix_layer_back(
+            order, grad_current, change, gate, carried, pieces
+        )
+        terms = outer_products(rows, part_grads, len(pieces) // 2)
+        if routed:
+            scatter.terms.update(zip([(f"highway{layer_index}", part) for part in "ab"], terms))
         else:
-            highway_grads.insert(
-                0, jnp.stack([own_rows(joined(pieces)) for pieces in part_grads], axis=1)
-            )
-        highway_bias_grads.insert(0, jnp.sum(grad_mixed_low.astype(f32), axis=0))
-        if routed:
-            grad_own, grad_other = unpermute_sum(order, *grad_whole)
-            grad_current = grad_carried + add(grad_own, swap(grad_other))
-        else:
-            grad_current = grad_carried + lax.psum_scatter(
-                add(*grad_whole).astype(bf16), "narrow", scatter_dimension=1, tiled=True
-            ).astype(f32)
+            highway_grads.insert(0, jnp.stack([own_rows(joined(part)) for part in terms], axis=1))
+        highway_bias_grads.insert(0, bias_sums)
+        grad_current = add(grad_own, swap(grad_other))
     highway_bias_local = jnp.stack(highway_bias_grads)
     grad_pooled = jax.vjp(gelu_exact, pooled)[1](grad_current)[0]
-    grad_filter, grad_marks = pool_back(
-        tile_chunks, spread_ids, tap_lanes, masked_filters, scale_row, lens, width_row, embedded,
-        pool_shift, grad_pooled,
-    )
+    grad_filter = jnp.zeros((LANES, own_filters), f32)
+    grad_marks = jnp.zeros((IDS, 2 * LANES), f32)
+    for (rows, id_rows, first, last, pool_back, results), time in zip(pool_pieces, POOL_BACK_TIMES):
+        chunks = tile_chunks[first:last]
+        if routed:
+            scatter.advance(time)
+            chunks = scatter.plan.after(chunks, time - 1.0)
+        grad_filter, grad_marks = pool_back(
+            chunks, spread_ids[id_rows], tap_lanes, masked_filters, scale_row, lens[rows], width_row,
+            results[0], results[2], grad_pooled[rows], grad_filter, grad_marks,
+        )
     grad_filter = grad_filter[: TAPS * CHAR_DIM]
     grad_conv_bias = jnp.sum(grad_pooled, axis=0)
     grad_marks = grad_marks[:CHAR_VOCAB, :LANES] + grad_marks[:CHAR_VOCAB, LANES:]
@@ -976,7 +1145,9 @@
         pair_sum(grad_chars),
     )
     if routed:
-        sums, small = scatter_matrices(terms, SCATTER_KINDS, packed(locals_small), READY)
+        scatter.small = packed(locals_small)
+        scatter.advance(float("inf"))
+        sums, small = scatter.sums()
         small_sums = unpacked(small, locals_small)
         highway_grads = [
             sums[f"highway{layer}"].reshape(highway_weight.shape[1:]) for layer in range(HW_LAYERS)

time: 660 us -> 582 us (0.88)
  waiting for transfers between devices: 265 us -> 207 us
  matrix products: 96.5 us -> 40.1 us
  Pallas kernels: 80.6 us -> 108 us
  local copies, waits for them, and re-layouts: 53.6 us -> 80.8 us
  other arithmetic: 82.1 us -> 57.7 us
    ppermute x74 -> x73, waiting for transfers between devices: 263 us -> 205 us  [step(): return lax.ppermute(value, 'wide', STEPS[axis])]
    dot_general x48 -> x0, matrix products: 54.9 us -> none  [the longest x16 22.2 us: per_device(): jnp.dot(columns.T, part_mixed, preferred_element_type=f32).astype(bf16)]
    pallas_call x6 -> x20, Pallas kernels: 73.3 us -> 101 us  [the longest x6 37.4 us: per_device(): pool_back(chunks, spread_ids[id_rows], tap_lanes, masked_filters, scale_r...]
    unnamed x427 -> x481, local copies, waits for them, and re-layouts: 24.4 us -> 36.6 us
    concatenate x16, other arithmetic: 12.9 us -> 1.81 us  [joined(): return pieces[0] if len(pieces) == 1 else jnp.concatenate(pieces, axis=0)]
    broadcast_in_dim x3 -> x0, other arithmetic: 6.98 us -> none  [the longest x2 4.1 us: highway_mix(): mixed_pre[:, 0]]
    ppermute x74 -> x73, starting transfers between devices: 66.9 us -> 71.5 us  [step(): return lax.ppermute(value, 'wide', STEPS[axis])]
    convert_element_type x20 -> x31, other arithmetic: 26.3 us -> 28.1 us  [the longest x12 16.2 us: kept(): self.held[key] = add(self.terms[name, part][half], got).astype(jnp.bfloat16)]
  transfers between devices with their start and end apart: 84 -> 83, of which waited for: 35 -> 28; matrix products, arithmetic and copies ran while one was open for 28% -> 21% of each run, Pallas kernels for 12% -> 19%
where the time goes in v3:
time: 582 us; the launch traced here: 571 us
  waiting for transfers between devices  207 us (36%)
  Pallas kernels  108 us (19%)
  local copies, waits for them, and re-layouts  80.8 us (14%)
  starting transfers between devices  72.2 us (12%)
  other arithmetic  57.7 us (10%)
  matrix products  40.1 us (7%)
    ppermute x73, waiting for transfers between devices, step(): return lax.ppermute(value, 'wide', STEPS[axis])  205 us
    ppermute x73, starting transfers between devices, step(): return lax.ppermute(value, 'wide', STEPS[axis])  71.5 us
    pallas_call x6, Pallas kernels, per_device(): pool_back(chunks, spread_ids[id_rows], tap_lanes, masked_filters, scale_r...  37.4 us
    unnamed x481, local copies, waits for them, and re-layouts  36.6 us
    pallas_call x6, Pallas kernels, per_device(): pool(chunks, spread_ids[id_rows], table_t, tap_lanes, masked_filters, sca...  24.4 us
    convert_element_type x12, other arithmetic, kept(): self.held[key] = add(self.terms[name, part][half], got).astype(jnp.bfloat16)  16.2 us
    pallas_call x2, Pallas kernels, mix_layer_back(): pl.pallas_call(partial(mix_back_kernel, count), out_shape=[low, low, full...  15.4 us
  transfers between devices with their start and end apart: 83, of which 28 were waited for; matrix products, arithmetic and copies ran while one was open for 21% of the time, Pallas kernels for 19%

profile of v3, /device:TPU:0, one launch (start us, length us, event | category | flops | bytes accessed | tf_op | source)
XLA Modules:
  0.0 571.4 jit_solution(11942095196783545099)
XLA Ops:
  36.5 9.1 %collective-permute-done.5 = bf16[256,1024]{1,0:T(8,128)(2,1)S(1)} collective-permute-done((bf16[256,1024]{1,0:T(8,128)(2,1)S(1)}, bf16[256,1024]{1,0:T(8,128)(2,1)S(1)}, u32[]{:S(2)}, u32[]{:S(2)}) %collective-permute-start.5) | collective-permute-done | bytes 524320 | tf_op jit(solution)/shard_map/ppermute | solution.py:278
  47.4 4.9 shard_map.289
  61.7 6.5 %collective-permute-done.9 = bf16[256,1024]{1,0:T(8,128)(2,1)S(1)} collective-permute-done((bf16[256,1024]{1,0:T(8,128)(2,1)S(1)}, bf16[256,1024]{1,0:T(8,128)(2,1)S(1)}, u32[]{:S(2)}, u32[]{:S(2)}) %collective-permute-start.9) | collective-permute-done | bytes 524320 | tf_op jit(solution)/shard_map/ppermute | solution.py:278
  71.4 8.0 %collective-permute-done.12 = bf16[128,2048]{1,0:T(8,128)(2,1)S(1)} collective-permute-done((bf16[128,2048]{1,0:T(8,128)(2,1)S(1)}, bf16[128,2048]{1,0:T(8,128)(2,1)S(1)}, u32[]{:S(2)}, u32[]{:S(2)}) %collective-permute-start.12) | collective-permute-done | bytes 524320 | tf_op jit(solution)/shard_map/ppermute | solution.py:278
  79.5 10.4 %collective-permute-done.13 = bf16[96,2560]{1,0:T(8,128)(2,1)S(1)} collective-permute-done((bf16[96,2560]{1,0:T(8,128)(2,1)S(1)}, bf16[96,2560]{1,0:T(8,128)(2,1)S(1)}, u32[]{:S(2)}, u32[]{:S(2)}) %collective-permute-start.13) | collective-permute-done | bytes 491552 | tf_op jit(solution)/shard_map/ppermute | solution.py:278
  93.2 8.0 %collective-permute-done.16 = bf16[256,1024]{1,0:T(8,128)(2,1)S(1)} collective-permute-done((bf16[256,1024]{1,0:T(8,128)(2,1)S(1)}, bf16[256,1024]{1,0:T(8,128)(2,1)S(1)}, u32[]{:S(2)}, u32[]{:S(2)}) %collective-permute-start.16) | collective-permute-done | bytes 524320 | tf_op jit(solution)/shard_map/ppermute | solution.py:278
  110.8 4.9 collective-permute-done.14.refs_6_
  118.1 6.2 %shard_map.294 = (bf16[64,128,128]{2,1,0:T(8,128)(2,1)S(1)}, f32[128,1024]{1,0:T(8,128)S(1)}, f32[128,1024]{1,0:T(8,128)S(1)}) custom-call(s32[8]{0:T(128)S(1)} %slice.418.tile_ref, s32[64,128]{1,0:T(8,128)S(1)} %slice.424.ids_ref, bf16[128,272]{1,0:T(8,128)(2,1)S(1)} %pad.42.table_ref, f32[8,128]{1,0:T(8,128)S(1)} %fusion.99.lanes_ref, ...), custom_call_target="tpu_custom_call" | custom-call | flops 2000000000 | bytes 8000000 | tf_op jit(solution)/shard_map/pallas_call | solution.py:949
  136.3 10.4 %collective-permute-done.23 = bf16[256,1024]{1,0:T(8,128)(2,1)S(1)} collective-permute-done((bf16[256,1024]{1,0:T(8,128)(2,1)S(1)}, bf16[256,1024]{1,0:T(8,128)(2,1)S(1)}, u32[]{:S(2)}, u32[]{:S(2)}) %collective-permute-start.23) | collective-permute-done | bytes 524320 | tf_op jit(solution)/shard_map/ppermute | solution.py:278
  146.6 10.2 %collective-permute-done.26 = bf16[256,1024]{1,0:T(8,128)(2,1)S(1)} collective-permute-done((bf16[256,1024]{1,0:T(8,128)(2,1)S(1)}, bf16[256,1024]{1,0:T(8,128)(2,1)S(1)}, u32[]{:S(2)}, u32[]{:S(2)}) %collective-permute-start.26) | collective-permute-done | bytes 524320 | tf_op jit(solution)/shard_map/ppermute | solution.py:278
  160.8 4.9 shard_map.296
  165.9 17.5 %collective-permute-done.29 = bf16[96,3072]{1,0:T(8,128)(2,1)S(1)} collective-permute-done((bf16[96,3072]{1,0:T(8,128)(2,1)S(1)}, bf16[96,3072]{1,0:T(8,128)(2,1)S(1)}, u32[]{:S(2)}, u32[]{:S(2)}) %collective-permute-start.29) | collective-permute-done | bytes 589856 | tf_op jit(solution)/shard_map/ppermute | solution.py:278
  200.2 5.6 shard_map.298
  213.2 8.3 %collective-permute-done.37 = bf16[96,3072]{1,0:T(8,128)(2,1)S(1)} collective-permute-done((bf16[96,3072]{1,0:T(8,128)(2,1)S(1)}, bf16[96,3072]{1,0:T(8,128)(2,1)S(1)}, u32[]{:S(2)}, u32[]{:S(2)}) %collective-permute-start.37) | collective-permute-done | bytes 589856 | tf_op jit(solution)/shard_map/ppermute | solution.py:278
  238.4 8.9 %collective-permute-done.38.refs_3_ = bf16[192,3072]{1,0:T(8,128)(2,1)} collective-permute-done((bf16[192,3072]{1,0:T(8,128)(2,1)S(1)}, bf16[192,3072]{1,0:T(8,128)(2,1)}, u32[]{:S(2)}, u32[]{:S(2)}) %collective-permute-start.38) | collective-permute-done | bytes 1179680 | tf_op jit(solution)/shard_map/ppermute | solution.py:278
  251.6 5.7 multiply_convert_fusion.1
  312.9 7.7 %shard_map.302 = (bf16[256,1024]{1,0:T(8,128)(2,1)S(1)}, bf16[256,1024]{1,0:T(8,128)(2,1)S(1)}, f32[256,1024]{1,0:T(8,128)}, f32[2,1024]{1,0:T(2,128)S(1)}, f32[...) custom-call(s32[2,16]{1,0:T(2,128)S(1)} %slice.437.order_ref, f32[256,1024]{1,0:T(8,128)S(1)} %fusion.24.grad_ref, ...), custom_call_target="tpu_custom_call" | custom-call | flops 4300000256 | bytes 16000000 | tf_op jit(solution)/shard_map/pallas_call | solution.py:737
  320.6 5.0 shard_map.303
  338.4 7.7 %shard_map.305 = (bf16[256,1024]{1,0:T(8,128)(2,1)S(1)}, bf16[256,1024]{1,0:T(8,128)(2,1)S(1)}, f32[256,1024]{1,0:T(8,128)}, f32[2,1024]{1,0:T(2,128)S(1)}, f32[...) custom-call(s32[2,16]{1,0:T(2,128)S(1)} %slice.447.order_ref, f32[256,1024]{1,0:T(8,128)S(1)} %convert_add_fusion.3.grad_ref, ...), custom_call_target="tpu_custom_call" | custom-call | flops 4300000256 | bytes 16000000 | tf_op jit(solution)/shard_map/pallas_call | solution.py:737
  372.7 7.9 %shard_map.307 = (f32[128,1024]{1,0:T(8,128)S(1)}, f32[272,256]{1,0:T(8,128)S(1)}) custom-call(s32[1]{0:T(128)} %get-tuple-element.407.tile_ref, s32[8,128]{1,0:T(8,128)S(1)} %copy-done.69, f32[8,128]{1,0:T(8,128)S(1)} %copy-done.75, bf16[128,1024]{1,0:T(8,128)(2,1)S(1)} %copy-done.42, f32[1,1024]{1,0:T(1,128)S(1)} %copy-done.71, f32[16,1]{1,0:T(8,128)S(1)} %copy-done.62, ...), custom_call_target="tpu_custom_call" | custom-call | flops 4000000000 | bytes 10000000 | tf_op jit(solution)/shard_map/pallas_call | solution.py:1122
  389.4 7.8 %collective-permute-done.51 = bf16[96,2560]{1,0:T(8,128)(2,1)S(1)} collective-permute-done((bf16[96,2560]{1,0:T(8,128)(2,1)S(1)}, bf16[96,2560]{1,0:T(8,128)(2,1)S(1)}, u32[]{:S(2)}, u32[]{:S(2)}) %collective-permute-start.51) | collective-permute-done | bytes 491552 | tf_op jit(solution)/shard_map/ppermute | solution.py:278
  420.0 5.8 %shard_map.310 = (f32[128,1024]{1,0:T(8,128)S(1)}, f32[272,256]{1,0:T(8,128)S(1)}) custom-call(s32[2]{0:T(128)S(1)} %copy-done.107, s32[16,128]{1,0:T(8,128)S(1)} %copy-done.56, f32[8,128]{1,0:T(8,128)S(1)} %copy-done.75, bf16[128,1024]{1,0:T(8,128)(2,1)S(1)} %copy-done.42, f32[1,1024]{1,0:T(1,128)S(1)} %copy-done.71, f32[32,1]{1,0:T(8,128)S(1)} %copy.158.lens_ref, ...), custom_call_target="tpu_custom_call" | custom-call | flops 4000000000 | bytes 10000000 | tf_op jit(solution)/shard_map/pallas_call | solution.py:1122
  425.8 6.4 %collective-permute-done.57 = bf16[48,2560]{1,0:T(8,128)(2,1)S(1)} collective-permute-done((bf16[48,2560]{1,0:T(8,128)(2,1)S(1)}, bf16[48,2560]{1,0:T(8,128)(2,1)S(1)}, u32[]{:S(2)}, u32[]{:S(2)}) %collective-permute-start.57) | collective-permute-done | bytes 245792 | tf_op jit(solution)/shard_map/ppermute | solution.py:278
  449.8 9.2 %shard_map.312 = (f32[128,1024]{1,0:T(8,128)S(1)}, f32[272,256]{1,0:T(8,128)S(1)}) custom-call(s32[8]{0:T(128)S(1)} %copy-done.103, s32[64,128]{1,0:T(8,128)S(1)} %copy-done.46, f32[8,128]{1,0:T(8,128)S(1)} %copy-done.75, bf16[128,1024]{1,0:T(8,128)(2,1)S(1)} %copy-done.42, f32[1,1024]{1,0:T(1,128)S(1)} %copy-done.71, f32[128,1]{1,0:T(8,128)S(1)} %copy-done.44, ...), custom_call_target="tpu_custom_call" | custom-call | flops 4000000000 | bytes 10000000 | tf_op jit(solution)/shard_map/pallas_call | solution.py:1122
  468.7 5.7 collective-permute-done.66
  478.0 5.9 %collective-permute-done.70 = bf16[128,2048]{1,0:T(8,128)(2,1)S(1)} collective-permute-done((bf16[128,2048]{1,0:T(8,128)(2,1)S(1)}, bf16[128,2048]{1,0:T(8,128)(2,1)S(1)}, u32[]{:S(2)}, u32[]{:S(2)}) %collective-permute-start.70) | collective-permute-done | bytes 524320 | tf_op jit(solution)/shard_map/ppermute | solution.py:278
  493.5 7.3 %collective-permute-done.71 = bf16[256,1024]{1,0:T(8,128)(2,1)S(1)} collective-permute-done((bf16[256,1024]{1,0:T(8,128)(2,1)S(1)}, bf16[256,1024]{1,0:T(8,128)(2,1)S(1)}, u32[]{:S(2)}, u32[]{:S(2)}) %collective-permute-start.71) | collective-permute-done | bytes 524320 | tf_op jit(solution)/shard_map/ppermute | solution.py:278
  503.1 8.9 %collective-permute-done.79 = bf16[256,1024]{1,0:T(8,128)(2,1)S(1)} collective-permute-done((bf16[256,1024]{1,0:T(8,128)(2,1)S(1)}, bf16[256,1024]{1,0:T(8,128)(2,1)S(1)}, u32[]{:S(2)}, u32[]{:S(2)}) %collective-permute-start.79) | collective-permute-done | bytes 524320 | tf_op jit(solution)/shard_map/ppermute | solution.py:278
  512.5 5.3 collective-permute-done.75
  522.0 5.4 collective-permute-done.78
  530.4 9.7 %collective-permute-done.81 = bf16[128,2048]{1,0:T(8,128)(2,1)} collective-permute-done((bf16[128,2048]{1,0:T(8,128)(2,1)}, bf16[128,2048]{1,0:T(8,128)(2,1)}, u32[]{:S(2)}, u32[]{:S(2)}) %collective-permute-start.81) | collective-permute-done | bytes 524320 | tf_op jit(solution)/shard_map/ppermute | solution.py:278
  542.2 20.1 %collective-permute-done.80 = bf16[144,1024]{1,0:T(8,128)(2,1)S(1)} collective-permute-done((bf16[144,1024]{1,0:T(8,128)(2,1)S(1)}, bf16[144,1024]{1,0:T(8,128)(2,1)S(1)}, u32[]{:S(2)}, u32[]{:S(2)}) %collective-permute-start.80) | collective-permute-done | bytes 294944 | tf_op jit(solution)/shard_map/ppermute | solution.py:278
  (917 shorter events, 311.2 us)
Async XLA Ops:
  2.4 43.3 %collective-permute-start.3 = (bf16[48,3072]{1,0:T(8,128)(2,1)}, bf16[48,3072]{1,0:T(8,128)(2,1)S(1)}, u32[]{:S(2)}, u32[]{:S(2)}) collective-permute-start(bf16[48,3072]{1,0:T(8,128)(2,1)} %pad_maximum_fusion.23), channel_id=1, source_target_pairs={{0,4},{2,6},{4,0},{6,2},{8,12},{10,14},{12,8},{14,10},{16,20},{18,... | collective-permute-start | bytes 884744 | tf_op jit(solution)/shard_map/ppermute | solution.py:278
  45.8 45.8 %collective-permute-start.11 = (bf16[512,1024]{1,0:T(8,128)(2,1)S(1)}, bf16[512,1024]{1,0:T(8,128)(2,1)S(1)}, u32[]{:S(2)}, u32[]{:S(2)}) collective-permute-start(bf16[512,1024]{1,0:T(8,128)(2,1)S(1)} %pad_maximum_fusion.5.refs_0_), channel_id=1, source_target_pairs={{0,4},{2,6},{4,0},{6,2},{8,12},{10,14},{12,8},{14,10},{16,20},{18,... | collective-permute-start | bytes 3145736 | tf_op jit(solution)/shard_map/ppermute | solution.py:278
  52.5 40.7 %collective-permute-start.10 = (bf16[512,1024]{1,0:T(8,128)(2,1)S(1)}, bf16[512,1024]{1,0:T(8,128)(2,1)S(1)}, u32[]{:S(2)}, u32[]{:S(2)}) collective-permute-start(bf16[512,1024]{1,0:T(8,128)(2,1)S(1)} %pad_maximum_fusion.4.refs_4_), channel_id=1, source_target_pairs={{0,2},{2,0},{4,6},{6,4},{8,10},{10,8},{12,14},{14,12},{16,18},{18,... | collective-permute-start | bytes 3145736 | tf_op jit(solution)/shard_map/ppermute | solution.py:278
  56.9 44.2 %collective-permute-start.15 = (bf16[512,1024]{1,0:T(8,128)(2,1)S(1)}, bf16[512,1024]{1,0:T(8,128)(2,1)S(1)}, u32[]{:S(2)}, u32[]{:S(2)}) collective-permute-start(bf16[512,1024]{1,0:T(8,128)(2,1)S(1)} %pad_maximum_fusion.7.refs_0_), channel_id=1, source_target_pairs={{0,4},{2,6},{4,0},{6,2},{8,12},{10,14},{12,8},{14,10},{16,20},{18,... | collective-permute-start | bytes 3145736 | tf_op jit(solution)/shard_map/ppermute | solution.py:278
  91.6 35.8 %collective-permute-start.18 = (bf16[256,1024]{1,0:T(8,128)(2,1)S(1)}, bf16[256,1024]{1,0:T(8,128)(2,1)S(1)}, u32[]{:S(2)}, u32[]{:S(2)}) collective-permute-start(bf16[256,1024]{1,0:T(8,128)(2,1)S(1)} %pad_maximum_fusion.19), channel_id=1, source_target_pairs={{0,4},{2,6},{4,0},{6,2},{8,12},{10,14},{12,8},{14,10},{16,20},{18,... | collective-permute-start | bytes 1572872 | tf_op jit(solution)/shard_map/ppermute | solution.py:278
  93.2 36.8 %collective-permute-start.20 = (bf16[256,1024]{1,0:T(8,128)(2,1)S(1)}, bf16[256,1024]{1,0:T(8,128)(2,1)S(1)}, u32[]{:S(2)}, u32[]{:S(2)}) collective-permute-start(bf16[256,1024]{1,0:T(8,128)(2,1)S(1)} %collective-permute-done.9), channel_id=1, source_target_pairs={{0,8},{2,10},{4,12},{6,14},{8,16},{10,18},{12,20},{14,22},{16,24},... | collective-permute-start | bytes 1572872 | tf_op jit(solution)/shard_map/ppermute | solution.py:278
  101.2 28.2 %collective-permute-start.21 = (bf16[96,2560]{1,0:T(8,128)(2,1)S(1)}, bf16[96,2560]{1,0:T(8,128)(2,1)S(1)}, u32[]{:S(2)}, u32[]{:S(2)}) collective-permute-start(bf16[96,2560]{1,0:T(8,128)(2,1)S(1)} %collective-permute-done.13), channel_id=1, source_target_pairs={{0,8},{2,10},{4,12},{6,14},{8,16},{10,18},{12,20},{14,22},{16,24},... | collective-permute-start | bytes 1474568 | tf_op jit(solution)/shard_map/ppermute | solution.py:278
  101.2 26.5 %collective-permute-start.22 = (bf16[256,1024]{1,0:T(8,128)(2,1)S(1)}, bf16[256,1024]{1,0:T(8,128)(2,1)S(1)}, u32[]{:S(2)}, u32[]{:S(2)}) collective-permute-start(bf16[256,1024]{1,0:T(8,128)(2,1)S(1)} %pad_maximum_fusion.18), channel_id=1, source_target_pairs={{0,2},{2,0},{4,6},{6,4},{8,10},{10,8},{12,14},{14,12},{16,18},{18,... | collective-permute-start | bytes 1572872 | tf_op jit(solution)/shard_map/ppermute | solution.py:278
  116.7 40.1 %collective-permute-start.24 = (bf16[192,2560]{1,0:T(8,128)(2,1)S(1)}, bf16[192,2560]{1,0:T(8,128)(2,1)S(1)}, u32[]{:S(2)}, u32[]{:S(2)}) collective-permute-start(bf16[192,2560]{1,0:T(8,128)(2,1)S(1)} %pad_maximum_fusion.10.refs_0_), channel_id=1, source_target_pairs={{0,4},{2,6},{4,0},{6,2},{8,12},{10,14},{12,8},{14,10},{16,20},{18,... | collective-permute-start | bytes 2949128 | tf_op jit(solution)/shard_map/ppermute | solution.py:278
  127.7 29.1 %collective-permute-start.19 = (bf16[512,1024]{1,0:T(8,128)(2,1)S(1)}, bf16[512,1024]{1,0:T(8,128)(2,1)S(1)}, u32[]{:S(2)}, u32[]{:S(2)}) collective-permute-start(bf16[512,1024]{1,0:T(8,128)(2,1)S(1)} %pad_maximum_fusion.8.refs_5_), channel_id=1, source_target_pairs={{0,2},{2,0},{4,6},{6,4},{8,10},{10,8},{12,14},{14,12},{16,18},{18,... | collective-permute-start | bytes 3145736 | tf_op jit(solution)/shard_map/ppermute | solution.py:278
  129.3 31.4 %collective-permute-start.25 = (bf16[512,1024]{1,0:T(8,128)(2,1)S(1)}, bf16[512,1024]{1,0:T(8,128)(2,1)S(1)}, u32[]{:S(2)}, u32[]{:S(2)}) collective-permute-start(bf16[512,1024]{1,0:T(8,128)(2,1)S(1)} %pad_maximum_fusion.9.refs_1_), channel_id=1, source_target_pairs={{0,4},{2,6},{4,0},{6,2},{8,12},{10,14},{12,8},{14,10},{16,20},{18,... | collective-permute-start | bytes 3145736 | tf_op jit(solution)/shard_map/ppermute | solution.py:278
  130.0 26.8 %collective-permute-start.26 = (bf16[256,1024]{1,0:T(8,128)(2,1)S(1)}, bf16[256,1024]{1,0:T(8,128)(2,1)S(1)}, u32[]{:S(2)}, u32[]{:S(2)}) collective-permute-start(bf16[256,1024]{1,0:T(8,128)(2,1)S(1)} %collective-permute-done.16), channel_id=1, source_target_pairs={{0,8},{2,10},{4,12},{6,14},{8,16},{10,18},{12,20},{14,22},{16,24},... | collective-permute-start | bytes 1572872 | tf_op jit(solution)/shard_map/ppermute | solution.py:278
  156.8 29.0 %collective-permute-start.31 = (bf16[96,2560]{1,0:T(8,128)(2,1)S(1)}, bf16[96,2560]{1,0:T(8,128)(2,1)S(1)}, u32[]{:S(2)}, u32[]{:S(2)}) collective-permute-start(bf16[96,2560]{1,0:T(8,128)(2,1)S(1)} %collective-permute-done.21), channel_id=1, source_target_pairs={{0,8},{2,10},{4,12},{6,14},{8,16},{10,18},{12,20},{14,22},{16,24},... | collective-permute-start | bytes 1474568 | tf_op jit(solution)/shard_map/ppermute | solution.py:278
  156.8 26.6 %collective-permute-start.29 = (bf16[96,3072]{1,0:T(8,128)(2,1)S(1)}, bf16[96,3072]{1,0:T(8,128)(2,1)S(1)}, u32[]{:S(2)}, u32[]{:S(2)}) collective-permute-start(bf16[96,3072]{1,0:T(8,128)(2,1)S(1)} %pad_maximum_fusion.11), channel_id=1, source_target_pairs={{0,8},{2,10},{4,12},{6,14},{8,16},{10,18},{12,20},{14,22},{16,24},... | collective-permute-start | bytes 1769480 | tf_op jit(solution)/shard_map/ppermute | solution.py:278
  158.7 35.9 %collective-permute-start.28 = (bf16[512,1024]{1,0:T(8,128)(2,1)}, bf16[512,1024]{1,0:T(8,128)(2,1)}, u32[]{:S(2)}, u32[]{:S(2)}) collective-permute-start(bf16[512,1024]{1,0:T(8,128)(2,1)} %constant_dynamic-update-slice_fusion.6.refs_5_), channel_id=1, source_target_pairs={{0,2},{2,0},{4,6},{6,4},{8,10},{10,8},{12,14},{14,12},{16,18},{18,... | collective-permute-start | bytes 3145736 | tf_op jit(solution)/shard_map/ppermute | solution.py:278
  160.1 34.5 %collective-permute-start.30 = (bf16[512,1024]{1,0:T(8,128)(2,1)}, bf16[512,1024]{1,0:T(8,128)(2,1)}, u32[]{:S(2)}, u32[]{:S(2)}) collective-permute-start(bf16[512,1024]{1,0:T(8,128)(2,1)} %constant_dynamic-update-slice_fusion.8.refs_1_), channel_id=1, source_target_pairs={{0,4},{2,6},{4,0},{6,2},{8,12},{10,14},{12,8},{14,10},{16,20},{18,... | collective-permute-start | bytes 3145736 | tf_op jit(solution)/shard_map/ppermute | solution.py:278
  183.5 27.4 %collective-permute-start.32 = (bf16[192,3072]{1,0:T(8,128)(2,1)S(1)}, bf16[192,3072]{1,0:T(8,128)(2,1)}, u32[]{:S(2)}, u32[]{:S(2)}) collective-permute-start(bf16[192,3072]{1,0:T(8,128)(2,1)S(1)} %pad_maximum_fusion.3.refs_0_), channel_id=1, source_target_pairs={{0,2},{2,0},{4,6},{6,4},{8,10},{10,8},{12,14},{14,12},{16,18},{18,... | collective-permute-start | bytes 3538952 | tf_op jit(solution)/shard_map/ppermute | solution.py:278
  275.3 34.6 %collective-permute-start.42 = (bf16[192,3072]{1,0:T(8,128)(2,1)}, bf16[192,3072]{1,0:T(8,128)(2,1)}, u32[]{:S(2)}, u32[]{:S(2)}) collective-permute-start(bf16[192,3072]{1,0:T(8,128)(2,1)} %get-tuple-element.316), channel_id=1, source_target_pairs={{0,2},{2,0},{4,6},{6,4},{8,10},{10,8},{12,14},{14,12},{16,18},{18,... | collective-permute-start | bytes 3538952 | tf_op jit(solution)/shard_map/ppermute | solution.py:278
  275.6 54.0 %collective-permute-start.45 = (bf16[192,3072]{1,0:T(8,128)(2,1)}, bf16[192,3072]{1,0:T(8,128)(2,1)}, u32[]{:S(2)}, u32[]{:S(2)}) collective-permute-start(bf16[192,3072]{1,0:T(8,128)(2,1)} %get-tuple-element.318), channel_id=1, source_target_pairs={{0,2},{2,0},{4,6},{6,4},{8,10},{10,8},{12,14},{14,12},{16,18},{18,... | collective-permute-start | bytes 3538952 | tf_op jit(solution)/shard_map/ppermute | solution.py:278
  305.3 27.4 %collective-permute-start.46 = (bf16[192,2560]{1,0:T(8,128)(2,1)}, bf16[192,2560]{1,0:T(8,128)(2,1)}, u32[]{:S(2)}, u32[]{:S(2)}) collective-permute-start(bf16[192,2560]{1,0:T(8,128)(2,1)} %get-tuple-element.330), channel_id=1, source_target_pairs={{0,4},{2,6},{4,0},{6,2},{8,12},{10,14},{12,8},{14,10},{16,20},{18,... | collective-permute-start | bytes 2949128 | tf_op jit(solution)/shard_map/ppermute | solution.py:278
  311.9 47.4 %collective-permute-start.43 = (bf16[192,2560]{1,0:T(8,128)(2,1)}, bf16[192,2560]{1,0:T(8,128)(2,1)}, u32[]{:S(2)}, u32[]{:S(2)}) collective-permute-start(bf16[192,2560]{1,0:T(8,128)(2,1)} %get-tuple-element.331), channel_id=1, source_target_pairs={{0,4},{2,6},{4,0},{6,2},{8,12},{10,14},{12,8},{14,10},{16,20},{18,... | collective-permute-start | bytes 2949128 | tf_op jit(solution)/shard_map/ppermute | solution.py:278
  328.6 33.9 %collective-permute-start.44 = (bf16[512,1024]{1,0:T(8,128)(2,1)}, bf16[512,1024]{1,0:T(8,128)(2,1)}, u32[]{:S(2)}, u32[]{:S(2)}) collective-permute-start(bf16[512,1024]{1,0:T(8,128)(2,1)} %get-tuple-element.335), channel_id=1, source_target_pairs={{0,2},{2,0},{4,6},{6,4},{8,10},{10,8},{12,14},{14,12},{16,18},{18,... | collective-permute-start | bytes 3145736 | tf_op jit(solution)/shard_map/ppermute | solution.py:278
  332.7 34.7 %collective-permute-start.49 = (bf16[96,3072]{1,0:T(8,128)(2,1)}, bf16[96,3072]{1,0:T(8,128)(2,1)}, u32[]{:S(2)}, u32[]{:S(2)}) collective-permute-start(bf16[96,3072]{1,0:T(8,128)(2,1)} %add_convert_fusion.14), channel_id=1, source_target_pairs={{0,8},{2,10},{4,12},{6,14},{8,16},{10,18},{12,20},{14,22},{16,24},... | collective-permute-start | bytes 1769480 | tf_op jit(solution)/shard_map/ppermute | solution.py:278
  335.8 28.6 %collective-permute-start.48 = (bf16[96,2560]{1,0:T(8,128)(2,1)}, bf16[96,2560]{1,0:T(8,128)(2,1)}, u32[]{:S(2)}, u32[]{:S(2)}) collective-permute-start(bf16[96,2560]{1,0:T(8,128)(2,1)} %slice.536), channel_id=1, source_target_pairs={{0,8},{2,10},{4,12},{6,14},{8,16},{10,18},{12,20},{14,22},{16,24},... | collective-permute-start | bytes 1474568 | tf_op jit(solution)/shard_map/ppermute | solution.py:278
  337.2 49.7 %collective-permute-start.54 = (bf16[512,1024]{1,0:T(8,128)(2,1)}, bf16[512,1024]{1,0:T(8,128)(2,1)}, u32[]{:S(2)}, u32[]{:S(2)}) collective-permute-start(bf16[512,1024]{1,0:T(8,128)(2,1)} %get-tuple-element.340), channel_id=1, source_target_pairs={{0,2},{2,0},{4,6},{6,4},{8,10},{10,8},{12,14},{14,12},{16,18},{18,... | collective-permute-start | bytes 3145736 | tf_op jit(solution)/shard_map/ppermute | solution.py:278
  369.1 28.3 %collective-permute-start.52 = (bf16[96,3072]{1,0:T(8,128)(2,1)S(1)}, bf16[96,3072]{1,0:T(8,128)(2,1)S(1)}, u32[]{:S(2)}, u32[]{:S(2)}) collective-permute-start(bf16[96,3072]{1,0:T(8,128)(2,1)S(1)} %add_convert_fusion.13), channel_id=1, source_target_pairs={{0,8},{2,10},{4,12},{6,14},{8,16},{10,18},{12,20},{14,22},{16,24},... | collective-permute-start | bytes 1769480 | tf_op jit(solution)/shard_map/ppermute | solution.py:278
  371.4 42.4 %collective-permute-start.50 = (bf16[512,1024]{1,0:T(8,128)(2,1)S(1)}, bf16[512,1024]{1,0:T(8,128)(2,1)S(1)}, u32[]{:S(2)}, u32[]{:S(2)}) collective-permute-start(bf16[512,1024]{1,0:T(8,128)(2,1)S(1)} %copy-done.96), channel_id=1, source_target_pairs={{0,4},{2,6},{4,0},{6,2},{8,12},{10,14},{12,8},{14,10},{16,20},{18,... | collective-permute-start | bytes 3145736 | tf_op jit(solution)/shard_map/ppermute | solution.py:278
  385.5 28.8 %collective-permute-start.59 = (bf16[512,1024]{1,0:T(8,128)(2,1)S(1)}, bf16[512,1024]{1,0:T(8,128)(2,1)S(1)}, u32[]{:S(2)}, u32[]{:S(2)}) collective-permute-start(bf16[512,1024]{1,0:T(8,128)(2,1)S(1)} %get-tuple-element.367), channel_id=1, source_target_pairs={{0,2},{2,0},{4,6},{6,4},{8,10},{10,8},{12,14},{14,12},{16,18},{18,... | collective-permute-start | bytes 3145736 | tf_op jit(solution)/shard_map/ppermute | solution.py:278
  419.6 28.4 %collective-permute-start.62 = (bf16[256,1024]{1,0:T(8,128)(2,1)S(1)}, bf16[256,1024]{1,0:T(8,128)(2,1)S(1)}, u32[]{:S(2)}, u32[]{:S(2)}) collective-permute-start(bf16[256,1024]{1,0:T(8,128)(2,1)S(1)} %slice.547), channel_id=1, source_target_pairs={{0,4},{2,6},{4,0},{6,2},{8,12},{10,14},{12,8},{14,10},{16,20},{18,... | collective-permute-start | bytes 1572872 | tf_op jit(solution)/shard_map/ppermute | solution.py:278
  437.7 36.8 %collective-permute-start.67 = (bf16[512,1024]{1,0:T(8,128)(2,1)}, bf16[512,1024]{1,0:T(8,128)(2,1)}, u32[]{:S(2)}, u32[]{:S(2)}) collective-permute-start(bf16[512,1024]{1,0:T(8,128)(2,1)} %get-tuple-element.387), channel_id=1, source_target_pairs={{0,4},{2,6},{4,0},{6,2},{8,12},{10,14},{12,8},{14,10},{16,20},{18,... | collective-permute-start | bytes 3145736 | tf_op jit(solution)/shard_map/ppermute | solution.py:278
  439.5 36.7 %collective-permute-start.68 = (bf16[512,1024]{1,0:T(8,128)(2,1)}, bf16[512,1024]{1,0:T(8,128)(2,1)}, u32[]{:S(2)}, u32[]{:S(2)}) collective-permute-start(bf16[512,1024]{1,0:T(8,128)(2,1)} %get-tuple-element.381), channel_id=1, source_target_pairs={{0,2},{2,0},{4,6},{6,4},{8,10},{10,8},{12,14},{14,12},{16,18},{18,... | collective-permute-start | bytes 3145736 | tf_op jit(solution)/shard_map/ppermute | solution.py:278
  528.5 33.8 %collective-permute-start.80 = (bf16[144,1024]{1,0:T(8,128)(2,1)S(1)}, bf16[144,1024]{1,0:T(8,128)(2,1)S(1)}, u32[]{:S(2)}, u32[]{:S(2)}) collective-permute-start(bf16[144,1024]{1,0:T(8,128)(2,1)S(1)} %add_convert_fusion.31), channel_id=1, source_target_pairs={{0,16},{2,18},{4,20},{6,22},{8,24},{10,26},{12,28},{14,30},{16,0},... | collective-permute-start | bytes 884744 | tf_op jit(solution)/shard_map/ppermute | solution.py:278
  (278 other events, 3913.4 us)
